TPU v7x, 32 devices: a whole 2x2x4 slice. The times are simulated.
32 devices in a mesh: dp: 16 (over z, y, core), mp: 2 (over x).
Axes of the slice: x: 2, y: 2, z: 4, core: 2. Of those that a mesh axis runs over, the one named last changes fastest.
Arguments:
- tokens: bfloat16 [6144, 2048], P('dp'), may hold values from -6 to 6
- doc_ids: int32 [16, 384], P('dp'), may hold values from 0 to 2, never falling along the last dimension, each value on 1 to 192 neighbouring positions
- frame_ids: int32 [16, 384], P('dp'), may hold values from 0 to 5, never falling along the last dimension, each value on 1 to 192 neighbouring positions
- gain_attn: float32 [2048], P('dp'), may hold values from 0.1 to 1.9
- w_query: bfloat16 [2048, 2048], P('dp', 'mp'), may hold values from -0.125 to 0.125
- w_key: bfloat16 [2048, 2048], P('dp', 'mp'), may hold values from -0.125 to 0.125
- w_value: bfloat16 [2048, 2048], P('dp', 'mp'), may hold values from -0.125 to 0.125
- w_output: bfloat16 [2048, 2048], P('mp', 'dp'), may hold values from -0.75 to 0.75
- gain_mlp: float32 [2048], P('dp'), may hold values from 0.1 to 1.9
- w_up: bfloat16 [2048, 8192], P('dp', 'mp'), may hold values from -0.125 to 0.125
- w_down: bfloat16 [8192, 2048], P('mp', 'dp'), may hold values from -0.09375 to 0.09375
- d_out: bfloat16 [6144, 2048], P('dp'), may hold values from -6 to 6
Outputs:
- result: float32 [6144, 2048], P('dp')
- d_tokens: float32 [6144, 2048], P('dp')
- d_gain_attn: float32 [2048], P('dp')
- d_w_query: float32 [2048, 2048], P('dp', 'mp')
- d_w_key: float32 [2048, 2048], P('dp', 'mp')
- d_w_value: float32 [2048, 2048], P('dp', 'mp')
- d_w_output: float32 [2048, 2048], P('mp', 'dp')
- d_gain_mlp: float32 [2048], P('dp')
- d_w_up: float32 [2048, 8192], P('dp', 'mp')
- d_w_down: float32 [8192, 2048], P('mp', 'dp')
Inputs may be any that keep to these rules, and one draw needn't show every extreme that they name: `doc_ids`: in each row, document numbers never decrease; every document holds 1 to 192 tokens. `frame_ids`: in each row, frame numbers never decrease; every frame holds 1 to 192 tokens.
All inputs are finite; a program needn't handle non-finite values.
Results may differ from a plain program's by a relative error of at most 0.035.
Values may be sent and summed in bfloat16 or wider, within the bound.
No kernel may reach another device: no remote copies, remote signals or barrier semaphores. Data moves between devices by JAX's collectives and lax.ppermute only.
A program may use at most 320 MiB of HBM per device.

v0:
```python
import math

import jax
import jax.numpy as jnp
from jax import lax
from jax.sharding import PartitionSpec as P

HEAD_DIM = 128


EPSILON = 1e-05
MASKED = -1e30


def product_plain(factor_one, factor_two):
    return jnp.dot(factor_one, factor_two, preferred_element_type=jnp.float32)


def product_inner(factor_one, factor_two):
    return lax.dot_general(
        factor_one, factor_two, (((0,), (0,)), ((), ())), preferred_element_type=jnp.float32
    )


def product_outer(factor_one, factor_two):
    return lax.dot_general(
        factor_one, factor_two, (((1,), (1,)), ((), ())), preferred_element_type=jnp.float32
    )


def norm_forward(values):
    centered = values - jnp.mean(values, axis=1, keepdims=True)
    inverse = lax.rsqrt(jnp.mean(centered * centered, axis=1, keepdims=True) + EPSILON)
    return (centered * inverse, inverse)


def norm_backward(grad_normed, scale_vec, standard, inverse):
    scaled = grad_normed * scale_vec
    return (
        scaled
        - jnp.mean(scaled, axis=1, keepdims=True)
        - standard * jnp.mean(scaled * standard, axis=1, keepdims=True)
    ) * inverse


def exact_gelu(values):
    return jax.nn.gelu(values, approximate=False)


def masked_scores(query_heads, key_heads, allowed):
    factor = 1.0 / math.sqrt(query_heads.shape[2])
    scores = (
        jnp.einsum("qhe,khe->hqk", query_heads, key_heads, preferred_element_type=jnp.float32)
        * factor
    )
    return jnp.where(allowed[None], scores, MASKED)


def shards(
    tokens,
    doc_ids,
    frame_ids,
    gain_attn,
    w_query,
    w_key,
    w_value,
    w_output,
    gain_mlp,
    w_up,
    w_down,
    d_out,
):
    head_dim = HEAD_DIM
    row_count = tokens.shape[0]
    doc_row = doc_ids[0]
    frame_row = frame_ids[0]
    allowed = (doc_row[:, None] == doc_row[None, :]) & (frame_row[None, :] <= frame_row[:, None])
    gain_one, query_full, key_full, value_full, output_full = (
        lax.all_gather(gain_attn.astype(jnp.bfloat16), "dp", axis=0, tiled=True).astype(
            gain_attn.dtype
        ),
        lax.all_gather(w_query, "dp", axis=0, tiled=True),
        lax.all_gather(w_key, "dp", axis=0, tiled=True),
        lax.all_gather(w_value, "dp", axis=0, tiled=True),
        lax.all_gather(w_output, "dp", axis=1, tiled=True),
    )
    inputs = tokens.astype(jnp.float32)
    standard_one, inverse_one = norm_forward(inputs)
    normed_one = (standard_one * gain_one).astype(jnp.bfloat16)
    query_heads = (
        product_plain(normed_one, query_full).astype(jnp.bfloat16).reshape(row_count, -1, head_dim)
    )
    key_heads = (
        product_plain(normed_one, key_full).astype(jnp.bfloat16).reshape(row_count, -1, head_dim)
    )
    value_heads = (
        product_plain(normed_one, value_full).astype(jnp.bfloat16).reshape(row_count, -1, head_dim)
    )
    scores = masked_scores(query_heads, key_heads, allowed)
    row_top = jnp.max(scores, axis=2, keepdims=True)
    shifted = jnp.exp(scores - row_top)
    totals = jnp.sum(shifted, axis=2, keepdims=True)
    log_total = row_top + jnp.log(totals)
    probs_low = (shifted / totals).astype(jnp.bfloat16)
    attended = jnp.einsum(
        "hqk,khe->qhe", probs_low, value_heads, preferred_element_type=jnp.float32
    )
    attended = attended.astype(jnp.bfloat16).reshape(row_count, -1)
    attn_out = lax.psum(product_plain(attended, output_full).astype(jnp.bfloat16), "mp").astype(
        jnp.float32
    )
    hidden = inputs + attn_out
    gain_two, up_full, down_full = (
        lax.all_gather(gain_mlp.astype(jnp.bfloat16), "dp", axis=0, tiled=True).astype(
            gain_mlp.dtype
        ),
        lax.all_gather(w_up, "dp", axis=0, tiled=True),
        lax.all_gather(w_down, "dp", axis=1, tiled=True),
    )
    standard_two, inverse_two = norm_forward(hidden)
    normed_two = (standard_two * gain_two).astype(jnp.bfloat16)
    pre_act = product_plain(normed_two, up_full)
    activated, gelu_back = jax.vjp(exact_gelu, pre_act)
    act_low = activated.astype(jnp.bfloat16)
    result = hidden + lax.psum(product_plain(act_low, down_full).astype(jnp.bfloat16), "mp").astype(
        jnp.float32
    )
    gain_two, up_full, down_full = (
        lax.all_gather(gain_mlp.astype(jnp.bfloat16), "dp", axis=0, tiled=True).astype(
            gain_mlp.dtype
        ),
        lax.all_gather(w_up, "dp", axis=0, tiled=True),
        lax.all_gather(w_down, "dp", axis=1, tiled=True),
    )
    grad_out = d_out.astype(jnp.float32)
    down_term = product_inner(act_low, d_out)
    grad_act = product_outer(d_out, down_full)
    grad_pre = gelu_back(grad_act)[0].astype(jnp.bfloat16)
    up_term = product_inner(normed_two, grad_pre)
    grad_normed_two = lax.psum(product_outer(grad_pre, up_full).astype(jnp.bfloat16), "mp").astype(
        jnp.float32
    )
    gain_two_term = jnp.sum(grad_normed_two * standard_two, axis=0)
    d_gain_mlp, d_w_up, d_w_down = (
        lax.psum_scatter(gain_two_term, "dp", scatter_dimension=0, tiled=True),
        lax.psum_scatter(up_term, "dp", scatter_dimension=0, tiled=True),
        lax.psum_scatter(down_term, "dp", scatter_dimension=1, tiled=True),
    )
    grad_hidden = grad_out + norm_backward(grad_normed_two, gain_two, standard_two, inverse_two)
    grad_low = grad_hidden.astype(jnp.bfloat16)
    gain_one, query_full, key_full, value_full, output_full = (
        lax.all_gather(gain_attn.astype(jnp.bfloat16), "dp", axis=0, tiled=True).astype(
            gain_attn.dtype
        ),
        lax.all_gather(w_query, "dp", axis=0, tiled=True),
        lax.all_gather(w_key, "dp", axis=0, tiled=True),
        lax.all_gather(w_value, "dp", axis=0, tiled=True),
        lax.all_gather(w_output, "dp", axis=1, tiled=True),
    )
    output_term = product_inner(attended, grad_low)
    grad_att = (
        product_outer(grad_low, output_full).astype(jnp.bfloat16).reshape(row_count, -1, head_dim)
    )
    again_scores = masked_scores(query_heads, key_heads, allowed)
    attn_probs = jnp.exp(again_scores - log_total)
    grad_probs = jnp.einsum(
        "qhe,khe->hqk", grad_att, value_heads, preferred_element_type=jnp.float32
    )
    delta = jnp.sum(grad_probs * attn_probs, axis=2, keepdims=True)
    grad_scores = (attn_probs * (grad_probs - delta)).astype(jnp.bfloat16)
    factor = 1.0 / math.sqrt(head_dim)
    grad_query = (
        jnp.einsum("hqk,khe->qhe", grad_scores, key_heads, preferred_element_type=jnp.float32)
        * factor
    )
    grad_query = grad_query.astype(jnp.bfloat16).reshape(row_count, -1)
    grad_key = (
        jnp.einsum("hqk,qhe->khe", grad_scores, query_heads, preferred_element_type=jnp.float32)
        * factor
    )
    grad_key = grad_key.astype(jnp.bfloat16).reshape(row_count, -1)
    grad_value = jnp.einsum("hqk,qhe->khe", probs_low, grad_att, preferred_element_type=jnp.float32)
    grad_value = grad_value.astype(jnp.bfloat16).reshape(row_count, -1)
    query_term = product_inner(normed_one, grad_query)
    key_term = product_inner(normed_one, grad_key)
    value_term = product_inner(normed_one, grad_value)
    partial_one = (
        product_outer(grad_query, query_full)
        + product_outer(grad_key, key_full)
        + product_outer(grad_value, value_full)
    )
    grad_normed_one = lax.psum(partial_one.astype(jnp.bfloat16), "mp").astype(jnp.float32)
    gain_one_term = jnp.sum(grad_normed_one * standard_one, axis=0)
    d_gain_attn, d_w_query, d_w_key, d_w_value, d_w_output = (
        lax.psum_scatter(gain_one_term, "dp", scatter_dimension=0, tiled=True),
        lax.psum_scatter(query_term, "dp", scatter_dimension=0, tiled=True),
        lax.psum_scatter(key_term, "dp", scatter_dimension=0, tiled=True),
        lax.psum_scatter(value_term, "dp", scatter_dimension=0, tiled=True),
        lax.psum_scatter(output_term, "dp", scatter_dimension=1, tiled=True),
    )
    d_tokens = grad_hidden + norm_backward(grad_normed_one, gain_one, standard_one, inverse_one)
    return (
        result,
        d_tokens,
        d_gain_attn,
        d_w_query,
        d_w_key,
        d_w_value,
        d_w_output,
        d_gain_mlp,
        d_w_up,
        d_w_down,
    )


def solution(mesh):
    return jax.shard_map(
        shards,
        mesh=mesh,
        in_specs=(
            P("dp", None),
            P("dp", None),
            P("dp", None),
            P("dp"),
            P("dp", "mp"),
            P("dp", "mp"),
            P("dp", "mp"),
            P("mp", "dp"),
            P("dp"),
            P("dp", "mp"),
            P("mp", "dp"),
            P("dp", None),
        ),
        out_specs=(
            P("dp", None),
            P("dp", None),
            P("dp"),
            P("dp", "mp"),
            P("dp", "mp"),
            P("dp", "mp"),
            P("mp", "dp"),
            P("dp"),
            P("dp", "mp"),
            P("mp", "dp"),
        ),
        check_vma=False,
    )
```

profile of v0, /device:TPU:0, one launch (start us, length us, event | category | flops | bytes accessed | tf_op | source)
XLA Modules:
  0.0 1860.1 jit_solution(18163562629698989611)
XLA Ops:
  12.1 23.2 %all-gather = bf16[16,1,128]{2,1,0:T(2,128)(2,1)S(1)} all-gather(bf16[1,1,128]{2,1,0:T(2,128)(2,1)S(1)} %convert_bitcast_fusion.1), channel_id=1, replica_groups=mesh['dp'=16,'mp'=2] {'dp'}, dimensions={0}, use_global_device_ids=true | all-gather | bytes 4352 | tf_op jit(solution)/shard_map/all_gather | solution.py:79
  35.3 1.7 convert_reduce_fusion
  37.8 25.7 %all-gather.13.cloned.1.call-done = bf16[2048,1024]{1,0:T(8,128)(2,1)} async-done(((bf16[128,1024]{1,0:T(8,128)(2,1)}), bf16[2048,1024]{1,0:T(8,128)(2,1)}) %all-gather.13.cloned.1.call-update) | async-done | bytes 4194320 | tf_op jit(solution)/shard_map/all_gather | solution.py:83
  63.5 4.0 convolution_convert_fusion.4
  67.9 46.8 %all-gather.11.cloned.1.call-done = bf16[2048,1024]{1,0:T(8,128)(2,1)} async-done(((bf16[128,1024]{1,0:T(8,128)(2,1)}), bf16[2048,1024]{1,0:T(8,128)(2,1)}) %all-gather.11.cloned.1.call-update) | async-done | bytes 4194320 | tf_op jit(solution)/shard_map/all_gather | solution.py:82
  114.7 4.9 convolution_convert_fusion.5
  122.2 2.2 copy-done.1
  125.3 40.7 %all-gather.9.cloned.1.call-done = bf16[2048,1024]{1,0:T(8,128)(2,1)} async-done(((bf16[128,1024]{1,0:T(8,128)(2,1)}), bf16[2048,1024]{1,0:T(8,128)(2,1)}) %all-gather.9.cloned.1.call-update) | async-done | bytes 4194320 | tf_op jit(solution)/shard_map/all_gather | solution.py:84
  166.0 4.2 fusion.31
  173.5 46.2 %all-gather.15.cloned.1.call-done = bf16[1024,2048]{1,0:T(8,128)(2,1)} async-done(((bf16[1024,128]{1,0:T(8,128)(2,1)}), bf16[1024,2048]{1,0:T(8,128)(2,1)}) %all-gather.15.cloned.1.call-update) | async-done | bytes 4194320 | tf_op jit(solution)/shard_map/all_gather | solution.py:85
  219.7 5.2 convolution_convert_fusion
  226.3 18.6 all-gather.1
  244.9 29.8 %all-reduce.8.cloned.1.call-done = bf16[384,2048]{1,0:T(8,128)(2,1)} async-done(((bf16[384,2048]{1,0:T(8,128)(2,1)}), bf16[384,2048]{1,0:T(8,128)(2,1)}) %all-reduce.8.cloned.1.call-update) | async-done | bytes 1572880 | tf_op jit(solution)/shard_map/psum | solution.py:109
  274.7 2.0 fusion.29
  277.5 126.4 %all-gather.17.cloned.1.call-done = bf16[2048,4096]{1,0:T(8,128)(2,1)} async-done(((bf16[128,4096]{1,0:T(8,128)(2,1)}), bf16[2048,4096]{1,0:T(8,128)(2,1)}) %all-gather.17.cloned.1.call-update) | async-done | bytes 16777232 | tf_op jit(solution)/shard_map/all_gather | solution.py:117
  403.9 11.9 fusion.41
  415.8 119.0 %all-gather.19.cloned.1.call-done = bf16[4096,2048]{1,0:T(8,128)(2,1)} async-done(((bf16[4096,128]{1,0:T(8,128)(2,1)}), bf16[4096,2048]{1,0:T(8,128)(2,1)}) %all-gather.19.cloned.1.call-update) | async-done | bytes 16777232 | tf_op jit(solution)/shard_map/all_gather | solution.py:118
  534.8 23.9 %add_convert_fusion = (bf16[384,4096]{1,0:T(8,128)(2,1)S(1)}, f32[384,4096]{1,0:T(8,128)S(1)}) fusion(f32[384,4096]{1,0:T(8,128)} %fusion.41, bf16[384,2048]{1,0:T(8,128)(2,1)} %param.23, bf16[4096,2048]{1,0:T(8,128)(2,1)} %all-gather.19.cloned.1.call-done), kind=kOutput, calls=%fused_computation.2 | convolution fusion | flops 6555697152 | bytes 34078720 | tf_op jit(solution)/shard_map/dot_general | solution.py:26
  558.7 3.0 multiply_convert_fusion
  561.8 11.6 convolution_convert_fusion.1
  573.5 12.7 convolution_convert_fusion.2
  586.2 37.1 %all-reduce.10.cloned.1.call-done = bf16[384,2048]{1,0:T(8,128)(2,1)} async-done(((bf16[384,2048]{1,0:T(8,128)(2,1)}), bf16[384,2048]{1,0:T(8,128)(2,1)}) %all-reduce.10.cloned.1.call-update) | async-done | bytes 1572880 | tf_op jit(solution)/shard_map/psum | solution.py:140
  623.3 3.1 fusion.26
  626.5 1.7 fusion.24
  628.1 1.7 copy-done.4
  629.8 2.8 convolution_convert_fusion.3
  632.6 2.3 copy.52
  634.9 2.9 convolution_convert_fusion.7
  637.8 4.1 multiply_reduce_fusion
  646.0 1.8 fusion.52
  648.1 2.0 fusion.53
  650.3 3.0 add_convert_fusion.1
  653.4 8.3 fusion.35
  662.4 7.1 fusion.42
  669.5 7.0 fusion.44
  677.0 7.0 fusion.46
  684.1 17.6 fusion.40
  701.9 17.6 fusion.54
  721.4 18.1 all-reduce.12.cloned.1.call-done
  739.5 2.8 fusion.28
  742.3 63.1 %all-reduce.2 = (f32[2048]{0:T(1024)S(1)}, f32[2048]{0:T(1024)S(1)}) all-reduce(f32[2048]{0:T(1024)S(1)} %get-tuple-element.12, f32[2048]{0:T(1024)S(1)} %get-tuple-element.10), channel_id=2, replica_groups=mesh['dp'=16,'mp'=2] {'dp'}, use_global_device_ids=true, to_apply=%region_16.17.clone | all-reduce | flops 4096 | bytes 32768
  806.5 5.5 fusion.20
  812.1 37.4 %reduce-scatter.13.cloned.1.call-done = f32[1024,128]{1,0:T(8,128)} async-done(((f32[1024,2048]{1,0:T(8,128)}), f32[1024,128]{1,0:T(8,128)}) %reduce-scatter.13.cloned.1.call-update) | async-done | bytes 524304 | tf_op jit(solution)/shard_map/reduce_scatter | solution.py:199
  849.5 109.7 %reduce-scatter.11.cloned.1.call-done = f32[128,1024]{1,0:T(8,128)} async-done(((f32[2048,1024]{1,0:T(8,128)}), f32[128,1024]{1,0:T(8,128)}) %reduce-scatter.11.cloned.1.call-update) | async-done | bytes 524304 | tf_op jit(solution)/shard_map/reduce_scatter | solution.py:198
  959.2 109.5 %reduce-scatter.9.cloned.1.call-done = f32[128,1024]{1,0:T(8,128)} async-done(((f32[2048,1024]{1,0:T(8,128)}), f32[128,1024]{1,0:T(8,128)}) %reduce-scatter.9.cloned.1.call-update) | async-done | bytes 524304 | tf_op jit(solution)/shard_map/reduce_scatter | solution.py:197
  1068.7 109.6 %reduce-scatter.7.cloned.1.call-done = f32[128,1024]{1,0:T(8,128)} async-done(((f32[2048,1024]{1,0:T(8,128)}), f32[128,1024]{1,0:T(8,128)}) %reduce-scatter.7.cloned.1.call-update) | async-done | bytes 524304 | tf_op jit(solution)/shard_map/reduce_scatter | solution.py:196
  1178.3 337.8 %reduce-scatter.15.cloned.1.call-done = f32[128,4096]{1,0:T(8,128)} async-done(((f32[2048,4096]{1,0:T(8,128)}), f32[128,4096]{1,0:T(8,128)}) %reduce-scatter.15.cloned.1.call-update) | async-done | bytes 2097168 | tf_op jit(solution)/shard_map/reduce_scatter | solution.py:146
  1516.2 337.2 %reduce-scatter.17.cloned.1.call-done = f32[4096,128]{1,0:T(8,128)} async-done(((f32[4096,2048]{1,0:T(8,128)}), f32[4096,128]{1,0:T(8,128)}) %reduce-scatter.17.cloned.1.call-update) | async-done | bytes 2097168 | tf_op jit(solution)/shard_map/reduce_scatter | solution.py:147
  (128 shorter events, 23.3 us)
Async XLA Ops:
  7.2 29.8 %copy-start = (bf16[384,2048]{1,0:T(8,128)(2,1)S(1)}, bf16[384,2048]{1,0:T(8,128)(2,1)}, u32[]{:S(2)}) copy-start(bf16[384,2048]{1,0:T(8,128)(2,1)} %param.12) | copy-start | bytes 4718596
  7.2 56.3 %all-gather.13.cloned.1.call-start = ((), (), s32[]{:S(2)}) async-start(), calls=%async_computation.8 | async-start | bytes 4456448 | tf_op jit(solution)/shard_map/all_gather | solution.py:83
  7.9 106.8 %all-gather.11.cloned.1.call-start = ((), (), s32[]{:S(2)}) async-start(), calls=%async_computation.7 | async-start | bytes 4456448 | tf_op jit(solution)/shard_map/all_gather | solution.py:82
  8.7 157.3 %all-gather.9.cloned.1.call-start = ((), (), s32[]{:S(2)}) async-start(), calls=%async_computation.6 | async-start | bytes 4456448 | tf_op jit(solution)/shard_map/all_gather | solution.py:84
  9.4 210.3 %all-gather.15.cloned.1.call-start = ((), (), s32[]{:S(2)}) async-start(), calls=%async_computation.9 | async-start | bytes 4456448 | tf_op jit(solution)/shard_map/all_gather | solution.py:85
  10.0 264.7 %all-reduce.8.cloned.1.call-start = ((), (), s32[]{:S(2)}) async-start(), calls=%async_computation.10 | async-start | bytes 3145728 | tf_op jit(solution)/shard_map/psum | solution.py:109
  35.3 130.7 %copy-start.21 = (f32[16,1,128]{2,1,0:T(1,128)}, f32[16,1,128]{2,1,0:T(1,128)S(1)}, u32[]{:S(2)}) copy-start(f32[16,1,128]{2,1,0:T(1,128)S(1)} %convert_element_type.136) | copy-start | bytes 24580
  37.0 129.0 %copy-start.23 = (f32[384]{0:T(512)}, f32[384]{0:T(512)S(1)}, u32[]{:S(2)}) copy-start(f32[384]{0:T(512)S(1)} %broadcast_multiply_fusion.5) | copy-start | bytes 4612
  37.6 128.4 %copy-start.25 = (f32[384]{0:T(512)}, f32[384]{0:T(512)S(1)}, u32[]{:S(2)}) copy-start(f32[384]{0:T(512)S(1)} %add_rsqrt_fusion.1) | copy-start | bytes 4612
  67.9 53.3 %copy-start.7 = (bf16[384,1024]{0,1:T(8,128)(2,1)}, bf16[384,1024]{0,1:T(8,128)(2,1)S(1)}, u32[]{:S(2)}) copy-start(bf16[384,1024]{0,1:T(8,128)(2,1)S(1)} %copy.51) | copy-start | bytes 2359300
  121.1 1.0 copy-start.9
  122.2 2.2 copy-start.1
  166.0 4.2 copy-start.2
  170.2 1.2 copy-start.19
  171.4 1.4 copy-start.5
  173.5 51.4 %copy-start.14 = (bf16[8,128,384]{2,1,0:T(8,128)(2,1)}, bf16[8,128,384]{2,1,0:T(8,128)(2,1)S(1)}, u32[]{:S(2)}) copy-start(bf16[8,128,384]{2,1,0:T(8,128)(2,1)S(1)} %convolution_convert_fusion.8) | copy-start | bytes 2359300
  224.9 1.4 copy-start.31
  224.9 179.0 %all-gather.17.cloned.1.call-start = ((), (), s32[]{:S(2)}) async-start(), calls=%async_computation.11 | async-start | bytes 17825792 | tf_op jit(solution)/shard_map/all_gather | solution.py:117
  225.5 309.3 %all-gather.19.cloned.1.call-start = ((), (), s32[]{:S(2)}) async-start(), calls=%async_computation.12 | async-start | bytes 17825792 | tf_op jit(solution)/shard_map/all_gather | solution.py:118
  226.3 397.0 %all-reduce.10.cloned.1.call-start = ((), (), s32[]{:S(2)}) async-start(), calls=%async_computation.13 | async-start | bytes 3145728 | tf_op jit(solution)/shard_map/psum | solution.py:140
  274.7 2.0 copy-start.3
  534.8 23.9 %copy-start.12 = (f32[384,4096]{1,0:T(8,128)S(1)}, f32[384,4096]{1,0:T(8,128)}, u32[]{:S(2)}) copy-start(f32[384,4096]{1,0:T(8,128)} %fusion.41) | copy-start | bytes 18874372
  558.7 3.1 copy-start.18
  573.4 166.0 %all-reduce.12.cloned.1.call-start = ((), (), s32[]{:S(2)}) async-start(), calls=%async_computation.20 | async-start | bytes 6291456 | tf_op jit(solution)/shard_map/psum | solution.py:125
  623.3 3.2 copy-start.11
  623.3 3.2 copy-start.13
  626.4 3.4 copy-start.30
  628.1 1.7 copy-start.4
  634.9 2.9 copy-start.6
  634.9 2.9 copy-start.20
  634.9 7.0 slice-start
  637.8 12.4 copy-start.16
  637.8 4.1 slice-start.1
  641.9 1.3 copy-start.10
  643.2 1.1 copy-start.8
  643.2 2.7 copy-start.28
  644.4 3.4 copy-start.17
  645.1 2.7 copy-start.15
  646.0 2.2 copy-start.27
  648.1 2.2 copy-start.29
  653.4 196.2 %reduce-scatter.13.cloned.1.call-start = ((), (), s32[]{:S(2)}) async-start(), calls=%async_computation.17 | async-start | bytes 8912896 | tf_op jit(solution)/shard_map/reduce_scatter | solution.py:199
  661.7 0.7 copy-start.24
  661.7 0.7 copy-start.26
  661.7 297.5 %reduce-scatter.11.cloned.1.call-start = ((), (), s32[]{:S(2)}) async-start(), calls=%async_computation.16 | async-start | bytes 8912896 | tf_op jit(solution)/shard_map/reduce_scatter | solution.py:198
  669.5 399.2 %reduce-scatter.9.cloned.1.call-start = ((), (), s32[]{:S(2)}) async-start(), calls=%async_computation.15 | async-start | bytes 8912896 | tf_op jit(solution)/shard_map/reduce_scatter | solution.py:197
  676.6 501.8 %reduce-scatter.7.cloned.1.call-start = ((), (), s32[]{:S(2)}) async-start(), calls=%async_computation.14 | async-start | bytes 8912896 | tf_op jit(solution)/shard_map/reduce_scatter | solution.py:196
  684.0 832.1 %reduce-scatter.15.cloned.1.call-start = ((), (), s32[]{:S(2)}) async-start(), calls=%async_computation.18 | async-start | bytes 35651584 | tf_op jit(solution)/shard_map/reduce_scatter | solution.py:146
  701.7 1151.7 %reduce-scatter.17.cloned.1.call-start = ((), (), s32[]{:S(2)}) async-start(), calls=%async_computation.19 | async-start | bytes 35651584 | tf_op jit(solution)/shard_map/reduce_scatter | solution.py:147
  (2 other events, 1.4 us)
Sparse Core Ops, SparseCore 0:
  10.2 53.2 all-gather.12
  65.6 49.0 all-gather.10
  116.9 49.0 all-gather.8
  168.0 51.6 all-gather.14
  225.0 49.6 all-reduce.7
  277.0 126.8 all-gather.16
  406.3 128.5 all-gather.18
  573.6 49.6 all-reduce.9
  653.5 85.9 all-reduce.11
  744.5 104.9 reduce-scatter.12
  854.7 104.4 reduce-scatter.10
  964.2 104.4 reduce-scatter.8
  1073.9 104.4 reduce-scatter.6
  1183.6 332.4 reduce-scatter.14
  1521.4 331.8 reduce-scatter.16
where the time goes:
time: 1870 us; the launch traced here: 1860 us
  waiting for transfers between devices  1530 us (82%)
  matrix products  163 us (9%)
  blocking collectives  105 us (6%)
  other arithmetic  26.9 us (1%)
    reduce_scatter x1, waiting for transfers between devices, shards(): lax.psum_scatter(up_term, 'dp', scatter_dimension=0, tiled=True)  338 us
    reduce_scatter x1, waiting for transfers between devices, shards(): lax.psum_scatter(down_term, 'dp', scatter_dimension=1, tiled=True)  337 us
    all_gather x1, waiting for transfers between devices, shards(): lax.all_gather(w_up, 'dp', axis=0, tiled=True)  126 us
    all_gather x1, waiting for transfers between devices, shards(): lax.all_gather(w_down, 'dp', axis=1, tiled=True)  119 us
    reduce_scatter x1, waiting for transfers between devices, shards(): lax.psum_scatter(value_term, 'dp', scatter_dimension=0, tiled=True)  110 us
    reduce_scatter x1, waiting for transfers between devices, shards(): lax.psum_scatter(query_term, 'dp', scatter_dimension=0, tiled=True)  110 us
    reduce_scatter x1, waiting for transfers between devices, shards(): lax.psum_scatter(key_term, 'dp', scatter_dimension=0, tiled=True)  110 us
    dot_general x6, matrix products, product_inner(): lax.dot_general(factor_one, factor_two, (((0,), (0,)), ((), ())), preferr...  64.5 us
  transfers between devices with their start and end apart: 15, of which 15 were waited for; matrix products, arithmetic and copies ran while one was open for 7% of the time, Pallas kernels for 0%

commit v1 on v0

v1 whole, which is shorter than its diff:
```python
import functools
import math

import jax
import jax.numpy as jnp
from jax import lax
from jax.sharding import PartitionSpec as P

HEAD_DIM = 128
EPSILON = 1e-05
MASKED = -1e30
LOW = jnp.bfloat16
WIDE = jnp.float32


def plain(one, two):
    return jnp.dot(one, two, preferred_element_type=WIDE)


def inner(one, two):
    return lax.dot_general(one, two, (((0,), (0,)), ((), ())), preferred_element_type=WIDE)


def outer(one, two):
    return lax.dot_general(one, two, (((1,), (1,)), ((), ())), preferred_element_type=WIDE)


def norm_forward(values):
    centered = values - jnp.mean(values, axis=1, keepdims=True)
    inverse = lax.rsqrt(jnp.mean(centered * centered, axis=1, keepdims=True) + EPSILON)
    return centered * inverse, inverse


def norm_backward(scaled, standard, inverse):
    return (
        scaled
        - jnp.mean(scaled, axis=1, keepdims=True)
        - standard * jnp.mean(scaled * standard, axis=1, keepdims=True)
    ) * inverse


def gelu_parts(values):
    half = 0.5 * (1.0 + lax.erf(values * (1.0 / math.sqrt(2.0))))
    slope = half + values * jnp.exp(-0.5 * values * values) * (1.0 / math.sqrt(2.0 * math.pi))
    return values * half, slope


def take(values, index, size, axis):
    return lax.dynamic_slice_in_dim(values, index * size, size, axis)


def put(whole, part, index, axis):
    return lax.dynamic_update_slice_in_dim(whole, part, index * part.shape[axis], axis)


class Links:
    def __init__(self, count):
        self.ring_size = count // 4
        self.to = {k: [(i, i ^ k) for i in range(count)] for k in (1, 2, 3)}
        self.next = [(i, (i + 4) % count) for i in range(count)]
        place = lax.axis_index("dp")
        self.ring_at = place // 4
        self.cell = place % 4
        self.row = self.cell // 2
        self.core = self.cell % 2

    def swap(self, values, k):
        return lax.ppermute(values, "dp", self.to[k])

    def step(self, values):
        return lax.ppermute(values, "dp", self.next)

    def across(self, values):
        return lax.ppermute(values, "mp", [(0, 1), (1, 0)])

    def behind(self, k):
        return lax.rem(self.ring_at - k + 2 * self.ring_size, self.ring_size)


def both_cores(links, own, other, axis):
    return jnp.where(
        links.core == 0,
        jnp.concatenate([own, other], axis=axis),
        jnp.concatenate([other, own], axis=axis),
    )


def gather_pair(links, block, axis):
    size = list(block.shape)
    size[axis] *= 2 * links.ring_size
    whole = jnp.zeros(size, block.dtype)
    for k in range(links.ring_size):
        if k:
            block = links.step(block)
        at = links.behind(k) * 2
        whole = put(whole, block, at + links.row, axis)
        whole = put(whole, links.swap(block, 2), at + 1 - links.row, axis)
    return whole


def gather_ring(links, block, axis):
    size = list(block.shape)
    size[axis] *= links.ring_size
    whole = jnp.zeros(size, block.dtype)
    for k in range(links.ring_size):
        if k:
            block = links.step(block)
        whole = put(whole, block, links.behind(k), axis)
    return whole


def exchange(links, whole, cut_axis, join_axis, finish=lambda part: part, own=None):
    size = whole.shape[cut_axis] // 4
    shape = list(whole.shape)
    shape[cut_axis] = size
    shape[join_axis] *= 4
    parts = [take(whole if own is None else own, links.cell, size, cut_axis)]
    for k in (1, 2, 3):
        parts.append(links.swap(take(whole, links.cell ^ k, size, cut_axis), k))
    parts = [finish(part) for part in parts]
    joined = jnp.zeros(shape, parts[0].dtype)
    for k in range(4):
        joined = put(joined, parts[k], links.cell ^ k, join_axis)
    return joined


def tokens_of_plane(links, own):
    far = links.swap(own, 2)
    return jnp.concatenate([own, links.swap(own, 1), far, links.swap(far, 1)], axis=0)


def sum_over_cores(links, partial):
    rows = partial.shape[0] // 2
    other = links.swap(partial[rows:].astype(LOW), 1)
    return partial[:rows] + other.astype(WIDE)


def sum_across(links, partial):
    low = partial.astype(LOW)
    return low.astype(WIDE) + links.across(low).astype(WIDE)


def sum_over_plane(links, partial):
    rows = partial.shape[0] // 4
    to_core = jnp.concatenate([partial[rows : 2 * rows], partial[3 * rows :]], axis=0).astype(LOW)
    from_core = links.swap(to_core, 1).astype(WIDE)
    far = partial[2 * rows : 3 * rows] + from_core[rows:]
    near = partial[:rows] + from_core[:rows] + links.swap(far.astype(LOW), 2).astype(WIDE)
    return sum_across(links, near)


def shards(
    count,
    tokens,
    doc_ids,
    frame_ids,
    gain_attn,
    w_query,
    w_key,
    w_value,
    w_output,
    gain_mlp,
    w_up,
    w_down,
    d_out,
):
    links = Links(count)
    rows, width = tokens.shape
    ring = links.ring_size
    shard_rows = width // count
    half = w_query.shape[1] // 2
    heads = half // HEAD_DIM

    def scaled_by(weight, gain):
        return (weight.astype(WIDE) * gain[:, None]).astype(LOW)

    halves = [
        scaled_by(weight, gain_attn).reshape(shard_rows, 2, half)
        for weight in (w_query, w_key, w_value)
    ]
    qkv_shard = jnp.concatenate(halves, axis=2)
    qkv_own = lax.dynamic_index_in_dim(qkv_shard, links.core, 1, keepdims=False)
    qkv_other = lax.dynamic_index_in_dim(qkv_shard, 1 - links.core, 1, keepdims=False)
    qkv_block = both_cores(links, qkv_own, links.swap(qkv_other, 1), 0)
    qkv_full = gather_pair(links, qkv_block, 0)

    out_own = take(w_output, links.core, half, 0)
    out_other = take(w_output, 1 - links.core, half, 0)
    out_block = both_cores(links, out_own, links.swap(out_other, 1), 1)
    out_full = gather_pair(links, out_block, 1)

    up_block = exchange(links, scaled_by(w_up, gain_mlp), 1, 0)
    up_full = gather_ring(links, up_block, 0)
    down_block = exchange(links, w_down, 0, 1)
    down_full = gather_ring(links, down_block, 1)

    inputs = tokens.astype(WIDE)
    standard_one, inverse_one = norm_forward(inputs)
    normed_own = standard_one.astype(LOW)
    normed_one = jnp.concatenate([normed_own, links.swap(normed_own, 1)], axis=0)
    docs = jnp.concatenate([doc_ids, links.swap(doc_ids, 1)], axis=0)
    frames = jnp.concatenate([frame_ids, links.swap(frame_ids, 1)], axis=0)
    allowed = (docs[:, :, None] == docs[:, None, :]) & (frames[:, None, :] <= frames[:, :, None])
    qkv = plain(normed_one, qkv_full).astype(LOW)

    def heads_of(values):
        return values.reshape(2, rows, heads, HEAD_DIM)

    query, key, value = (heads_of(qkv[:, i * half : (i + 1) * half]) for i in range(3))
    factor = 1.0 / math.sqrt(HEAD_DIM)
    scores = jnp.einsum("gqhe,gkhe->ghqk", query, key, preferred_element_type=WIDE) * factor
    scores = jnp.where(allowed[:, None], scores, MASKED)
    shifted = jnp.exp(scores - jnp.max(scores, axis=3, keepdims=True))
    probs = shifted / jnp.sum(shifted, axis=3, keepdims=True)
    probs_low = probs.astype(LOW)
    attended = jnp.einsum("ghqk,gkhe->gqhe", probs_low, value, preferred_element_type=WIDE)
    attended = attended.astype(LOW).reshape(2 * rows, half)
    hidden = inputs + sum_across(links, sum_over_cores(links, plain(attended, out_full)))

    standard_two, inverse_two = norm_forward(hidden)
    normed_two = tokens_of_plane(links, standard_two.astype(LOW))
    grad_plane = tokens_of_plane(links, d_out)
    pre_act = plain(normed_two, up_full)
    activated, slope = gelu_parts(pre_act)
    act_low = activated.astype(LOW)
    block = width // ring

    def ring_sum(part_of):
        total = None
        for k in range(1, ring + 1):
            part = part_of(links.behind(k))
            if total is not None:
                part = part + links.step(total.astype(LOW)).astype(WIDE)
            total = part
        return total

    down_sum = ring_sum(lambda at: inner(act_low, take(grad_plane, at, block, 1)))
    result = hidden + sum_over_plane(links, plain(act_low, down_full))
    grad_act = outer(grad_plane, down_full)
    grad_pre = (grad_act * slope).astype(LOW)
    up_sum = ring_sum(lambda at: inner(take(normed_two, at, block, 1), grad_pre))
    scaled_two = sum_over_plane(links, outer(grad_pre, up_full))
    grad_hidden = d_out.astype(WIDE) + norm_backward(scaled_two, standard_two, inverse_two)

    low_own = grad_hidden.astype(LOW)
    grad_low = jnp.concatenate([low_own, links.swap(low_own, 1)], axis=0)
    pair = block // 2

    def pair_sum(part_of, axis):
        total = None
        for k in range(1, ring + 1):
            part = part_of(links.behind(k))
            away = links.swap(take(part, 1 - links.row, pair, axis).astype(LOW), 2)
            part = take(part, links.row, pair, axis) + away.astype(WIDE)
            if total is not None:
                part = part + links.step(total.astype(LOW)).astype(WIDE)
            total = part
        return total

    out_sum = pair_sum(lambda at: inner(attended, take(grad_low, at, block, 1)), 1)
    grad_att = heads_of(outer(grad_low, out_full).astype(LOW))
    grad_probs = jnp.einsum("gqhe,gkhe->ghqk", grad_att, value, preferred_element_type=WIDE)
    delta = jnp.sum(grad_probs * probs, axis=3, keepdims=True)
    grad_scores = (probs * (grad_probs - delta)).astype(LOW)
    grad_query = jnp.einsum("ghqk,gkhe->gqhe", grad_scores, key, preferred_element_type=WIDE)
    grad_key = jnp.einsum("ghqk,gqhe->gkhe", grad_scores, query, preferred_element_type=WIDE)
    grad_value = jnp.einsum("ghqk,gqhe->gkhe", probs_low, grad_att, preferred_element_type=WIDE)
    grad_qkv = jnp.concatenate(
        [
            values.astype(LOW).reshape(2 * rows, half)
            for values in (grad_query * factor, grad_key * factor, grad_value)
        ],
        axis=1,
    )
    qkv_sum = pair_sum(lambda at: inner(take(normed_one, at, block, 1), grad_qkv), 0)
    scaled_one = sum_across(links, sum_over_cores(links, outer(grad_qkv, qkv_full)))
    d_tokens = grad_hidden + norm_backward(scaled_one, standard_one, inverse_one)

    def core_rows(total, axis, join_axis):
        own = take(total, links.core, shard_rows, axis)
        other = links.swap(take(total, 1 - links.core, shard_rows, axis).astype(LOW), 1)
        return both_cores(links, own, other.astype(WIDE), join_axis)

    d_w_output = core_rows(out_sum, 1, 0)
    own = take(qkv_sum, links.core, shard_rows, 0)
    other = links.swap(take(qkv_sum, 1 - links.core, shard_rows, 0).astype(LOW), 1).astype(WIDE)
    raw = [
        both_cores(links, own[:, i * half : (i + 1) * half], other[:, i * half : (i + 1) * half], 1)
        for i in range(3)
    ]
    d_w_query, d_w_key, d_w_value = (part * gain_attn[:, None] for part in raw)
    raw_up = exchange(links, up_sum.astype(LOW), 0, 1, lambda part: part.astype(WIDE), up_sum)
    d_w_up = raw_up * gain_mlp[:, None]
    d_w_down = exchange(links, down_sum.astype(LOW), 1, 0, lambda part: part.astype(WIDE), down_sum)

    def gain_sum(pairs):
        own = sum(jnp.sum(weight.astype(WIDE) * part, axis=1) for weight, part in pairs)
        return own + links.across(own)

    d_gain_attn = gain_sum(zip((w_query, w_key, w_value), raw))
    d_gain_mlp = gain_sum([(w_up, raw_up)])
    return (
        result,
        d_tokens,
        d_gain_attn,
        d_w_query,
        d_w_key,
        d_w_value,
        d_w_output,
        d_gain_mlp,
        d_w_up,
        d_w_down,
    )


def solution(mesh):
    return jax.shard_map(
        functools.partial(shards, mesh.shape["dp"]),
        mesh=mesh,
        in_specs=(
            P("dp", None),
            P("dp", None),
            P("dp", None),
            P("dp"),
            P("dp", "mp"),
            P("dp", "mp"),
            P("dp", "mp"),
            P("mp", "dp"),
            P("dp"),
            P("dp", "mp"),
            P("mp", "dp"),
            P("dp", None),
        ),
        out_specs=(
            P("dp", None),
            P("dp", None),
            P("dp"),
            P("dp", "mp"),
            P("dp", "mp"),
            P("dp", "mp"),
            P("mp", "dp"),
            P("dp"),
            P("dp", "mp"),
            P("mp", "dp"),
        ),
        check_vma=False,
    )
```

time: 1870 us -> 757 us (0.40)
  waiting for transfers between devices: 1530 us -> 466 us
  blocking collectives: 105 us -> 0 us
  local copies, waits for them, and re-layouts: 14 us -> 62.8 us
  matrix products: 163 us -> 120 us
  starting transfers between devices: 1.64 us -> 43 us
  other arithmetic: 26.9 us -> 56.6 us
    reduce_scatter x6 -> x0, waiting for transfers between devices: 1040 us -> none  [the longest x1 338 us: shards(): lax.psum_scatter(up_term, 'dp', scatter_dimension=0, tiled=True)]
    ppermute x0 -> x78, waiting for transfers between devices: none -> 466 us  [the longest x24 272 us: step(): return lax.ppermute(values, 'dp', self.next)]
    all_gather x6 -> x0, waiting for transfers between devices: 405 us -> none  [the longest x1 126 us: shards(): lax.all_gather(w_up, 'dp', axis=0, tiled=True)]
    psum x3 -> x0, waiting for transfers between devices: 85 us -> none  [the longest x1 37.1 us: shards(): lax.psum(product_outer(grad_pre, up_full).astype(jnp.bfloat16), 'mp')]
    unnamed x1 -> x0, blocking collectives: 63.1 us -> none
    dot_general x24 -> x29, matrix products: 163 us -> 116 us  [the longest x16 35.7 us: inner(): lax.dot_general(one, two, (((0,), (0,)), ((), ())), preferred_element_typ...]
    ppermute x0 -> x78, starting transfers between devices: none -> 43 us  [the longest x48 30.1 us: swap(): return lax.ppermute(values, 'dp', self.to[k])]
    all_gather x2 -> x0, blocking collectives: 41.7 us -> none  [the longest x1 23.2 us: shards(): lax.all_gather(gain_attn.astype(jnp.bfloat16), 'dp', axis=0, tiled=True)]
  transfers between devices with their start and end apart: 15 -> 78, of which waited for: 15 -> 38; matrix products, arithmetic and copies ran while one was open for 7% -> 23% of each run, Pallas kernels for 0% -> 0%
where the time goes in v1:
time: 757 us; the launch traced here: 751 us
  waiting for transfers between devices  466 us (62%)
  matrix products  120 us (16%)
  local copies, waits for them, and re-layouts  62.8 us (8%)
  other arithmetic  56.6 us (7%)
  starting transfers between devices  43 us (6%)
    ppermute x24, waiting for transfers between devices, step(): return lax.ppermute(values, 'dp', self.next)  272 us
    ppermute x48, waiting for transfers between devices, swap(): return lax.ppermute(values, 'dp', self.to[k])  158 us
    ppermute x6, waiting for transfers between devices, across(): return lax.ppermute(values, 'mp', [(0, 1), (1, 0)])  35.8 us
    dot_general x16, matrix products, inner(): lax.dot_general(one, two, (((0,), (0,)), ((), ())), preferred_element_typ...  35.7 us
    dot_general x4, matrix products, plain(): return jnp.dot(one, two, preferred_element_type=WIDE)  33.8 us
    dot_general x4, matrix products, outer(): lax.dot_general(one, two, (((1,), (1,)), ((), ())), preferred_element_typ...  31.2 us
    ppermute x48, starting transfers between devices, swap(): return lax.ppermute(values, 'dp', self.to[k])  30.1 us
    dynamic_update_slice x30, local copies, waits for them, and re-layouts, put(): lax.dynamic_update_slice_in_dim(whole, part, index * part.shape[axis], axis)  25.6 us
  transfers between devices with their start and end apart: 78, of which 38 were waited for; matrix products, arithmetic and copies ran while one was open for 23% of the time, Pallas kernels for 0%

profile of v1, /device:TPU:0, one launch (start us, length us, event | category | flops | bytes accessed | tf_op | source)
XLA Modules:
  0.0 751.2 jit_solution(7925049847684170524)
XLA Ops:
  15.4 14.4 %collective-permute-done.3 = bf16[256,1536]{1,0:T(8,128)(2,1)} collective-permute-done((bf16[256,1536]{1,0:T(8,128)(2,1)}, bf16[256,1536]{1,0:T(8,128)(2,1)}, u32[]{:S(2)}, u32[]{:S(2)}) %collective-permute-start.3) | collective-permute-done | bytes 786464 | tf_op jit(solution)/shard_map/ppermute | solution.py:71
  29.8 5.6 collective-permute-done.13
  38.5 18.7 %collective-permute-done.15 = bf16[512,256]{1,0:T(8,128)(2,1)S(1)} collective-permute-done((bf16[512,256]{1,0:T(8,128)(2,1)}, bf16[512,256]{1,0:T(8,128)(2,1)S(1)}, u32[]{:S(2)}, u32[]{:S(2)}) %collective-permute-start.15) | collective-permute-done | bytes 262176 | tf_op jit(solution)/shard_map/ppermute | solution.py:71
  61.9 5.7 collective-permute-done.17
  73.2 3.7 collective-permute-done.18
  79.7 8.9 %collective-permute-done.7 = bf16[256,1536]{1,0:T(8,128)(2,1)S(1)} collective-permute-done((bf16[256,1536]{1,0:T(8,128)(2,1)S(1)}, bf16[256,1536]{1,0:T(8,128)(2,1)S(1)}, u32[]{:S(2)}, u32[]{:S(2)}) %collective-permute-start.7) | collective-permute-done | bytes 786464 | tf_op jit(solution)/shard_map/ppermute | solution.py:71
  89.6 4.1 collective-permute-done.4
  95.6 15.0 %collective-permute-done.6 = bf16[256,1536]{1,0:T(8,128)(2,1)S(1)} collective-permute-done((bf16[256,1536]{1,0:T(8,128)(2,1)S(1)}, bf16[256,1536]{1,0:T(8,128)(2,1)S(1)}, u32[]{:S(2)}, u32[]{:S(2)}) %collective-permute-start.6) | collective-permute-done | bytes 786464 | tf_op jit(solution)/shard_map/ppermute | solution.py:68
  112.4 11.9 %collective-permute-done.8 = bf16[256,1536]{1,0:T(8,128)(2,1)S(1)} collective-permute-done((bf16[256,1536]{1,0:T(8,128)(2,1)S(1)}, bf16[256,1536]{1,0:T(8,128)(2,1)S(1)}, u32[]{:S(2)}, u32[]{:S(2)}) %collective-permute-start.8) | collective-permute-done | bytes 786464 | tf_op jit(solution)/shard_map/ppermute | solution.py:68
  125.3 9.5 %convolution_convert_fusion = bf16[768,1536]{1,0:T(8,128)(2,1)S(1)} fusion(bf16[2048,1536]{1,0:T(8,128)(2,1)} %constant_dynamic-update-slice_fusion.22, bf16[384,2048]{1,0:T(8,128)(2,1)S(1)} %collective-permute-done, bf16[384,2048]{1,0:T(8,128)(2,1)S(1)} %fusion.11), kind=kOutput, calls=%fused_computation.42 | convolution fusion | flops 4839309312 | bytes 11796480 | tf_op jit(solution)/shard_map/dot_general | solution.py:17
  138.5 3.9 fusion.160
  142.4 4.3 fusion.70
  150.4 3.4 collective-permute-done.19
  164.6 4.4 collective-permute-done.25
  175.6 38.4 %collective-permute-done.31 = bf16[1024,128]{1,0:T(8,128)(2,1)S(1)} collective-permute-done((bf16[1024,128]{1,0:T(8,128)(2,1)S(1)}, bf16[1024,128]{1,0:T(8,128)(2,1)S(1)}, u32[]{:S(2)}, u32[]{:S(2)}) %collective-permute-start.31) | collective-permute-done | bytes 262176 | tf_op jit(solution)/shard_map/ppermute | solution.py:68
  224.2 18.0 %collective-permute-done.27 = bf16[512,1024]{1,0:T(8,128)(2,1)} collective-permute-done((bf16[512,1024]{1,0:T(8,128)(2,1)}, bf16[512,1024]{1,0:T(8,128)(2,1)}, u32[]{:S(2)}, u32[]{:S(2)}) %collective-permute-start.27) | collective-permute-done | bytes 1048608 | tf_op jit(solution)/shard_map/ppermute | solution.py:71
  242.2 22.5 %collective-permute-done.33 = bf16[1024,512]{1,0:T(8,128)(2,1)} collective-permute-done((bf16[1024,512]{1,0:T(8,128)(2,1)}, bf16[1024,512]{1,0:T(8,128)(2,1)}, u32[]{:S(2)}, u32[]{:S(2)}) %collective-permute-start.33) | collective-permute-done | bytes 1048608 | tf_op jit(solution)/shard_map/ppermute | solution.py:71
  272.2 14.9 %collective-permute-done.28 = bf16[512,1024]{1,0:T(8,128)(2,1)} collective-permute-done((bf16[512,1024]{1,0:T(8,128)(2,1)}, bf16[512,1024]{1,0:T(8,128)(2,1)}, u32[]{:S(2)}, u32[]{:S(2)}) %collective-permute-start.28) | collective-permute-done | bytes 1048608 | tf_op jit(solution)/shard_map/ppermute | solution.py:71
  287.1 22.5 %collective-permute-done.34 = bf16[1024,512]{1,0:T(8,128)(2,1)} collective-permute-done((bf16[1024,512]{1,0:T(8,128)(2,1)}, bf16[1024,512]{1,0:T(8,128)(2,1)}, u32[]{:S(2)}, u32[]{:S(2)}) %collective-permute-start.34) | collective-permute-done | bytes 1048608 | tf_op jit(solution)/shard_map/ppermute | solution.py:71
  315.5 16.5 %collective-permute-done.29 = bf16[512,1024]{1,0:T(8,128)(2,1)S(1)} collective-permute-done((bf16[512,1024]{1,0:T(8,128)(2,1)}, bf16[512,1024]{1,0:T(8,128)(2,1)S(1)}, u32[]{:S(2)}, u32[]{:S(2)}) %collective-permute-start.29) | collective-permute-done | bytes 1048608 | tf_op jit(solution)/shard_map/ppermute | solution.py:71
  332.1 19.7 %collective-permute-done.35 = bf16[1024,512]{1,0:T(8,128)(2,1)S(1)} collective-permute-done((bf16[1024,512]{1,0:T(8,128)(2,1)}, bf16[1024,512]{1,0:T(8,128)(2,1)S(1)}, u32[]{:S(2)}, u32[]{:S(2)}) %collective-permute-start.35) | collective-permute-done | bytes 1048608 | tf_op jit(solution)/shard_map/ppermute | solution.py:71
  352.0 13.3 %multiply_convert_fusion = (bf16[1536,1024]{1,0:T(8,128)(2,1)S(1)}, f32[1536,1024]{1,0:T(8,128)}) fusion(bf16[2048,1024]{1,0:T(8,128)(2,1)S(1)} %constant_dynamic-update-slice_fusion.7, bf16[384,2048]{1,0:T(8,128)(2,1)S(1)} %collective-permute-done.23, bf16[384,2048]{1,0:T(8,128)(2,1)} %collective-permute-done.22, ...), kind=kOutput, calls=%fused_computation.9 | convolution fusion | flops 6475481088 | bytes 19922944 | tf_op jit(solution)/shard_map/dot_general | solution.py:17
  365.3 4.4 fusion.58
  369.9 9.2 %fusion.162 = (bf16[1536,2048]{1,0:T(8,128)(2,1)S(1)}, f32[1536,2048]{1,0:T(8,128)}) fusion(bf16[1536,1024]{1,0:T(8,128)(2,1)S(1)} %get-tuple-element.69, bf16[1024,2048]{1,0:T(8,128)(2,1)S(1)} %constant_dynamic-update-slice_fusion), kind=kOutput, calls=%fused_computation.308 | convolution fusion | flops 6445596672 | bytes 26214400 | tf_op jit(solution)/shard_map/dot_general | solution.py:17
  379.1 11.2 %fusion.6 = bf16[1536,1024]{1,0:T(8,128)(2,1)S(1)} fusion(f32[1536,1024]{1,0:T(8,128)} %get-tuple-element.70, bf16[1536,2048]{1,0:T(8,128)(2,1)} %copy-done.38, bf16[1024,2048]{1,0:T(8,128)(2,1)S(1)} %constant_dynamic-update-slice_fusion), kind=kOutput, calls=%fused_computation.7 | convolution fusion | flops 6458179584 | bytes 19922944 | tf_op jit(solution)/shard_map/dot_general | solution.py:25
  393.1 10.6 %fusion.161 = (bf16[1536,2048]{1,0:T(8,128)(2,1)}, f32[1536,2048]{1,0:T(8,128)}) fusion(bf16[1536,1024]{1,0:T(8,128)(2,1)S(1)} %fusion.6, bf16[2048,1024]{1,0:T(8,128)(2,1)S(1)} %constant_dynamic-update-slice_fusion.7), kind=kOutput, calls=%fused_computation.307 | convolution fusion | flops 6445596672 | bytes 26214400 | tf_op jit(solution)/shard_map/dot_general | solution.py:25
  415.6 4.2 add_convert_fusion.1
  420.3 23.1 %collective-permute-done.65 = bf16[512,1024]{1,0:T(8,128)(2,1)} collective-permute-done((bf16[512,1024]{1,0:T(8,128)(2,1)}, bf16[512,1024]{1,0:T(8,128)(2,1)}, u32[]{:S(2)}, u32[]{:S(2)}) %collective-permute-start.65) | collective-permute-done | bytes 1048608 | tf_op jit(solution)/shard_map/ppermute | solution.py:71
  443.4 4.5 add_convert_fusion.3
  448.0 17.9 %collective-permute-done.73 = bf16[1024,512]{1,0:T(8,128)(2,1)} collective-permute-done((bf16[1024,512]{1,0:T(8,128)(2,1)}, bf16[1024,512]{1,0:T(8,128)(2,1)}, u32[]{:S(2)}, u32[]{:S(2)}) %collective-permute-start.73) | collective-permute-done | bytes 1048608 | tf_op jit(solution)/shard_map/ppermute | solution.py:71
  465.9 3.5 add_convert_fusion
  482.4 5.9 collective-permute-done.66
  490.3 20.5 %collective-permute-done.74 = bf16[1024,512]{1,0:T(8,128)(2,1)S(1)} collective-permute-done((bf16[1024,512]{1,0:T(8,128)(2,1)S(1)}, bf16[1024,512]{1,0:T(8,128)(2,1)S(1)}, u32[]{:S(2)}, u32[]{:S(2)}) %collective-permute-start.74) | collective-permute-done | bytes 1048608 | tf_op jit(solution)/shard_map/ppermute | solution.py:71
  510.8 3.2 fusion.164
  517.4 26.3 %collective-permute-done.37 = bf16[384,2048]{1,0:T(8,128)(2,1)S(1)} collective-permute-done((bf16[384,2048]{1,0:T(8,128)(2,1)S(1)}, bf16[384,2048]{1,0:T(8,128)(2,1)S(1)}, u32[]{:S(2)}, u32[]{:S(2)}) %collective-permute-start.37) | collective-permute-done | bytes 1572896 | tf_op jit(solution)/shard_map/ppermute | solution.py:68
  555.7 30.0 %collective-permute-done.38 = bf16[384,2048]{1,0:T(8,128)(2,1)S(1)} collective-permute-done((bf16[384,2048]{1,0:T(8,128)(2,1)S(1)}, bf16[384,2048]{1,0:T(8,128)(2,1)S(1)}, u32[]{:S(2)}, u32[]{:S(2)}) %collective-permute-start.38) | collective-permute-done | bytes 1572896 | tf_op jit(solution)/shard_map/ppermute | solution.py:74
  585.6 5.5 fusion.153
  598.9 4.2 fusion.71
  603.1 3.2 multiply_reduce_fusion
  625.9 7.6 %fusion.165 = f32[768,2048]{1,0:T(8,128)S(1)} fusion(bf16[768,1536]{1,0:T(8,128)(2,1)S(1)} %bitcast_dynamic-update-slice_fusion, bf16[2048,1536]{1,0:T(8,128)(2,1)} %constant_dynamic-update-slice_fusion.22), kind=kOutput, calls=%fused_computation.311 | convolution fusion | flops 4831838208 | bytes 14942208 | tf_op jit(solution)/shard_map/dot_general | solution.py:25
  644.3 11.3 %collective-permute-done.51 = bf16[256,1536]{1,0:T(8,128)(2,1)S(1)} collective-permute-done((bf16[256,1536]{1,0:T(8,128)(2,1)S(1)}, bf16[256,1536]{1,0:T(8,128)(2,1)S(1)}, u32[]{:S(2)}, u32[]{:S(2)}) %collective-permute-start.51) | collective-permute-done | bytes 786464 | tf_op jit(solution)/shard_map/ppermute | solution.py:68
  657.3 23.1 %collective-permute-done.61 = bf16[512,256]{1,0:T(8,128)(2,1)S(1)} collective-permute-done((bf16[512,256]{1,0:T(8,128)(2,1)S(1)}, bf16[512,256]{1,0:T(8,128)(2,1)S(1)}, u32[]{:S(2)}, u32[]{:S(2)}) %collective-permute-start.61) | collective-permute-done | bytes 262176 | tf_op jit(solution)/shard_map/ppermute | solution.py:71
  683.9 7.2 collective-permute-done.58
  694.0 17.6 %collective-permute-done.49 = bf16[256,1536]{1,0:T(8,128)(2,1)S(1)} collective-permute-done((bf16[256,1536]{1,0:T(8,128)(2,1)S(1)}, bf16[256,1536]{1,0:T(8,128)(2,1)S(1)}, u32[]{:S(2)}, u32[]{:S(2)}) %collective-permute-start.49) | collective-permute-done | bytes 786464 | tf_op jit(solution)/shard_map/ppermute | solution.py:68
  712.3 4.9 collective-permute-done.57
  717.8 5.2 collective-permute-done.63
  728.2 8.8 %collective-permute-done.54 = bf16[256,1536]{1,0:T(8,128)(2,1)S(1)} collective-permute-done((bf16[256,1536]{1,0:T(8,128)(2,1)S(1)}, bf16[256,1536]{1,0:T(8,128)(2,1)S(1)}, u32[]{:S(2)}, u32[]{:S(2)}) %collective-permute-start.54) | collective-permute-done | bytes 786464 | tf_op jit(solution)/shard_map/ppermute | solution.py:71
  737.5 4.5 collective-permute-done.47
  (402 shorter events, 191.8 us)
Async XLA Ops:
  3.1 26.7 %collective-permute-start.10 = (s32[1,384]{1,0:T(1,128)S(1)}, s32[1,384]{1,0:T(1,128)S(1)}, u32[]{:S(2)}, u32[]{:S(2)}) collective-permute-start(s32[1,384]{1,0:T(1,128)S(1)} %copy-done.48), channel_id=1, source_target_pairs={{0,2},{2,0},{4,6},{6,4},{8,10},{10,8},{12,14},{14,12},{16,18},{18,... | collective-permute-start | bytes 4616 | tf_op jit(solution)/shard_map/ppermute | solution.py:68
  29.7 39.9 %collective-permute-start.5 = (bf16[256,1536]{1,0:T(8,128)(2,1)}, bf16[256,1536]{1,0:T(8,128)(2,1)S(1)}, u32[]{:S(2)}, u32[]{:S(2)}) collective-permute-start(bf16[256,1536]{1,0:T(8,128)(2,1)} %collective-permute-done.3), channel_id=1, source_target_pairs={{0,8},{2,10},{4,12},{6,14},{8,16},{10,18},{12,20},{14,22},{16,24},... | collective-permute-start | bytes 2359304 | tf_op jit(solution)/shard_map/ppermute | solution.py:71
  35.3 25.1 %collective-permute-start.14 = (bf16[512,256]{1,0:T(8,128)(2,1)}, bf16[512,256]{1,0:T(8,128)(2,1)S(1)}, u32[]{:S(2)}, u32[]{:S(2)}) collective-permute-start(bf16[512,256]{1,0:T(8,128)(2,1)} %collective-permute-done.13), channel_id=1, source_target_pairs={{0,4},{2,6},{4,0},{6,2},{8,12},{10,14},{12,8},{14,10},{16,20},{18,... | collective-permute-start | bytes 786440 | tf_op jit(solution)/shard_map/ppermute | solution.py:68
  37.1 34.3 %collective-permute-start.2 = (bf16[256,1536]{1,0:T(8,128)(2,1)}, bf16[256,1536]{1,0:T(8,128)(2,1)S(1)}, u32[]{:S(2)}, u32[]{:S(2)}) collective-permute-start(bf16[256,1536]{1,0:T(8,128)(2,1)} %get-tuple-element.19), channel_id=1, source_target_pairs={{0,4},{2,6},{4,0},{6,2},{8,12},{10,14},{12,8},{14,10},{16,20},{18,... | collective-permute-start | bytes 2359304 | tf_op jit(solution)/shard_map/ppermute | solution.py:68
  60.4 64.9 %collective-permute-start = (bf16[384,2048]{1,0:T(8,128)(2,1)S(1)}, bf16[384,2048]{1,0:T(8,128)(2,1)S(1)}, u32[]{:S(2)}, u32[]{:S(2)}) collective-permute-start(bf16[384,2048]{1,0:T(8,128)(2,1)S(1)} %fusion.11), channel_id=1, source_target_pairs={{0,2},{2,0},{4,6},{6,4},{8,10},{10,8},{12,14},{14,12},{16,18},{18,... | collective-permute-start | bytes 4718600 | tf_op jit(solution)/shard_map/ppermute | solution.py:68
  68.4 25.3 %collective-permute-start.4 = (bf16[256,1536]{1,0:T(8,128)(2,1)}, bf16[256,1536]{1,0:T(8,128)(2,1)S(1)}, u32[]{:S(2)}, u32[]{:S(2)}) collective-permute-start(bf16[256,1536]{1,0:T(8,128)(2,1)} %collective-permute-done.3), channel_id=1, source_target_pairs={{0,4},{2,6},{4,0},{6,2},{8,12},{10,14},{12,8},{14,10},{16,20},{18,... | collective-permute-start | bytes 2359304 | tf_op jit(solution)/shard_map/ppermute | solution.py:68
  72.4 38.1 %collective-permute-start.6 = (bf16[256,1536]{1,0:T(8,128)(2,1)S(1)}, bf16[256,1536]{1,0:T(8,128)(2,1)S(1)}, u32[]{:S(2)}, u32[]{:S(2)}) collective-permute-start(bf16[256,1536]{1,0:T(8,128)(2,1)S(1)} %collective-permute-done.5), channel_id=1, source_target_pairs={{0,4},{2,6},{4,0},{6,2},{8,12},{10,14},{12,8},{14,10},{16,20},{18,... | collective-permute-start | bytes 2359304 | tf_op jit(solution)/shard_map/ppermute | solution.py:68
  88.6 35.8 %collective-permute-start.8 = (bf16[256,1536]{1,0:T(8,128)(2,1)S(1)}, bf16[256,1536]{1,0:T(8,128)(2,1)S(1)}, u32[]{:S(2)}, u32[]{:S(2)}) collective-permute-start(bf16[256,1536]{1,0:T(8,128)(2,1)S(1)} %collective-permute-done.7), channel_id=1, source_target_pairs={{0,4},{2,6},{4,0},{6,2},{8,12},{10,14},{12,8},{14,10},{16,20},{18,... | collective-permute-start | bytes 2359304 | tf_op jit(solution)/shard_map/ppermute | solution.py:68
  154.3 64.8 %collective-permute-start.20 = (bf16[384,2048]{1,0:T(8,128)(2,1)S(1)}, bf16[384,2048]{1,0:T(8,128)(2,1)}, u32[]{:S(2)}, u32[]{:S(2)}) collective-permute-start(bf16[384,2048]{1,0:T(8,128)(2,1)S(1)} %fusion.26), channel_id=1, source_target_pairs={{0,1},{1,0},{2,3},{3,2},{4,5},{5,4},{6,7},{7,6},{8,9},{9,8},{10,11... | collective-permute-start | bytes 4718600 | tf_op jit(solution)/shard_map/ppermute | solution.py:74
  161.1 103.5 %collective-permute-start.40 = (bf16[384,2048]{1,0:T(8,128)(2,1)}, bf16[384,2048]{1,0:T(8,128)(2,1)}, u32[]{:S(2)}, u32[]{:S(2)}) collective-permute-start(bf16[384,2048]{1,0:T(8,128)(2,1)} %param.23), channel_id=1, source_target_pairs={{0,4},{2,6},{4,0},{6,2},{8,12},{10,14},{12,8},{14,10},{16,20},{18,... | collective-permute-start | bytes 4718600 | tf_op jit(solution)/shard_map/ppermute | solution.py:68
  162.5 51.5 %collective-permute-start.31 = (bf16[1024,128]{1,0:T(8,128)(2,1)S(1)}, bf16[1024,128]{1,0:T(8,128)(2,1)S(1)}, u32[]{:S(2)}, u32[]{:S(2)}) collective-permute-start(bf16[1024,128]{1,0:T(8,128)(2,1)S(1)} %get-tuple-element.44), channel_id=1, source_target_pairs={{0,4},{2,6},{4,0},{6,2},{8,12},{10,14},{12,8},{14,10},{16,20},{18,... | collective-permute-start | bytes 786440 | tf_op jit(solution)/shard_map/ppermute | solution.py:68
  169.0 48.9 %collective-permute-start.32 = (bf16[1024,128]{1,0:T(8,128)(2,1)S(1)}, bf16[1024,128]{1,0:T(8,128)(2,1)S(1)}, u32[]{:S(2)}, u32[]{:S(2)}) collective-permute-start(bf16[1024,128]{1,0:T(8,128)(2,1)S(1)} %get-tuple-element.41), channel_id=1, source_target_pairs={{0,6},{2,4},{4,2},{6,0},{8,14},{10,12},{12,10},{14,8},{16,22},{18,... | collective-permute-start | bytes 786440 | tf_op jit(solution)/shard_map/ppermute | solution.py:68
  173.0 96.0 %collective-permute-start.39 = (bf16[384,2048]{1,0:T(8,128)(2,1)}, bf16[384,2048]{1,0:T(8,128)(2,1)}, u32[]{:S(2)}, u32[]{:S(2)}) collective-permute-start(bf16[384,2048]{1,0:T(8,128)(2,1)} %param.23), channel_id=1, source_target_pairs={{0,2},{2,0},{4,6},{6,4},{8,10},{10,8},{12,14},{14,12},{16,18},{18,... | collective-permute-start | bytes 4718600 | tf_op jit(solution)/shard_map/ppermute | solution.py:68
  214.0 28.2 %collective-permute-start.27 = (bf16[512,1024]{1,0:T(8,128)(2,1)}, bf16[512,1024]{1,0:T(8,128)(2,1)}, u32[]{:S(2)}, u32[]{:S(2)}) collective-permute-start(bf16[512,1024]{1,0:T(8,128)(2,1)} %constant_dynamic-update-slice_fusion.11), channel_id=1, source_target_pairs={{0,8},{2,10},{4,12},{6,14},{8,16},{10,18},{12,20},{14,22},{16,24},... | collective-permute-start | bytes 3145736 | tf_op jit(solution)/shard_map/ppermute | solution.py:71
  218.6 46.0 %collective-permute-start.33 = (bf16[1024,512]{1,0:T(8,128)(2,1)}, bf16[1024,512]{1,0:T(8,128)(2,1)}, u32[]{:S(2)}, u32[]{:S(2)}) collective-permute-start(bf16[1024,512]{1,0:T(8,128)(2,1)} %constant_dynamic-update-slice_fusion.4), channel_id=1, source_target_pairs={{0,8},{2,10},{4,12},{6,14},{8,16},{10,18},{12,20},{14,22},{16,24},... | collective-permute-start | bytes 3145736 | tf_op jit(solution)/shard_map/ppermute | solution.py:71
  223.7 45.7 %collective-permute-start.22 = (bf16[384,2048]{1,0:T(8,128)(2,1)}, bf16[384,2048]{1,0:T(8,128)(2,1)}, u32[]{:S(2)}, u32[]{:S(2)}) collective-permute-start(bf16[384,2048]{1,0:T(8,128)(2,1)} %fusion.29), channel_id=1, source_target_pairs={{0,4},{2,6},{4,0},{6,2},{8,12},{10,14},{12,8},{14,10},{16,20},{18,... | collective-permute-start | bytes 4718600 | tf_op jit(solution)/shard_map/ppermute | solution.py:68
  242.2 44.9 %collective-permute-start.28 = (bf16[512,1024]{1,0:T(8,128)(2,1)}, bf16[512,1024]{1,0:T(8,128)(2,1)}, u32[]{:S(2)}, u32[]{:S(2)}) collective-permute-start(bf16[512,1024]{1,0:T(8,128)(2,1)} %collective-permute-done.27), channel_id=1, source_target_pairs={{0,8},{2,10},{4,12},{6,14},{8,16},{10,18},{12,20},{14,22},{16,24},... | collective-permute-start | bytes 3145736 | tf_op jit(solution)/shard_map/ppermute | solution.py:71
  264.7 44.9 %collective-permute-start.34 = (bf16[1024,512]{1,0:T(8,128)(2,1)}, bf16[1024,512]{1,0:T(8,128)(2,1)}, u32[]{:S(2)}, u32[]{:S(2)}) collective-permute-start(bf16[1024,512]{1,0:T(8,128)(2,1)} %collective-permute-done.33), channel_id=1, source_target_pairs={{0,8},{2,10},{4,12},{6,14},{8,16},{10,18},{12,20},{14,22},{16,24},... | collective-permute-start | bytes 3145736 | tf_op jit(solution)/shard_map/ppermute | solution.py:71
  264.7 50.7 %collective-permute-start.41 = (bf16[384,2048]{1,0:T(8,128)(2,1)}, bf16[384,2048]{1,0:T(8,128)(2,1)S(1)}, u32[]{:S(2)}, u32[]{:S(2)}) collective-permute-start(bf16[384,2048]{1,0:T(8,128)(2,1)} %collective-permute-done.40), channel_id=1, source_target_pairs={{0,2},{2,0},{4,6},{6,4},{8,10},{10,8},{12,14},{14,12},{16,18},{18,... | collective-permute-start | bytes 4718600 | tf_op jit(solution)/shard_map/ppermute | solution.py:68
  268.9 83.1 %collective-permute-start.21 = (bf16[384,2048]{1,0:T(8,128)(2,1)}, bf16[384,2048]{1,0:T(8,128)(2,1)S(1)}, u32[]{:S(2)}, u32[]{:S(2)}) collective-permute-start(bf16[384,2048]{1,0:T(8,128)(2,1)} %fusion.29), channel_id=1, source_target_pairs={{0,2},{2,0},{4,6},{6,4},{8,10},{10,8},{12,14},{14,12},{16,18},{18,... | collective-permute-start | bytes 4718600 | tf_op jit(solution)/shard_map/ppermute | solution.py:68
  269.4 82.6 %collective-permute-start.23 = (bf16[384,2048]{1,0:T(8,128)(2,1)}, bf16[384,2048]{1,0:T(8,128)(2,1)S(1)}, u32[]{:S(2)}, u32[]{:S(2)}) collective-permute-start(bf16[384,2048]{1,0:T(8,128)(2,1)} %collective-permute-done.22), channel_id=1, source_target_pairs={{0,2},{2,0},{4,6},{6,4},{8,10},{10,8},{12,14},{14,12},{16,18},{18,... | collective-permute-start | bytes 4718600 | tf_op jit(solution)/shard_map/ppermute | solution.py:68
  287.1 44.8 %collective-permute-start.29 = (bf16[512,1024]{1,0:T(8,128)(2,1)}, bf16[512,1024]{1,0:T(8,128)(2,1)S(1)}, u32[]{:S(2)}, u32[]{:S(2)}) collective-permute-start(bf16[512,1024]{1,0:T(8,128)(2,1)} %collective-permute-done.28), channel_id=1, source_target_pairs={{0,8},{2,10},{4,12},{6,14},{8,16},{10,18},{12,20},{14,22},{16,24},... | collective-permute-start | bytes 3145736 | tf_op jit(solution)/shard_map/ppermute | solution.py:71
  309.6 42.2 %collective-permute-start.35 = (bf16[1024,512]{1,0:T(8,128)(2,1)}, bf16[1024,512]{1,0:T(8,128)(2,1)S(1)}, u32[]{:S(2)}, u32[]{:S(2)}) collective-permute-start(bf16[1024,512]{1,0:T(8,128)(2,1)} %collective-permute-done.34), channel_id=1, source_target_pairs={{0,8},{2,10},{4,12},{6,14},{8,16},{10,18},{12,20},{14,22},{16,24},... | collective-permute-start | bytes 3145736 | tf_op jit(solution)/shard_map/ppermute | solution.py:71
  369.6 45.7 %collective-permute-start.72 = (bf16[1024,512]{1,0:T(8,128)(2,1)S(1)}, bf16[1024,512]{1,0:T(8,128)(2,1)S(1)}, u32[]{:S(2)}, u32[]{:S(2)}) collective-permute-start(bf16[1024,512]{1,0:T(8,128)(2,1)S(1)} %fusion.58), channel_id=1, source_target_pairs={{0,8},{2,10},{4,12},{6,14},{8,16},{10,18},{12,20},{14,22},{16,24},... | collective-permute-start | bytes 3145736 | tf_op jit(solution)/shard_map/ppermute | solution.py:71
  393.0 82.4 %collective-permute-start.36 = (bf16[768,2048]{1,0:T(8,128)(2,1)}, bf16[768,2048]{1,0:T(8,128)(2,1)}, u32[]{:S(2)}, u32[]{:S(2)}) collective-permute-start(bf16[768,2048]{1,0:T(8,128)(2,1)} %pad_maximum_fusion.5), channel_id=1, source_target_pairs={{0,2},{2,0},{4,6},{6,4},{8,10},{10,8},{12,14},{14,12},{16,18},{18,... | collective-permute-start | bytes 9437192 | tf_op jit(solution)/shard_map/ppermute | solution.py:68
  408.0 61.5 %collective-permute-start.42 = (bf16[768,2048]{1,0:T(8,128)(2,1)}, bf16[768,2048]{1,0:T(8,128)(2,1)}, u32[]{:S(2)}, u32[]{:S(2)}) collective-permute-start(bf16[768,2048]{1,0:T(8,128)(2,1)} %pad_maximum_fusion.6), channel_id=1, source_target_pairs={{0,2},{2,0},{4,6},{6,4},{8,10},{10,8},{12,14},{14,12},{16,18},{18,... | collective-permute-start | bytes 9437192 | tf_op jit(solution)/shard_map/ppermute | solution.py:68
  415.0 28.5 %collective-permute-start.65 = (bf16[512,1024]{1,0:T(8,128)(2,1)}, bf16[512,1024]{1,0:T(8,128)(2,1)}, u32[]{:S(2)}, u32[]{:S(2)}) collective-permute-start(bf16[512,1024]{1,0:T(8,128)(2,1)} %fusion.55), channel_id=1, source_target_pairs={{0,8},{2,10},{4,12},{6,14},{8,16},{10,18},{12,20},{14,22},{16,24},... | collective-permute-start | bytes 3145736 | tf_op jit(solution)/shard_map/ppermute | solution.py:71
  419.8 46.1 %collective-permute-start.73 = (bf16[1024,512]{1,0:T(8,128)(2,1)}, bf16[1024,512]{1,0:T(8,128)(2,1)}, u32[]{:S(2)}, u32[]{:S(2)}) collective-permute-start(bf16[1024,512]{1,0:T(8,128)(2,1)} %add_convert_fusion.1), channel_id=1, source_target_pairs={{0,8},{2,10},{4,12},{6,14},{8,16},{10,18},{12,20},{14,22},{16,24},... | collective-permute-start | bytes 3145736 | tf_op jit(solution)/shard_map/ppermute | solution.py:71
  447.9 40.4 %collective-permute-start.66 = (bf16[512,1024]{1,0:T(8,128)(2,1)S(1)}, bf16[512,1024]{1,0:T(8,128)(2,1)S(1)}, u32[]{:S(2)}, u32[]{:S(2)}) collective-permute-start(bf16[512,1024]{1,0:T(8,128)(2,1)S(1)} %add_convert_fusion.3), channel_id=1, source_target_pairs={{0,8},{2,10},{4,12},{6,14},{8,16},{10,18},{12,20},{14,22},{16,24},... | collective-permute-start | bytes 3145736 | tf_op jit(solution)/shard_map/ppermute | solution.py:71
  469.5 41.3 %collective-permute-start.74 = (bf16[1024,512]{1,0:T(8,128)(2,1)S(1)}, bf16[1024,512]{1,0:T(8,128)(2,1)S(1)}, u32[]{:S(2)}, u32[]{:S(2)}) collective-permute-start(bf16[1024,512]{1,0:T(8,128)(2,1)S(1)} %add_convert_fusion), channel_id=1, source_target_pairs={{0,8},{2,10},{4,12},{6,14},{8,16},{10,18},{12,20},{14,22},{16,24},... | collective-permute-start | bytes 3145736 | tf_op jit(solution)/shard_map/ppermute | solution.py:71
  474.9 39.1 %collective-permute-start.43 = (bf16[384,2048]{1,0:T(8,128)(2,1)S(1)}, bf16[384,2048]{1,0:T(8,128)(2,1)S(1)}, u32[]{:S(2)}, u32[]{:S(2)}) collective-permute-start(bf16[384,2048]{1,0:T(8,128)(2,1)S(1)} %fusion.20), channel_id=1, source_target_pairs={{0,4},{2,6},{4,0},{6,2},{8,12},{10,14},{12,8},{14,10},{16,20},{18,... | collective-permute-start | bytes 4718600 | tf_op jit(solution)/shard_map/ppermute | solution.py:68
  480.8 62.9 %collective-permute-start.37 = (bf16[384,2048]{1,0:T(8,128)(2,1)S(1)}, bf16[384,2048]{1,0:T(8,128)(2,1)S(1)}, u32[]{:S(2)}, u32[]{:S(2)}) collective-permute-start(bf16[384,2048]{1,0:T(8,128)(2,1)S(1)} %fusion.23), channel_id=1, source_target_pairs={{0,4},{2,6},{4,0},{6,2},{8,12},{10,14},{12,8},{14,10},{16,20},{18,... | collective-permute-start | bytes 4718600 | tf_op jit(solution)/shard_map/ppermute | solution.py:68
  490.2 58.8 %collective-permute-start.67 = (bf16[512,1024]{1,0:T(8,128)(2,1)S(1)}, bf16[512,1024]{1,0:T(8,128)(2,1)}, u32[]{:S(2)}, u32[]{:S(2)}) collective-permute-start(bf16[512,1024]{1,0:T(8,128)(2,1)S(1)} %add_convert_fusion.2), channel_id=1, source_target_pairs={{0,8},{2,10},{4,12},{6,14},{8,16},{10,18},{12,20},{14,22},{16,24},... | collective-permute-start | bytes 3145736 | tf_op jit(solution)/shard_map/ppermute | solution.py:71
  516.8 37.4 %collective-permute-start.44 = (bf16[384,2048]{1,0:T(8,128)(2,1)S(1)}, bf16[384,2048]{1,0:T(8,128)(2,1)S(1)}, u32[]{:S(2)}, u32[]{:S(2)}) collective-permute-start(bf16[384,2048]{1,0:T(8,128)(2,1)S(1)} %fusion.22), channel_id=1, source_target_pairs={{0,1},{1,0},{2,3},{3,2},{4,5},{5,4},{6,7},{7,6},{8,9},{9,8},{10,11... | collective-permute-start | bytes 4718600 | tf_op jit(solution)/shard_map/ppermute | solution.py:74
  546.5 39.1 %collective-permute-start.38 = (bf16[384,2048]{1,0:T(8,128)(2,1)S(1)}, bf16[384,2048]{1,0:T(8,128)(2,1)S(1)}, u32[]{:S(2)}, u32[]{:S(2)}) collective-permute-start(bf16[384,2048]{1,0:T(8,128)(2,1)S(1)} %fusion.25), channel_id=1, source_target_pairs={{0,1},{1,0},{2,3},{3,2},{4,5},{5,4},{6,7},{7,6},{8,9},{9,8},{10,11... | collective-permute-start | bytes 4718600 | tf_op jit(solution)/shard_map/ppermute | solution.py:74
  547.9 43.2 %collective-permute-start.75 = (bf16[1024,128]{1,0:T(8,128)(2,1)S(1)}, bf16[1024,128]{1,0:T(8,128)(2,1)S(1)}, u32[]{:S(2)}, u32[]{:S(2)}) collective-permute-start(bf16[1024,128]{1,0:T(8,128)(2,1)S(1)} %get-tuple-element.37), channel_id=1, source_target_pairs={{0,2},{2,0},{4,6},{6,4},{8,10},{10,8},{12,14},{14,12},{16,18},{18,... | collective-permute-start | bytes 786440 | tf_op jit(solution)/shard_map/ppermute | solution.py:68
  547.9 43.9 %collective-permute-start.76 = (bf16[1024,128]{1,0:T(8,128)(2,1)S(1)}, bf16[1024,128]{1,0:T(8,128)(2,1)S(1)}, u32[]{:S(2)}, u32[]{:S(2)}) collective-permute-start(bf16[1024,128]{1,0:T(8,128)(2,1)S(1)} %get-tuple-element.36), channel_id=1, source_target_pairs={{0,4},{2,6},{4,0},{6,2},{8,12},{10,14},{12,8},{14,10},{16,20},{18,... | collective-permute-start | bytes 786440 | tf_op jit(solution)/shard_map/ppermute | solution.py:68
  552.1 39.8 %collective-permute-start.68 = (bf16[128,1024]{1,0:T(8,128)(2,1)S(1)}, bf16[128,1024]{1,0:T(8,128)(2,1)S(1)}, u32[]{:S(2)}, u32[]{:S(2)}) collective-permute-start(bf16[128,1024]{1,0:T(8,128)(2,1)S(1)} %get-tuple-element.40), channel_id=1, source_target_pairs={{0,2},{2,0},{4,6},{6,4},{8,10},{10,8},{12,14},{14,12},{16,18},{18,... | collective-permute-start | bytes 786440 | tf_op jit(solution)/shard_map/ppermute | solution.py:68
  554.2 37.8 %collective-permute-start.69 = (bf16[128,1024]{1,0:T(8,128)(2,1)S(1)}, bf16[128,1024]{1,0:T(8,128)(2,1)S(1)}, u32[]{:S(2)}, u32[]{:S(2)}) collective-permute-start(bf16[128,1024]{1,0:T(8,128)(2,1)S(1)} %get-tuple-element.39), channel_id=1, source_target_pairs={{0,4},{2,6},{4,0},{6,2},{8,12},{10,14},{12,8},{14,10},{16,20},{18,... | collective-permute-start | bytes 786440 | tf_op jit(solution)/shard_map/ppermute | solution.py:68
  612.3 44.9 %collective-permute-start.59 = (bf16[512,256]{1,0:T(8,128)(2,1)}, bf16[512,256]{1,0:T(8,128)(2,1)}, u32[]{:S(2)}, u32[]{:S(2)}) collective-permute-start(bf16[512,256]{1,0:T(8,128)(2,1)} %dynamic-slice_convert_fusion.6), channel_id=1, source_target_pairs={{0,4},{2,6},{4,0},{6,2},{8,12},{10,14},{12,8},{14,10},{16,20},{18,... | collective-permute-start | bytes 786440 | tf_op jit(solution)/shard_map/ppermute | solution.py:68
  616.0 39.8 %collective-permute-start.60 = (bf16[512,256]{1,0:T(8,128)(2,1)}, bf16[512,256]{1,0:T(8,128)(2,1)}, u32[]{:S(2)}, u32[]{:S(2)}) collective-permute-start(bf16[512,256]{1,0:T(8,128)(2,1)} %dynamic-slice_convert_fusion.5), channel_id=1, source_target_pairs={{0,4},{2,6},{4,0},{6,2},{8,12},{10,14},{12,8},{14,10},{16,20},{18,... | collective-permute-start | bytes 786440 | tf_op jit(solution)/shard_map/ppermute | solution.py:68
  638.0 44.4 %collective-permute-start.50 = (bf16[256,1536]{1,0:T(8,128)(2,1)S(1)}, bf16[256,1536]{1,0:T(8,128)(2,1)S(1)}, u32[]{:S(2)}, u32[]{:S(2)}) collective-permute-start(bf16[256,1536]{1,0:T(8,128)(2,1)S(1)} %dynamic-slice_convert_fusion.1), channel_id=1, source_target_pairs={{0,4},{2,6},{4,0},{6,2},{8,12},{10,14},{12,8},{14,10},{16,20},{18,... | collective-permute-start | bytes 2359304 | tf_op jit(solution)/shard_map/ppermute | solution.py:68
  640.5 51.5 %collective-permute-start.46 = (bf16[384,2048]{1,0:T(8,128)(2,1)S(1)}, bf16[384,2048]{1,0:T(8,128)(2,1)S(1)}, u32[]{:S(2)}, u32[]{:S(2)}) collective-permute-start(bf16[384,2048]{1,0:T(8,128)(2,1)S(1)} %slice.156), channel_id=1, source_target_pairs={{0,2},{2,0},{4,6},{6,4},{8,10},{10,8},{12,14},{14,12},{16,18},{18,... | collective-permute-start | bytes 4718600 | tf_op jit(solution)/shard_map/ppermute | solution.py:68
  655.8 27.7 %collective-permute-start.52 = (bf16[256,1536]{1,0:T(8,128)(2,1)S(1)}, bf16[256,1536]{1,0:T(8,128)(2,1)S(1)}, u32[]{:S(2)}, u32[]{:S(2)}) collective-permute-start(bf16[256,1536]{1,0:T(8,128)(2,1)S(1)} %add_convert_fusion.6), channel_id=1, source_target_pairs={{0,8},{2,10},{4,12},{6,14},{8,16},{10,18},{12,20},{14,22},{16,24},... | collective-permute-start | bytes 2359304 | tf_op jit(solution)/shard_map/ppermute | solution.py:71
  657.2 66.2 %collective-permute-start.77 = (bf16[1024,128]{1,0:T(8,128)(2,1)S(1)}, bf16[1024,128]{1,0:T(8,128)(2,1)S(1)}, u32[]{:S(2)}, u32[]{:S(2)}) collective-permute-start(bf16[1024,128]{1,0:T(8,128)(2,1)S(1)} %copy-done.39), channel_id=1, source_target_pairs={{0,6},{2,4},{4,2},{6,0},{8,14},{10,12},{12,10},{14,8},{16,22},{18,... | collective-permute-start | bytes 786440 | tf_op jit(solution)/shard_map/ppermute | solution.py:68
  680.3 44.0 %collective-permute-start.71 = (f32[128]{0:T(128)S(1)}, f32[128]{0:T(128)S(1)}, u32[]{:S(2)}, u32[]{:S(2)}) collective-permute-start(f32[128]{0:T(128)S(1)} %get-tuple-element.31), channel_id=1, source_target_pairs={{0,1},{1,0},{2,3},{3,2},{4,5},{5,4},{6,7},{7,6},{8,9},{9,8},{10,11... | collective-permute-start | bytes 1544 | tf_op jit(solution)/shard_map/ppermute | solution.py:74
  692.1 25.1 %collective-permute-start.57 = (bf16[512,256]{1,0:T(8,128)(2,1)S(1)}, bf16[512,256]{1,0:T(8,128)(2,1)S(1)}, u32[]{:S(2)}, u32[]{:S(2)}) collective-permute-start(bf16[512,256]{1,0:T(8,128)(2,1)S(1)} %dynamic-slice_convert_fusion.8), channel_id=1, source_target_pairs={{0,4},{2,6},{4,0},{6,2},{8,12},{10,14},{12,8},{14,10},{16,20},{18,... | collective-permute-start | bytes 786440 | tf_op jit(solution)/shard_map/ppermute | solution.py:68
  717.1 24.8 %collective-permute-start.47 = (bf16[384,2048]{1,0:T(8,128)(2,1)S(1)}, bf16[384,2048]{1,0:T(8,128)(2,1)S(1)}, u32[]{:S(2)}, u32[]{:S(2)}) collective-permute-start(bf16[384,2048]{1,0:T(8,128)(2,1)S(1)} %fusion.19), channel_id=1, source_target_pairs={{0,1},{1,0},{2,3},{3,2},{4,5},{5,4},{6,7},{7,6},{8,9},{9,8},{10,11... | collective-permute-start | bytes 4718600 | tf_op jit(solution)/shard_map/ppermute | solution.py:74
  (90 other events, 981.7 us)

commit v2 on v1

v2 whole, which is shorter than its diff:
```python
import functools
import math

import jax
import jax.numpy as jnp
from jax import lax
from jax.sharding import PartitionSpec as P

HEAD_DIM = 128
EPSILON = 1e-05
MASKED = -1e30
LOW = jnp.bfloat16
WIDE = jnp.float32


def plain(one, two):
    return jnp.dot(one, two, preferred_element_type=WIDE)


def inner(one, two):
    return lax.dot_general(one, two, (((0,), (0,)), ((), ())), preferred_element_type=WIDE)


def outer(one, two):
    return lax.dot_general(one, two, (((1,), (1,)), ((), ())), preferred_element_type=WIDE)


def norm_forward(values):
    centered = values - jnp.mean(values, axis=1, keepdims=True)
    inverse = lax.rsqrt(jnp.mean(centered * centered, axis=1, keepdims=True) + EPSILON)
    return centered * inverse, inverse


def norm_backward(scaled, standard, inverse):
    return (
        scaled
        - jnp.mean(scaled, axis=1, keepdims=True)
        - standard * jnp.mean(scaled * standard, axis=1, keepdims=True)
    ) * inverse


def gelu_parts(values):
    half = 0.5 * (1.0 + lax.erf(values * (1.0 / math.sqrt(2.0))))
    slope = half + values * jnp.exp(-0.5 * values * values) * (1.0 / math.sqrt(2.0 * math.pi))
    return values * half, slope


def take(values, index, size, axis):
    return lax.dynamic_slice_in_dim(values, index * size, size, axis)


def put(whole, part, index, axis):
    return lax.dynamic_update_slice_in_dim(whole, part, index * part.shape[axis], axis)


def wide(values):
    return values.astype(WIDE)


class Order:
    def __init__(self, token):
        self.token = token

    def tie(self, *values):
        tied = lax.optimization_barrier((*values, self.token))[:-1]
        return tied if len(tied) > 1 else tied[0]

    def wait(self, *values):
        *values, self.token = lax.optimization_barrier((*values, self.token))
        return values if len(values) > 1 else values[0]

    def run(self, step, *values):
        values = lax.optimization_barrier((*values, self.token))[:-1]
        results = step(*values)
        if not isinstance(results, tuple):
            return self.wait(results)
        return self.wait(*results)


class Links:
    def __init__(self, count, order):
        self.order = order
        self.ring_size = count // 4
        self.to = {k: [(i, i ^ k) for i in range(count)] for k in (1, 2, 3)}
        self.next = [(i, (i + 4) % count) for i in range(count)]
        place = lax.axis_index("dp")
        self.ring_at = place // 4
        self.cell = place % 4
        self.row = self.cell // 2
        self.core = self.cell % 2

    def swap(self, values, k):
        return lax.ppermute(self.order.tie(values), "dp", self.to[k])

    def step(self, values):
        return lax.ppermute(self.order.tie(values), "dp", self.next)

    def across(self, values):
        return lax.ppermute(self.order.tie(values), "mp", [(0, 1), (1, 0)])

    def behind(self, k):
        return lax.rem(self.ring_at - k + 2 * self.ring_size, self.ring_size)

    def by_core(self, own, other, axis):
        return jnp.where(
            self.core == 0,
            jnp.concatenate([own, other], axis=axis),
            jnp.concatenate([other, own], axis=axis),
        )

    def join(self, parts, axis):
        shape = list(parts[0].shape)
        shape[axis] *= len(parts)
        joined = jnp.zeros(shape, parts[0].dtype)
        for k, part in enumerate(parts):
            joined = put(joined, part, self.cell ^ k, axis)
        return joined

    def lay(self, blocks, axis):
        shape = list(blocks[0].shape)
        shape[axis] *= len(blocks)
        whole = jnp.zeros(shape, blocks[0].dtype)
        for k, block in enumerate(blocks):
            whole = put(whole, block, self.behind(k), axis)
        return whole

    def lay_pairs(self, near, far, axis):
        shape = list(near[0].shape)
        shape[axis] *= 2 * len(near)
        whole = jnp.zeros(shape, near[0].dtype)
        for k in range(len(near)):
            at = self.behind(k) * 2
            whole = put(whole, near[k], at + self.row, axis)
            whole = put(whole, far[k], at + 1 - self.row, axis)
        return whole


def shards(
    count,
    tokens,
    doc_ids,
    frame_ids,
    gain_attn,
    w_query,
    w_key,
    w_value,
    w_output,
    gain_mlp,
    w_up,
    w_down,
    d_out,
):
    order = Order(doc_ids)
    run, wait = order.run, order.wait
    links = Links(count, order)
    swap, step, across = links.swap, links.step, links.across
    ring = links.ring_size
    rows, width = tokens.shape
    owned = width // count
    half = w_query.shape[1] // 2
    heads = half // HEAD_DIM
    hidden_part = w_up.shape[1] // 4
    block = width // ring
    pair = block // 2
    others = range(1, ring)

    chunk = rows // 2

    def chunks(values):
        return values[:chunk], values[chunk:]

    def qkv_shard(core, gain, *weights):
        taken = [(wide(take(w, core, half, 1)) * gain[:, None]).astype(LOW) for w in weights]
        return jnp.concatenate(taken, axis=1)

    qkv_send = run(
        lambda *w: qkv_shard(1 - links.core, *w), gain_attn, w_query, w_key, w_value
    )
    qkv_other = swap(qkv_send, 1)
    out_other = swap(run(lambda w: take(w, 1 - links.core, half, 0), w_output), 1)
    qkv_own = run(lambda *w: qkv_shard(links.core, *w), gain_attn, w_query, w_key, w_value)
    qkv_other, out_other = wait(qkv_other, out_other)
    qkv_block, out_block = run(
        lambda a, b, w, o: (
            links.by_core(a, b, 0),
            links.by_core(take(w, links.core, half, 0), o, 1),
        ),
        qkv_own,
        qkv_other,
        w_output,
        out_other,
    )

    qkv_next, out_next, qkv_far = step(qkv_block), step(out_block), swap(qkv_block, 2)

    def up_shard(weight, gain):
        scaled = (wide(weight) * gain[:, None]).astype(LOW)
        return tuple(take(scaled, links.cell ^ k, hidden_part, 1) for k in (0, 2, 1, 3))

    up_own, up_row, up_core, up_last = run(up_shard, w_up, gain_mlp)
    up_row, up_core = swap(up_row, 2), swap(up_core, 1)
    normed_own = run(lambda x: norm_forward(wide(x))[0].astype(LOW), tokens)
    normed_other = swap(normed_own, 1)
    docs_other, frames_other = swap(doc_ids, 1), swap(frame_ids, 1)

    def put_near(whole, part, k, axis):
        return put(whole, part, links.behind(k) * 2 + links.row, axis)

    def put_far(whole, part, k, axis):
        return put(whole, part, links.behind(k) * 2 + 1 - links.row, axis)

    qkv_full = jnp.zeros((width, 3 * half), LOW)
    out_full = jnp.zeros((half, width), LOW)
    qkv_full, out_full = run(
        lambda q, o, a, b: (put_near(q, a, 0, 0), put_near(o, b, 0, 1)),
        qkv_full,
        out_full,
        qkv_block,
        out_block,
    )
    down_parts = run(
        lambda w: tuple(take(w, links.cell ^ k, hidden_part, 0) for k in range(4)), w_down
    )
    out_blocks = [out_block]
    for k in others:
        if k == 2 or ring < 3:
            qkv_block, out_block, qkv_far, up_row, up_core = wait(
                qkv_next, out_next, qkv_far, up_row, up_core
            )
        elif k == 3:
            qkv_block, out_block, qkv_far, up_last = wait(qkv_next, out_next, qkv_far, up_last)
        else:
            qkv_block, out_block, qkv_far = wait(qkv_next, out_next, qkv_far)
        if k < ring - 1:
            qkv_next, out_next = step(qkv_block), step(out_block)
        qkv_far, far_arrived = swap(qkv_block, 2), qkv_far
        if k == 1:
            up_last = swap(up_last, 3)
        out_blocks.append(out_block)
        if k == ring - 1:
            out_far = swap(out_blocks[0], 2)
            up_block = run(
                lambda *p: links.join(p, 0), up_own, up_core, up_row, up_last
            )
            up_next = step(up_block)
        qkv_full, out_full = run(
            lambda q, o, a, b, f: (
                put_far(put_near(q, a, k, 0), f, k - 1, 0),
                put_near(o, b, k, 1),
            ),
            qkv_full,
            out_full,
            qkv_block,
            out_block,
            far_arrived,
        )
    normed_other, docs_other, frames_other = wait(normed_other, docs_other, frames_other)
    normed_one = run(lambda a, b: jnp.concatenate([a, b], axis=0), normed_own, normed_other)
    up_full = jnp.zeros((width, hidden_part), LOW)
    up_full = run(lambda w, b: put(w, b, links.behind(0), 0), up_full, up_block)
    up_block, qkv_far, out_far = wait(up_next, qkv_far, out_far)
    if ring > 2:
        up_next = step(up_block)
    out_fars = [out_far] + [swap(out_blocks[k], 2) for k in others]
    down_own, down_core, down_row, down_last = down_parts
    down_row = swap(down_row, 2)
    d_out_core = swap(d_out, 1)
    qkv_full = run(lambda w, f: put_far(w, f, ring - 1, 0), qkv_full, qkv_far)
    qkv = run(lambda a, b: plain(a, b).astype(LOW), normed_one, qkv_full)

    def heads_of(values):
        return values.reshape(2, rows, heads, HEAD_DIM)

    factor = 1.0 / math.sqrt(HEAD_DIM)

    def attention(qkv, docs_own, docs_other, frames_own, frames_other):
        docs = jnp.concatenate([docs_own, docs_other], axis=0)
        frames = jnp.concatenate([frames_own, frames_other], axis=0)
        allowed = docs[:, :, None] == docs[:, None, :]
        allowed &= frames[:, None, :] <= frames[:, :, None]
        query, key, value = (heads_of(qkv[:, i * half : (i + 1) * half]) for i in range(3))
        scores = jnp.einsum("gqhe,gkhe->ghqk", query, key, preferred_element_type=WIDE) * factor
        scores = jnp.where(allowed[:, None], scores, MASKED)
        shifted = jnp.exp(scores - jnp.max(scores, axis=3, keepdims=True))
        probs = shifted / jnp.sum(shifted, axis=3, keepdims=True)
        attended = jnp.einsum("ghqk,gkhe->gqhe", probs.astype(LOW), value, preferred_element_type=WIDE)
        return attended.astype(LOW).reshape(2 * rows, half), probs, query, key, value

    attended, probs, query, key, value = run(
        attention, qkv, doc_ids, docs_other, frame_ids, frames_other
    )
    out_full = run(lambda w, f: put_far(w, f, 0, 1), out_full, out_fars[0])
    if ring > 2:
        up_arrived, down_row, *out_fars[1:] = wait(up_next, down_row, *out_fars[1:])
        if ring > 3:
            up_next = step(up_arrived)
    else:
        up_arrived = up_block
        down_row, *out_fars[1:] = wait(down_row, *out_fars[1:])
    down_last, down_core = swap(down_last, 3), swap(down_core, 1)
    d_out_chunks = chunks(d_out)
    d_out_far = [swap(d_out_chunks[0], 2)]

    def put_fars(whole, *fars):
        for k, far in zip(others, fars):
            whole = put_far(whole, far, k, 1)
        return whole

    out_full = run(put_fars, out_full, *out_fars[1:])
    yours = run(lambda a, w: chunks(plain(a[rows:], w).astype(LOW)), attended, out_full)
    yours = [swap(part, 1) for part in yours]
    mine = run(lambda a, w: chunks(plain(a[:rows], w)), attended, out_full)
    out_low, out_cross = [], []
    for j in range(2):
        out_low.append(run(lambda a, b: (a + wide(b)).astype(LOW), mine[j], wait(yours[j])))
        out_cross.append(across(out_low[j]))
    up_full = run(
        lambda w, a, b: put(put(w, a, links.behind(1), 0), b, links.behind(min(2, ring - 1)), 0),
        up_full,
        up_block,
        up_arrived,
    )
    down_last, down_core = wait(down_last, down_core)
    down_block = run(
        lambda *p: links.join(p, 1), down_own, down_core, down_row, down_last
    )
    for k in range(3, ring):
        up_block = wait(up_next)
        if k < ring - 1:
            up_next = step(up_block)
        else:
            down_next = step(down_block)
        if k == ring - 1:
            out_cross[0], d_out_core, d_out_far[0] = wait(out_cross[0], d_out_core, d_out_far[0])
            d_out_far.append(swap(d_out_chunks[1], 2))
        else:
            up_full = run(lambda w, b: put(w, b, links.behind(k), 0), up_full, up_block)
    if ring <= 3:
        out_cross[0], d_out_core, d_out_far[0] = wait(out_cross[0], d_out_core, d_out_far[0])
        d_out_far.append(swap(d_out_chunks[1], 2))
        down_next = step(down_block)
    d_out_last = [swap(d_out_far[0], 1)]

    def second_norm(tokens, low, cross):
        hidden = wide(tokens) + (wide(low) + wide(cross))
        standard, inverse = norm_forward(hidden)
        return hidden, standard, inverse, standard.astype(LOW)

    token_chunks = chunks(tokens)
    seconds, far_two, core_two = [], [], []
    for j in range(2):
        if j:
            out_cross[j] = wait(out_cross[j])
        seconds.append(run(second_norm, token_chunks[j], out_low[j], out_cross[j]))
        far_two.append(swap(seconds[j][3], 2))
        core_two.append(swap(seconds[j][3], 1))
    if ring > 3:
        up_full = run(lambda w, b: put(w, b, links.behind(ring - 1), 0), up_full, up_block)
    down_full = jnp.zeros((hidden_part, width), LOW)
    down_full = run(lambda w, b: put(w, b, links.behind(0), 1), down_full, down_block)
    down_block, d_out_far[1] = wait(down_next, d_out_far[1])
    if ring > 2:
        down_next = step(down_block)
    d_out_last.append(swap(d_out_far[1], 1))
    down_full = run(lambda w, b: put(w, b, links.behind(1), 1), down_full, down_block)
    far_two[0], core_two[0], core_two[1], d_out_last[0] = wait(
        far_two[0], core_two[0], core_two[1], d_out_last[0]
    )
    last_two = [swap(far_two[0], 1)]
    for k in range(2, ring - 1):
        down_block = wait(down_next)
        down_next = step(down_block)
        down_full = run(lambda w, b: put(w, b, links.behind(k), 1), down_full, down_block)
    far_two[1], d_out_last[1] = wait(far_two[1], d_out_last[1])
    last_two.append(swap(far_two[1], 1))
    grad_plane = run(
        lambda *p: jnp.concatenate(p, axis=0), d_out, d_out_core, *d_out_far, *d_out_last
    )
    last_two = wait(*last_two)
    normed_two = run(
        lambda *p: jnp.concatenate(p, axis=0),
        seconds[0][3],
        seconds[1][3],
        *core_two,
        *far_two,
        *last_two,
    )

    def feed_up(normed, weights):
        activated, slope = gelu_parts(plain(normed, weights))
        return activated.astype(LOW), slope.astype(LOW)

    act_low, slope = run(feed_up, normed_two, up_full)

    def part_down(act, grad, k, *arrived):
        part = inner(act, take(grad, links.behind(k), block, 1))
        for total in arrived:
            part = part + wide(total)
        return part.astype(LOW) if k < ring else part

    def part_up(normed, grad, k, *arrived):
        part = inner(take(normed, links.behind(k), block, 1), grad)
        for total in arrived:
            part = part + wide(total)
        return part.astype(LOW) if k < ring else part

    def ring_down(k, *arrived):
        total = run(lambda a, g, *t: part_down(a, g, k, *t), act_low, grad_plane, *arrived)
        return step(total) if k < ring else total

    def ring_up(k, *arrived):
        total = run(lambda n, g, *t: part_up(n, g, k, *t), normed_two, grad_pre, *arrived)
        return step(total) if k < ring else total

    down_sum = ring_down(1)
    if ring > 2:
        down_block = wait(down_next)
        down_full = run(lambda w, b: put(w, b, links.behind(ring - 1), 1), down_full, down_block)
    grad_pre = run(
        lambda g, w, s: (outer(g, w) * wide(s)).astype(LOW), grad_plane, down_full, slope
    )

    def group(product, at, left, weights):
        return chunks(product(left[at * rows : (at + 1) * rows], weights))

    def low_group(product, at, left, weights):
        return tuple(part.astype(LOW) for part in group(product, at, left, weights))

    def pairwise(one, two):
        return [run(lambda a, b: a + wide(b), a, b) for a, b in zip(one, two)]

    def lowered(values):
        return [value.astype(LOW) for value in values]

    last_n = run(lambda a, w: low_group(outer, 3, a, w), grad_pre, up_full)
    last_n = [swap(part, 1) for part in last_n]
    far_own = run(lambda a, w: group(outer, 2, a, w), grad_pre, up_full)
    far_n = []
    for j in range(2):
        far = run(lambda a, b: (a + wide(b)).astype(LOW), far_own[j], wait(last_n[j]))
        far_n.append(swap(far, 2))
    up_sum = ring_up(1)
    core_n = run(lambda a, w: low_group(outer, 1, a, w), grad_pre, up_full)
    core_n = [swap(part, 1) for part in core_n]
    own_n = run(lambda a, w: group(outer, 0, a, w), grad_pre, up_full)
    down_arrived, core_n[0], core_n[1], far_n[0] = wait(down_sum, core_n[0], core_n[1], far_n[0])
    low_n, cross_n = [], []

    def near_sum(own, core, far):
        return (own + wide(core) + wide(far)).astype(LOW)

    low_n.append(run(near_sum, own_n[0], core_n[0], far_n[0]))
    cross_n.append(across(low_n[0]))
    down_sum = ring_down(2, down_arrived)
    last_r = run(lambda a, w: low_group(plain, 3, a, w), act_low, down_full)
    far_n[1] = wait(far_n[1])
    low_n.append(run(near_sum, own_n[1], core_n[1], far_n[1]))
    cross_n.append(across(low_n[1]))
    last_r = [swap(part, 1) for part in last_r]
    core_r = run(lambda a, w: low_group(plain, 1, a, w), act_low, down_full)
    up_arrived, last_r[0], last_r[1] = wait(up_sum, *last_r)
    up_sum = ring_up(2, up_arrived)
    core_r = [swap(part, 1) for part in core_r]
    far_r = run(lambda a, w: group(plain, 2, a, w), act_low, down_full)
    far_r = run(
        lambda a, b, c, d: ((a + wide(c)).astype(LOW), (b + wide(d)).astype(LOW)), *far_r, *last_r
    )
    far_r = [swap(part, 2) for part in far_r]
    own_r = run(lambda a, w: group(plain, 0, a, w), act_low, down_full)

    def second_back(d_out, low, cross, standard, inverse):
        scaled = wide(low) + wide(cross)
        grad_hidden = wide(d_out) + norm_backward(scaled, standard, inverse)
        return grad_hidden, grad_hidden.astype(LOW)

    grad_hidden, low_own, low_other = [], [], []
    if ring > 2:
        down_arrived, cross_n[0], core_r[0], core_r[1] = wait(down_sum, cross_n[0], *core_r)
        down_sum = ring_down(3, down_arrived)
    else:
        cross_n[0], core_r[0], core_r[1] = wait(cross_n[0], *core_r)
    for j in range(2):
        if j:
            cross_n[1] = wait(cross_n[1])
        grad, low = run(
            second_back, d_out_chunks[j], low_n[j], cross_n[j], seconds[j][1], seconds[j][2]
        )
        grad_hidden.append(grad)
        low_own.append(low)
        low_other.append(swap(low, 1))
    if ring > 2:
        up_arrived, far_r[0], far_r[1] = wait(up_sum, *far_r)
        up_sum = ring_up(3, up_arrived)
    else:
        far_r = wait(*far_r)
    low_r, cross_r = [], []
    for j in range(2):
        low_r.append(run(near_sum, own_r[j], core_r[j], far_r[j]))
        cross_r.append(across(low_r[j]))
    low_other = wait(*low_other)
    grad_low = run(lambda *p: jnp.concatenate(p, axis=0), *low_own, *low_other)

    def part_qkv(normed, grad, k):
        part = inner(take(normed, links.behind(k), block, 1), grad)
        return take(part, links.row, pair, 0), take(part, 1 - links.row, pair, 0).astype(LOW)

    def part_out(attended, grad, k):
        part = inner(attended, take(grad, links.behind(k), block, 1))
        return take(part, links.row, pair, 1), take(part, 1 - links.row, pair, 1).astype(LOW)

    out_owns, out_fars = [], []
    for k in range(1, ring + 1):
        own, far = run(lambda a, g: part_out(a, g, k), attended, grad_low)
        out_owns.append(own)
        out_fars.append(swap(far, 2))

    def attention_back(grad_low, out_full, probs, query, key, value):
        grad_att = heads_of(outer(grad_low, out_full).astype(LOW))
        grad_probs = jnp.einsum("gqhe,gkhe->ghqk", grad_att, value, preferred_element_type=WIDE)
        delta = jnp.sum(grad_probs * probs, axis=3, keepdims=True)
        grad_scores = (probs * (grad_probs - delta)).astype(LOW)
        to_query = jnp.einsum("ghqk,gkhe->gqhe", grad_scores, key, preferred_element_type=WIDE)
        to_key = jnp.einsum("ghqk,gqhe->gkhe", grad_scores, query, preferred_element_type=WIDE)
        to_value = jnp.einsum(
            "ghqk,gqhe->gkhe", probs.astype(LOW), grad_att, preferred_element_type=WIDE
        )
        return jnp.concatenate(
            [
                values.astype(LOW).reshape(2 * rows, half)
                for values in (to_query * factor, to_key * factor, to_value)
            ],
            axis=1,
        )

    grad_qkv = run(attention_back, grad_low, out_full, probs, query, key, value)
    qkv_owns, qkv_fars = [], []
    for k in range(1, ring + 1):
        own, far = run(lambda n, g: part_qkv(n, g, k), normed_one, grad_qkv)
        qkv_owns.append(own)
        qkv_fars.append(swap(far, 2) if k < 3 else far)
    out_fars = list(wait(*out_fars))
    out_sum = run(lambda a, b: (a + wide(b)).astype(LOW), out_owns[0], out_fars[0])
    out_next = step(out_sum)

    def first_partial(grad, weights, at):
        return chunks(outer(grad[at * rows : (at + 1) * rows], weights))

    core_m = run(lambda g, w: tuple(lowered(first_partial(g, w, 1))), grad_qkv, qkv_full)
    core_m = [swap(part, 1) for part in core_m]
    own_m = run(lambda g, w: first_partial(g, w, 0), grad_qkv, qkv_full)
    down_arrived = wait(down_sum) if ring > 2 else down_sum
    for k in range(4, ring + 1) if ring > 2 else (2,):
        down_sum = ring_down(k, down_arrived)
        if k < ring:
            down_arrived = wait(down_sum)
    up_arrived = wait(up_sum) if ring > 2 else up_sum
    for k in range(4, ring + 1) if ring > 2 else (2,):
        up_sum = ring_up(k, up_arrived)
        if k < ring:
            up_arrived = wait(up_sum)
    core_m = wait(*core_m)
    low_m, cross_m = [], []
    for j in range(2):
        low_m.append(run(lambda a, b: (a + wide(b)).astype(LOW), own_m[j], core_m[j]))
        cross_m.append(across(low_m[j]))

    def cut(total, axis, size):
        parts = [take(total, links.cell, size, axis)]
        parts += [take(total, links.cell ^ k, size, axis).astype(LOW) for k in (1, 2, 3)]
        return tuple(parts)

    up_ends = list(run(lambda t: cut(t, 0, owned), up_sum))
    down_ends = list(run(lambda t: cut(t, 1, owned), down_sum))

    def add_row(own, far, *arrived):
        total = own + wide(far)
        for part in arrived:
            total = total + wide(part)
        return total

    def add_low(*parts):
        return add_row(*parts).astype(LOW)

    for k in range(1, ring + 1):
        if k == 1:
            qkv_far = wait(qkv_fars[0])
            qkv_sum = run(add_low, qkv_owns[0], qkv_far)
        else:
            qkv_far, qkv_arrived, out_arrived = wait(qkv_fars[k - 1], qkv_next, out_next)
            add = add_low if k < ring else add_row
            qkv_sum, out_sum = run(
                lambda *p: (add(*p[:3]), add(*p[3:])),
                qkv_owns[k - 1],
                qkv_far,
                qkv_arrived,
                out_owns[k - 1],
                out_fars[k - 1],
                out_arrived,
            )
        if k < ring:
            qkv_next = step(qkv_sum)
            if k > 1:
                out_next = step(out_sum)
        if k + 1 < ring:
            qkv_fars[k + 1] = swap(qkv_fars[k + 1], 2)
        if k == 1:
            for j in (1, 2, 3):
                up_ends[j] = swap(up_ends[j], j)
                down_ends[j] = swap(down_ends[j], j)
        if k == 2:
            cross_m = wait(*cross_m)

            def first_back(tokens, grads, lows, crosses):
                standard, inverse = norm_forward(wide(tokens))
                scaled = wide(jnp.concatenate(lows)) + wide(jnp.concatenate(crosses))
                return jnp.concatenate(grads) + norm_backward(scaled, standard, inverse)

            d_tokens = run(
                lambda t, *p: first_back(t, p[:2], p[2:4], p[4:]),
                tokens,
                *grad_hidden,
                *low_m,
                *cross_m,
            )
        if k == min(3, ring):
            up_ends, down_ends = list(wait(*up_ends)), list(wait(*down_ends))

            def up_end(gain, weight, *parts):
                raw = links.join([wide(part) for part in parts], 1)
                return raw * gain[:, None], jnp.sum(wide(weight) * raw, axis=1)

            d_w_up, gain_mlp_own = run(up_end, gain_mlp, w_up, *up_ends)
            gain_mlp_other = across(gain_mlp_own)
            d_w_down = run(lambda *p: links.join([wide(part) for part in p], 0), *down_ends)
            cross_r = wait(*cross_r)
            result = run(
                lambda *p: jnp.concatenate(p[:2])
                + (wide(jnp.concatenate(p[2:4])) + wide(jnp.concatenate(p[4:]))),
                seconds[0][0],
                seconds[1][0],
                *low_r,
                *cross_r,
            )

    def ends(qkv, out):
        return (
            take(qkv, links.core, owned, 0),
            take(qkv, 1 - links.core, owned, 0).astype(LOW),
            take(out, links.core, owned, 1),
            take(out, 1 - links.core, owned, 1).astype(LOW),
        )

    qkv_mine, qkv_yours, out_mine, out_yours = run(ends, qkv_sum, out_sum)
    qkv_yours, out_yours = swap(qkv_yours, 1), swap(out_yours, 1)
    qkv_yours, out_yours = wait(qkv_yours, out_yours)
    d_w_output = links.by_core(out_mine, wide(out_yours), 0)
    raw = [
        links.by_core(qkv_mine[:, at : at + half], wide(qkv_yours[:, at : at + half]), 1)
        for at in (0, half, 2 * half)
    ]
    gain_attn_own = sum(
        jnp.sum(wide(weight) * part, axis=1) for weight, part in zip((w_query, w_key, w_value), raw)
    )
    d_gain_attn = gain_attn_own + across(gain_attn_own)
    d_gain_mlp = gain_mlp_own + gain_mlp_other
    d_w_query, d_w_key, d_w_value = (part * gain_attn[:, None] for part in raw)
    return (
        result,
        d_tokens,
        d_gain_attn,
        d_w_query,
        d_w_key,
        d_w_value,
        d_w_output,
        d_gain_mlp,
        d_w_up,
        d_w_down,
    )


def solution(mesh):
    return jax.shard_map(
        functools.partial(shards, mesh.shape["dp"]),
        mesh=mesh,
        in_specs=(
            P("dp", None),
            P("dp", None),
            P("dp", None),
            P("dp"),
            P("dp", "mp"),
            P("dp", "mp"),
            P("dp", "mp"),
            P("mp", "dp"),
            P("dp"),
            P("dp", "mp"),
            P("mp", "dp"),
            P("dp", None),
        ),
        out_specs=(
            P("dp", None),
            P("dp", None),
            P("dp"),
            P("dp", "mp"),
            P("dp", "mp"),
            P("dp", "mp"),
            P("mp", "dp"),
            P("dp"),
            P("dp", "mp"),
            P("mp", "dp"),
        ),
        check_vma=False,
    )
```

time: 757 us -> 634 us (0.84)
  waiting for transfers between devices: 466 us -> 297 us
  local copies, waits for them, and re-layouts: 62.8 us -> 109 us
  starting transfers between devices: 43 us -> 70.7 us
  matrix products: 120 us -> 102 us
  other arithmetic: 56.6 us -> 44.8 us
    ppermute x78 -> x98, waiting for transfers between devices: 466 us -> 297 us  [the longest x64 163 us: swap(): return lax.ppermute(self.order.tie(values), 'dp', self.to[k])]
    ppermute x78 -> x98, starting transfers between devices: 43 us -> 70.7 us  [the longest x64 38.4 us: swap(): return lax.ppermute(self.order.tie(values), 'dp', self.to[k])]
    dynamic_update_slice x30 -> x34, local copies, waits for them, and re-layouts: 25.6 us -> 38.8 us  [put(): lax.dynamic_update_slice_in_dim(whole, part, index * part.shape[axis], axis)]
    unnamed x127 -> x200, local copies, waits for them, and re-layouts: 13.2 us -> 25.2 us
    convert_element_type x21 -> x29, other arithmetic: 30.4 us -> 22.2 us  [the longest x5 4.91 us: add_low(): return add_row(*parts).astype(LOW)]
    dynamic_slice x6 -> x16, local copies, waits for them, and re-layouts: 2.69 us -> 10.7 us  [take(): return lax.dynamic_slice_in_dim(values, index * size, size, axis)]
    dot_general x4 -> x8, matrix products: 31.2 us -> 23.8 us  [outer(): lax.dot_general(one, two, (((1,), (1,)), ((), ())), preferred_element_typ...]
    dot_general x5 -> x6, matrix products: 15.2 us -> 14.6 us  [the longest x1 4.22 us: attention_back(): jnp.einsum('ghqk,gqhe->gkhe', probs.astype(LOW), grad_att, preferred_elem...]
  transfers between devices with their start and end apart: 78 -> 98, of which waited for: 38 -> 40; matrix products, arithmetic and copies ran while one was open for 23% -> 38% of each run, Pallas kernels for 0% -> 0%
where the time goes in v2:
time: 634 us; the launch traced here: 627 us
  waiting for transfers between devices  297 us (47%)
  local copies, waits for them, and re-layouts  109 us (17%)
  matrix products  102 us (16%)
  starting transfers between devices  70.7 us (11%)
  other arithmetic  44.8 us (7%)
    ppermute x64, waiting for transfers between devices, swap(): return lax.ppermute(self.order.tie(values), 'dp', self.to[k])  163 us
    ppermute x24, waiting for transfers between devices, step(): return lax.ppermute(self.order.tie(values), 'dp', self.next)  70 us
    ppermute x10, waiting for transfers between devices, across(): return lax.ppermute(self.order.tie(values), 'mp', [(0, 1), (1, 0)])  63.8 us
    dynamic_update_slice x34, local copies, waits for them, and re-layouts, put(): lax.dynamic_update_slice_in_dim(whole, part, index * part.shape[axis], axis)  38.8 us
    ppermute x64, starting transfers between devices, swap(): return lax.ppermute(self.order.tie(values), 'dp', self.to[k])  38.4 us
    dot_general x8, matrix products, plain(): return jnp.dot(one, two, preferred_element_type=WIDE)  33.5 us
    dot_general x16, matrix products, inner(): lax.dot_general(one, two, (((0,), (0,)), ((), ())), preferred_element_typ...  29.9 us
    unnamed x200, local copies, waits for them, and re-layouts  25.2 us
  transfers between devices with their start and end apart: 98, of which 40 were waited for; matrix products, arithmetic and copies ran while one was open for 38% of the time, Pallas kernels for 0%

profile of v2, /device:TPU:0, one launch (start us, length us, event | category | flops | bytes accessed | tf_op | source)
XLA Modules:
  0.0 626.6 jit_solution(5906447534929703832)
XLA Ops:
  4.4 3.0 collective-permute-start.5
  18.0 14.8 %collective-permute-done.6 = bf16[512,256]{1,0:T(8,128)(2,1)S(1)} collective-permute-done((bf16[512,256]{1,0:T(8,128)(2,1)S(1)}, bf16[512,256]{1,0:T(8,128)(2,1)S(1)}, u32[]{:S(2)}, u32[]{:S(2)}) %collective-permute-start.6) | collective-permute-done | bytes 262176 | tf_op jit(solution)/shard_map/ppermute | solution.py:96
  43.5 15.2 %collective-permute-done.11 = bf16[128,1024]{1,0:T(8,128)(2,1)S(1)} collective-permute-done((bf16[128,1024]{1,0:T(8,128)(2,1)}, bf16[128,1024]{1,0:T(8,128)(2,1)S(1)}, u32[]{:S(2)}, u32[]{:S(2)}) %collective-permute-start.11) | collective-permute-done | bytes 262176 | tf_op jit(solution)/shard_map/ppermute | solution.py:93
  70.4 13.3 %collective-permute-done.16 = bf16[128,1024]{1,0:T(8,128)(2,1)S(1)} collective-permute-done((bf16[128,1024]{1,0:T(8,128)(2,1)S(1)}, bf16[128,1024]{1,0:T(8,128)(2,1)S(1)}, u32[]{:S(2)}, u32[]{:S(2)}) %collective-permute-start.16) | collective-permute-done | bytes 262176 | tf_op jit(solution)/shard_map/ppermute | solution.py:93
  95.9 17.2 %collective-permute-done.19 = bf16[512,256]{1,0:T(8,128)(2,1)S(1)} collective-permute-done((bf16[512,256]{1,0:T(8,128)(2,1)S(1)}, bf16[512,256]{1,0:T(8,128)(2,1)S(1)}, u32[]{:S(2)}, u32[]{:S(2)}) %collective-permute-start.19) | collective-permute-done | bytes 262176 | tf_op jit(solution)/shard_map/ppermute | solution.py:93
  117.9 5.3 convolution_convert_fusion
  124.5 2.5 reshape.158
  160.4 17.1 %collective-permute-done.30 = bf16[1024,128]{1,0:T(8,128)(2,1)S(1)} collective-permute-done((bf16[1024,128]{1,0:T(8,128)(2,1)S(1)}, bf16[1024,128]{1,0:T(8,128)(2,1)S(1)}, u32[]{:S(2)}, u32[]{:S(2)}) %collective-permute-start.30) | collective-permute-done | bytes 262176 | tf_op jit(solution)/shard_map/ppermute | solution.py:93
  185.5 17.0 %collective-permute-done.33 = bf16[192,2048]{1,0:T(8,128)(2,1)S(1)} collective-permute-done((bf16[192,2048]{1,0:T(8,128)(2,1)S(1)}, bf16[192,2048]{1,0:T(8,128)(2,1)S(1)}, u32[]{:S(2)}, u32[]{:S(2)}) %collective-permute-start.33) | collective-permute-done | bytes 786464 | tf_op jit(solution)/shard_map/ppermute | solution.py:99
  208.9 2.6 broadcast_in_dim.35
  213.8 9.0 %collective-permute-done.39 = bf16[192,2048]{1,0:T(8,128)(2,1)} collective-permute-done((bf16[192,2048]{1,0:T(8,128)(2,1)}, bf16[192,2048]{1,0:T(8,128)(2,1)}, u32[]{:S(2)}, u32[]{:S(2)}) %collective-permute-start.39) | collective-permute-done | bytes 786464 | tf_op jit(solution)/shard_map/ppermute | solution.py:93
  225.0 2.4 constant_dynamic-update-slice_fusion.18
  227.4 15.9 %collective-permute-done.34 = bf16[192,2048]{1,0:T(8,128)(2,1)} collective-permute-done((bf16[192,2048]{1,0:T(8,128)(2,1)S(1)}, bf16[192,2048]{1,0:T(8,128)(2,1)}, u32[]{:S(2)}, u32[]{:S(2)}) %collective-permute-start.34) | collective-permute-done | bytes 786464 | tf_op jit(solution)/shard_map/ppermute | solution.py:93
  243.3 5.6 collective-permute-done.42
  251.3 6.9 %collective-permute-done.40 = bf16[192,2048]{1,0:T(8,128)(2,1)} collective-permute-done((bf16[192,2048]{1,0:T(8,128)(2,1)}, bf16[192,2048]{1,0:T(8,128)(2,1)}, u32[]{:S(2)}, u32[]{:S(2)}) %collective-permute-start.40) | collective-permute-done | bytes 786464 | tf_op jit(solution)/shard_map/ppermute | solution.py:93
  263.4 3.9 collective-permute-start.45
  273.8 9.9 %fusion.5 = (bf16[1536,1024]{1,0:T(8,128)(2,1)}, bf16[1536,1024]{1,0:T(8,128)(2,1)S(1)}) fusion(bf16[1536,2048]{1,0:T(8,128)(2,1)S(1)} %constant_dynamic-update-slice_fusion.6, bf16[2048,1024]{1,0:T(8,128)(2,1)S(1)} %copy-done.28), kind=kOutput, calls=%fused_computation.6 | convolution fusion | flops 6459752448 | bytes 16777216 | tf_op jit(solution)/shard_map/dot_general | solution.py:17
  286.7 4.7 collective-permute-done.45
  292.5 9.4 %multiply_convert_fusion = bf16[1536,1024]{1,0:T(8,128)(2,1)S(1)} fusion(bf16[1536,1024]{1,0:T(8,128)(2,1)} %get-tuple-element.1030, bf16[1536,2048]{1,0:T(8,128)(2,1)S(1)} %constant_dynamic-update-slice_fusion, bf16[1024,2048]{1,0:T(8,128)(2,1)} %constant_dynamic-update-slice_fusion.16), kind=kOutput, calls=%fused_computation.7 | convolution fusion | flops 6447169536 | bytes 16777216 | tf_op jit(solution)/shard_map/dot_general | solution.py:25
  318.5 14.0 %collective-permute-done.52 = bf16[192,2048]{1,0:T(8,128)(2,1)S(1)} collective-permute-done((bf16[192,2048]{1,0:T(8,128)(2,1)S(1)}, bf16[192,2048]{1,0:T(8,128)(2,1)S(1)}, u32[]{:S(2)}, u32[]{:S(2)}) %collective-permute-start.52) | collective-permute-done | bytes 786464 | tf_op jit(solution)/shard_map/ppermute | solution.py:93
  334.7 4.0 convolution_convert_fusion.2
  338.8 9.7 %collective-permute-done.53 = bf16[192,2048]{1,0:T(8,128)(2,1)S(1)} collective-permute-done((bf16[192,2048]{1,0:T(8,128)(2,1)S(1)}, bf16[192,2048]{1,0:T(8,128)(2,1)S(1)}, u32[]{:S(2)}, u32[]{:S(2)}) %collective-permute-start.53) | collective-permute-done | bytes 786464 | tf_op jit(solution)/shard_map/ppermute | solution.py:93
  349.4 4.0 convolution_convert_fusion.1
  360.1 4.2 fusion.107
  365.0 4.2 fusion.105
  369.6 6.5 %collective-permute-done.57 = bf16[192,2048]{1,0:T(8,128)(2,1)S(1)} collective-permute-done((bf16[192,2048]{1,0:T(8,128)(2,1)S(1)}, bf16[192,2048]{1,0:T(8,128)(2,1)S(1)}, u32[]{:S(2)}, u32[]{:S(2)}) %collective-permute-start.57) | collective-permute-done | bytes 786464 | tf_op jit(solution)/shard_map/ppermute | solution.py:99
  377.1 3.4 collective-permute-done.56
  381.8 4.7 add_convert_fusion.1
  392.2 2.8 fusion.141
  397.2 12.9 %collective-permute-done.61 = bf16[192,2048]{1,0:T(8,128)(2,1)S(1)} collective-permute-done((bf16[192,2048]{1,0:T(8,128)(2,1)S(1)}, bf16[192,2048]{1,0:T(8,128)(2,1)S(1)}, u32[]{:S(2)}, u32[]{:S(2)}) %collective-permute-start.61) | collective-permute-done | bytes 786464 | tf_op jit(solution)/shard_map/ppermute | solution.py:93
  410.1 2.9 add_convert_fusion
  427.3 4.2 fusion.70
  431.6 3.2 multiply_reduce_fusion
  467.2 5.2 collective-permute-done.71
  473.5 4.6 collective-permute-done.70
  479.1 4.6 collective-permute-done.69
  484.5 2.6 convolution_convert_fusion.5
  487.3 2.6 fusion.78
  491.8 3.5 convert_add_fusion.2
  495.4 3.2 convert_add_fusion.1
  502.7 10.5 %collective-permute-done.76 = bf16[256,1536]{1,0:T(8,128)(2,1)S(1)} collective-permute-done((bf16[256,1536]{1,0:T(8,128)(2,1)S(1)}, bf16[256,1536]{1,0:T(8,128)(2,1)S(1)}, u32[]{:S(2)}, u32[]{:S(2)}) %collective-permute-start.76) | collective-permute-done | bytes 786464 | tf_op jit(solution)/shard_map/ppermute | solution.py:93
  517.1 20.2 %collective-permute-done.86 = bf16[512,256]{1,0:T(8,128)(2,1)} collective-permute-done((bf16[512,256]{1,0:T(8,128)(2,1)}, bf16[512,256]{1,0:T(8,128)(2,1)}, u32[]{:S(2)}, u32[]{:S(2)}) %collective-permute-start.86) | collective-permute-done | bytes 262176 | tf_op jit(solution)/shard_map/ppermute | solution.py:96
  542.8 3.9 collective-permute-done.89
  553.0 4.4 fusion.16
  559.8 12.7 %collective-permute-done.87 = bf16[256,1536]{1,0:T(8,128)(2,1)S(1)} collective-permute-done((bf16[256,1536]{1,0:T(8,128)(2,1)S(1)}, bf16[256,1536]{1,0:T(8,128)(2,1)S(1)}, u32[]{:S(2)}, u32[]{:S(2)}) %collective-permute-start.87) | collective-permute-done | bytes 786464 | tf_op jit(solution)/shard_map/ppermute | solution.py:96
  581.6 12.8 %collective-permute-done.65 = bf16[192,2048]{1,0:T(8,128)(2,1)S(1)} collective-permute-done((bf16[192,2048]{1,0:T(8,128)(2,1)S(1)}, bf16[192,2048]{1,0:T(8,128)(2,1)S(1)}, u32[]{:S(2)}, u32[]{:S(2)}) %collective-permute-start.65) | collective-permute-done | bytes 786464 | tf_op jit(solution)/shard_map/ppermute | solution.py:99
  594.4 16.5 %collective-permute-done.64 = bf16[192,2048]{1,0:T(8,128)(2,1)S(1)} collective-permute-done((bf16[192,2048]{1,0:T(8,128)(2,1)S(1)}, bf16[192,2048]{1,0:T(8,128)(2,1)S(1)}, u32[]{:S(2)}, u32[]{:S(2)}) %collective-permute-start.64) | collective-permute-done | bytes 786464 | tf_op jit(solution)/shard_map/ppermute | solution.py:99
  614.8 2.8 collective-permute-done.97
  (569 shorter events, 256.6 us)
Async XLA Ops:
  4.4 28.5 %collective-permute-start.5 = (bf16[256,1536]{1,0:T(8,128)(2,1)S(1)}, bf16[256,1536]{1,0:T(8,128)(2,1)}, u32[]{:S(2)}, u32[]{:S(2)}) collective-permute-start(bf16[256,1536]{1,0:T(8,128)(2,1)S(1)} %maximum_select_fusion), channel_id=1, source_target_pairs={{0,8},{2,10},{4,12},{6,14},{8,16},{10,18},{12,20},{14,22},{16,24},... | collective-permute-start | bytes 2359304 | tf_op jit(solution)/shard_map/ppermute | solution.py:96
  7.4 25.5 %collective-permute-start.7 = (bf16[256,1536]{1,0:T(8,128)(2,1)S(1)}, bf16[256,1536]{1,0:T(8,128)(2,1)S(1)}, u32[]{:S(2)}, u32[]{:S(2)}) collective-permute-start(bf16[256,1536]{1,0:T(8,128)(2,1)S(1)} %maximum_select_fusion), channel_id=1, source_target_pairs={{0,4},{2,6},{4,0},{6,2},{8,12},{10,14},{12,8},{14,10},{16,20},{18,... | collective-permute-start | bytes 2359304 | tf_op jit(solution)/shard_map/ppermute | solution.py:93
  33.8 27.8 %collective-permute-start.10 = (bf16[256,1536]{1,0:T(8,128)(2,1)}, bf16[256,1536]{1,0:T(8,128)(2,1)}, u32[]{:S(2)}, u32[]{:S(2)}) collective-permute-start(bf16[256,1536]{1,0:T(8,128)(2,1)} %collective-permute-done.5), channel_id=1, source_target_pairs={{0,4},{2,6},{4,0},{6,2},{8,12},{10,14},{12,8},{14,10},{16,20},{18,... | collective-permute-start | bytes 2359304 | tf_op jit(solution)/shard_map/ppermute | solution.py:93
  35.3 26.3 %collective-permute-start.8 = (bf16[256,1536]{1,0:T(8,128)(2,1)}, bf16[256,1536]{1,0:T(8,128)(2,1)}, u32[]{:S(2)}, u32[]{:S(2)}) collective-permute-start(bf16[256,1536]{1,0:T(8,128)(2,1)} %collective-permute-done.5), channel_id=1, source_target_pairs={{0,8},{2,10},{4,12},{6,14},{8,16},{10,18},{12,20},{14,22},{16,24},... | collective-permute-start | bytes 2359304 | tf_op jit(solution)/shard_map/ppermute | solution.py:96
  36.5 22.1 %collective-permute-start.11 = (bf16[128,1024]{1,0:T(8,128)(2,1)}, bf16[128,1024]{1,0:T(8,128)(2,1)S(1)}, u32[]{:S(2)}, u32[]{:S(2)}) collective-permute-start(bf16[128,1024]{1,0:T(8,128)(2,1)} %get-tuple-element.792), channel_id=1, source_target_pairs={{0,4},{2,6},{4,0},{6,2},{8,12},{10,14},{12,8},{14,10},{16,20},{18,... | collective-permute-start | bytes 786440 | tf_op jit(solution)/shard_map/ppermute | solution.py:93
  37.1 24.5 %collective-permute-start.9 = (bf16[512,256]{1,0:T(8,128)(2,1)}, bf16[512,256]{1,0:T(8,128)(2,1)}, u32[]{:S(2)}, u32[]{:S(2)}) collective-permute-start(bf16[512,256]{1,0:T(8,128)(2,1)} %copy-done.63), channel_id=1, source_target_pairs={{0,8},{2,10},{4,12},{6,14},{8,16},{10,18},{12,20},{14,22},{16,24},... | collective-permute-start | bytes 786440 | tf_op jit(solution)/shard_map/ppermute | solution.py:96
  61.6 25.4 %collective-permute-start.13 = (bf16[256,1536]{1,0:T(8,128)(2,1)}, bf16[256,1536]{1,0:T(8,128)(2,1)}, u32[]{:S(2)}, u32[]{:S(2)}) collective-permute-start(bf16[256,1536]{1,0:T(8,128)(2,1)} %collective-permute-done.8), channel_id=1, source_target_pairs={{0,8},{2,10},{4,12},{6,14},{8,16},{10,18},{12,20},{14,22},{16,24},... | collective-permute-start | bytes 2359304 | tf_op jit(solution)/shard_map/ppermute | solution.py:96
  61.7 25.4 %collective-permute-start.15 = (bf16[256,1536]{1,0:T(8,128)(2,1)}, bf16[256,1536]{1,0:T(8,128)(2,1)}, u32[]{:S(2)}, u32[]{:S(2)}) collective-permute-start(bf16[256,1536]{1,0:T(8,128)(2,1)} %collective-permute-done.8), channel_id=1, source_target_pairs={{0,4},{2,6},{4,0},{6,2},{8,12},{10,14},{12,8},{14,10},{16,20},{18,... | collective-permute-start | bytes 2359304 | tf_op jit(solution)/shard_map/ppermute | solution.py:93
  63.8 29.9 %collective-permute-start.2 = (bf16[384,2048]{1,0:T(8,128)(2,1)}, bf16[384,2048]{1,0:T(8,128)(2,1)S(1)}, u32[]{:S(2)}, u32[]{:S(2)}) collective-permute-start(bf16[384,2048]{1,0:T(8,128)(2,1)} %fusion.19), channel_id=1, source_target_pairs={{0,2},{2,0},{4,6},{6,4},{8,10},{10,8},{12,14},{14,12},{16,18},{18,... | collective-permute-start | bytes 4718600 | tf_op jit(solution)/shard_map/ppermute | solution.py:93
  87.3 25.8 %collective-permute-start.18 = (bf16[256,1536]{1,0:T(8,128)(2,1)}, bf16[256,1536]{1,0:T(8,128)(2,1)S(1)}, u32[]{:S(2)}, u32[]{:S(2)}) collective-permute-start(bf16[256,1536]{1,0:T(8,128)(2,1)} %collective-permute-done.13), channel_id=1, source_target_pairs={{0,4},{2,6},{4,0},{6,2},{8,12},{10,14},{12,8},{14,10},{16,20},{18,... | collective-permute-start | bytes 2359304 | tf_op jit(solution)/shard_map/ppermute | solution.py:93
  88.4 27.2 %collective-permute-start.17 = (bf16[512,1024]{1,0:T(8,128)(2,1)S(1)}, bf16[512,1024]{1,0:T(8,128)(2,1)}, u32[]{:S(2)}, u32[]{:S(2)}) collective-permute-start(bf16[512,1024]{1,0:T(8,128)(2,1)S(1)} %constant_dynamic-update-slice_fusion.36), channel_id=1, source_target_pairs={{0,8},{2,10},{4,12},{6,14},{8,16},{10,18},{12,20},{14,22},{16,24},... | collective-permute-start | bytes 3145736 | tf_op jit(solution)/shard_map/ppermute | solution.py:96
  115.6 29.2 %collective-permute-start.24 = (bf16[512,256]{1,0:T(8,128)(2,1)}, bf16[512,256]{1,0:T(8,128)(2,1)}, u32[]{:S(2)}, u32[]{:S(2)}) collective-permute-start(bf16[512,256]{1,0:T(8,128)(2,1)} %collective-permute-done.14), channel_id=1, source_target_pairs={{0,4},{2,6},{4,0},{6,2},{8,12},{10,14},{12,8},{14,10},{16,20},{18,... | collective-permute-start | bytes 786440 | tf_op jit(solution)/shard_map/ppermute | solution.py:93
  116.6 28.3 %collective-permute-start.23 = (bf16[512,256]{1,0:T(8,128)(2,1)}, bf16[512,256]{1,0:T(8,128)(2,1)}, u32[]{:S(2)}, u32[]{:S(2)}) collective-permute-start(bf16[512,256]{1,0:T(8,128)(2,1)} %collective-permute-done.9), channel_id=1, source_target_pairs={{0,4},{2,6},{4,0},{6,2},{8,12},{10,14},{12,8},{14,10},{16,20},{18,... | collective-permute-start | bytes 786440 | tf_op jit(solution)/shard_map/ppermute | solution.py:93
  117.6 27.3 %collective-permute-start.20 = (bf16[512,1024]{1,0:T(8,128)(2,1)}, bf16[512,1024]{1,0:T(8,128)(2,1)}, u32[]{:S(2)}, u32[]{:S(2)}) collective-permute-start(bf16[512,1024]{1,0:T(8,128)(2,1)} %collective-permute-done.17), channel_id=1, source_target_pairs={{0,8},{2,10},{4,12},{6,14},{8,16},{10,18},{12,20},{14,22},{16,24},... | collective-permute-start | bytes 3145736 | tf_op jit(solution)/shard_map/ppermute | solution.py:96
  144.8 38.8 %collective-permute-start.27 = (bf16[384,2048]{1,0:T(8,128)(2,1)}, bf16[384,2048]{1,0:T(8,128)(2,1)S(1)}, u32[]{:S(2)}, u32[]{:S(2)}) collective-permute-start(bf16[384,2048]{1,0:T(8,128)(2,1)} %param.23), channel_id=1, source_target_pairs={{0,2},{2,0},{4,6},{6,4},{8,10},{10,8},{12,14},{14,12},{16,18},{18,... | collective-permute-start | bytes 4718600 | tf_op jit(solution)/shard_map/ppermute | solution.py:93
  152.0 31.3 %collective-permute-start.29 = (bf16[512,1024]{1,0:T(8,128)(2,1)}, bf16[512,1024]{1,0:T(8,128)(2,1)S(1)}, u32[]{:S(2)}, u32[]{:S(2)}) collective-permute-start(bf16[512,1024]{1,0:T(8,128)(2,1)} %collective-permute-done.20), channel_id=1, source_target_pairs={{0,8},{2,10},{4,12},{6,14},{8,16},{10,18},{12,20},{14,22},{16,24},... | collective-permute-start | bytes 3145736 | tf_op jit(solution)/shard_map/ppermute | solution.py:96
  152.6 30.9 %collective-permute-start.28 = (bf16[192,2048]{1,0:T(8,128)(2,1)S(1)}, bf16[192,2048]{1,0:T(8,128)(2,1)}, u32[]{:S(2)}, u32[]{:S(2)}) collective-permute-start(bf16[192,2048]{1,0:T(8,128)(2,1)S(1)} %copy-done.33), channel_id=1, source_target_pairs={{0,4},{2,6},{4,0},{6,2},{8,12},{10,14},{12,8},{14,10},{16,20},{18,... | collective-permute-start | bytes 2359304 | tf_op jit(solution)/shard_map/ppermute | solution.py:93
  153.9 29.7 %collective-permute-start.26 = (bf16[192,2048]{1,0:T(8,128)(2,1)S(1)}, bf16[192,2048]{1,0:T(8,128)(2,1)S(1)}, u32[]{:S(2)}, u32[]{:S(2)}) collective-permute-start(bf16[192,2048]{1,0:T(8,128)(2,1)S(1)} %add_convert_fusion.18), channel_id=1, source_target_pairs={{0,1},{1,0},{2,3},{3,2},{4,5},{5,4},{6,7},{7,6},{8,9},{9,8},{10,11... | collective-permute-start | bytes 2359304 | tf_op jit(solution)/shard_map/ppermute | solution.py:99
  183.3 30.5 %collective-permute-start.38 = (bf16[1024,512]{1,0:T(8,128)(2,1)}, bf16[1024,512]{1,0:T(8,128)(2,1)}, u32[]{:S(2)}, u32[]{:S(2)}) collective-permute-start(bf16[1024,512]{1,0:T(8,128)(2,1)} %constant_dynamic-update-slice_fusion.21), channel_id=1, source_target_pairs={{0,8},{2,10},{4,12},{6,14},{8,16},{10,18},{12,20},{14,22},{16,24},... | collective-permute-start | bytes 3145736 | tf_op jit(solution)/shard_map/ppermute | solution.py:96
  222.7 26.2 %collective-permute-start.42 = (bf16[1024,512]{1,0:T(8,128)(2,1)}, bf16[1024,512]{1,0:T(8,128)(2,1)}, u32[]{:S(2)}, u32[]{:S(2)}) collective-permute-start(bf16[1024,512]{1,0:T(8,128)(2,1)} %collective-permute-done.38), channel_id=1, source_target_pairs={{0,8},{2,10},{4,12},{6,14},{8,16},{10,18},{12,20},{14,22},{16,24},... | collective-permute-start | bytes 3145736 | tf_op jit(solution)/shard_map/ppermute | solution.py:96
  223.8 34.5 %collective-permute-start.40 = (bf16[192,2048]{1,0:T(8,128)(2,1)}, bf16[192,2048]{1,0:T(8,128)(2,1)}, u32[]{:S(2)}, u32[]{:S(2)}) collective-permute-start(bf16[192,2048]{1,0:T(8,128)(2,1)} %get-tuple-element.1002), channel_id=1, source_target_pairs={{0,4},{2,6},{4,0},{6,2},{8,12},{10,14},{12,8},{14,10},{16,20},{18,... | collective-permute-start | bytes 2359304 | tf_op jit(solution)/shard_map/ppermute | solution.py:93
  224.8 33.4 %collective-permute-start.41 = (bf16[192,2048]{1,0:T(8,128)(2,1)}, bf16[192,2048]{1,0:T(8,128)(2,1)}, u32[]{:S(2)}, u32[]{:S(2)}) collective-permute-start(bf16[192,2048]{1,0:T(8,128)(2,1)} %collective-permute-done.39), channel_id=1, source_target_pairs={{0,2},{2,0},{4,6},{6,4},{8,10},{10,8},{12,14},{14,12},{16,18},{18,... | collective-permute-start | bytes 2359304 | tf_op jit(solution)/shard_map/ppermute | solution.py:93
  243.3 24.0 %collective-permute-start.43 = (bf16[192,2048]{1,0:T(8,128)(2,1)}, bf16[192,2048]{1,0:T(8,128)(2,1)S(1)}, u32[]{:S(2)}, u32[]{:S(2)}) collective-permute-start(bf16[192,2048]{1,0:T(8,128)(2,1)} %collective-permute-done.34), channel_id=1, source_target_pairs={{0,2},{2,0},{4,6},{6,4},{8,10},{10,8},{12,14},{14,12},{16,18},{18,... | collective-permute-start | bytes 2359304 | tf_op jit(solution)/shard_map/ppermute | solution.py:93
  263.4 28.0 %collective-permute-start.45 = (bf16[1024,512]{1,0:T(8,128)(2,1)}, bf16[1024,512]{1,0:T(8,128)(2,1)S(1)}, u32[]{:S(2)}, u32[]{:S(2)}) collective-permute-start(bf16[1024,512]{1,0:T(8,128)(2,1)} %collective-permute-done.42), channel_id=1, source_target_pairs={{0,8},{2,10},{4,12},{6,14},{8,16},{10,18},{12,20},{14,22},{16,24},... | collective-permute-start | bytes 3145736 | tf_op jit(solution)/shard_map/ppermute | solution.py:96
  285.6 30.7 %collective-permute-start.49 = (bf16[1024,512]{1,0:T(8,128)(2,1)S(1)}, bf16[1024,512]{1,0:T(8,128)(2,1)S(1)}, u32[]{:S(2)}, u32[]{:S(2)}) collective-permute-start(bf16[1024,512]{1,0:T(8,128)(2,1)S(1)} %fusion.48), channel_id=1, source_target_pairs={{0,8},{2,10},{4,12},{6,14},{8,16},{10,18},{12,20},{14,22},{16,24},... | collective-permute-start | bytes 3145736 | tf_op jit(solution)/shard_map/ppermute | solution.py:96
  315.2 33.3 %collective-permute-start.53 = (bf16[192,2048]{1,0:T(8,128)(2,1)S(1)}, bf16[192,2048]{1,0:T(8,128)(2,1)S(1)}, u32[]{:S(2)}, u32[]{:S(2)}) collective-permute-start(bf16[192,2048]{1,0:T(8,128)(2,1)S(1)} %add_convert_fusion.15), channel_id=1, source_target_pairs={{0,4},{2,6},{4,0},{6,2},{8,12},{10,14},{12,8},{14,10},{16,20},{18,... | collective-permute-start | bytes 2359304 | tf_op jit(solution)/shard_map/ppermute | solution.py:93
  316.3 40.2 %collective-permute-start.48 = (bf16[512,1024]{1,0:T(8,128)(2,1)S(1)}, bf16[512,1024]{1,0:T(8,128)(2,1)S(1)}, u32[]{:S(2)}, u32[]{:S(2)}) collective-permute-start(bf16[512,1024]{1,0:T(8,128)(2,1)S(1)} %fusion.51), channel_id=1, source_target_pairs={{0,8},{2,10},{4,12},{6,14},{8,16},{10,18},{12,20},{14,22},{16,24},... | collective-permute-start | bytes 3145736 | tf_op jit(solution)/shard_map/ppermute | solution.py:96
  353.5 27.0 %collective-permute-start.56 = (bf16[1024,512]{1,0:T(8,128)(2,1)S(1)}, bf16[1024,512]{1,0:T(8,128)(2,1)S(1)}, u32[]{:S(2)}, u32[]{:S(2)}) collective-permute-start(bf16[1024,512]{1,0:T(8,128)(2,1)S(1)} %add_convert_fusion.3), channel_id=1, source_target_pairs={{0,8},{2,10},{4,12},{6,14},{8,16},{10,18},{12,20},{14,22},{16,24},... | collective-permute-start | bytes 3145736 | tf_op jit(solution)/shard_map/ppermute | solution.py:96
  356.4 35.3 %collective-permute-start.63 = (bf16[192,2048]{1,0:T(8,128)(2,1)S(1)}, bf16[192,2048]{1,0:T(8,128)(2,1)S(1)}, u32[]{:S(2)}, u32[]{:S(2)}) collective-permute-start(bf16[192,2048]{1,0:T(8,128)(2,1)S(1)} %add_convert_fusion.13), channel_id=1, source_target_pairs={{0,1},{1,0},{2,3},{3,2},{4,5},{5,4},{6,7},{7,6},{8,9},{9,8},{10,11... | collective-permute-start | bytes 2359304 | tf_op jit(solution)/shard_map/ppermute | solution.py:99
  359.5 22.1 %collective-permute-start.59 = (bf16[192,2048]{1,0:T(8,128)(2,1)S(1)}, bf16[192,2048]{1,0:T(8,128)(2,1)S(1)}, u32[]{:S(2)}, u32[]{:S(2)}) collective-permute-start(bf16[192,2048]{1,0:T(8,128)(2,1)S(1)} %get-tuple-element.1129), channel_id=1, source_target_pairs={{0,2},{2,0},{4,6},{6,4},{8,10},{10,8},{12,14},{14,12},{16,18},{18,... | collective-permute-start | bytes 2359304 | tf_op jit(solution)/shard_map/ppermute | solution.py:93
  359.6 22.2 %collective-permute-start.58 = (bf16[192,2048]{1,0:T(8,128)(2,1)S(1)}, bf16[192,2048]{1,0:T(8,128)(2,1)S(1)}, u32[]{:S(2)}, u32[]{:S(2)}) collective-permute-start(bf16[192,2048]{1,0:T(8,128)(2,1)S(1)} %get-tuple-element.1127), channel_id=1, source_target_pairs={{0,2},{2,0},{4,6},{6,4},{8,10},{10,8},{12,14},{14,12},{16,18},{18,... | collective-permute-start | bytes 2359304 | tf_op jit(solution)/shard_map/ppermute | solution.py:93
  380.5 29.6 %collective-permute-start.61 = (bf16[192,2048]{1,0:T(8,128)(2,1)S(1)}, bf16[192,2048]{1,0:T(8,128)(2,1)S(1)}, u32[]{:S(2)}, u32[]{:S(2)}) collective-permute-start(bf16[192,2048]{1,0:T(8,128)(2,1)S(1)} %add_convert_fusion.12), channel_id=1, source_target_pairs={{0,4},{2,6},{4,0},{6,2},{8,12},{10,14},{12,8},{14,10},{16,20},{18,... | collective-permute-start | bytes 2359304 | tf_op jit(solution)/shard_map/ppermute | solution.py:93
  381.6 28.6 %collective-permute-start.60 = (bf16[512,1024]{1,0:T(8,128)(2,1)S(1)}, bf16[512,1024]{1,0:T(8,128)(2,1)S(1)}, u32[]{:S(2)}, u32[]{:S(2)}) collective-permute-start(bf16[512,1024]{1,0:T(8,128)(2,1)S(1)} %add_convert_fusion.2), channel_id=1, source_target_pairs={{0,8},{2,10},{4,12},{6,14},{8,16},{10,18},{12,20},{14,22},{16,24},... | collective-permute-start | bytes 3145736 | tf_op jit(solution)/shard_map/ppermute | solution.py:96
  396.6 93.8 %collective-permute-start.66 = (bf16[1024,512]{1,0:T(8,128)(2,1)}, bf16[1024,512]{1,0:T(8,128)(2,1)}, u32[]{:S(2)}, u32[]{:S(2)}) collective-permute-start(bf16[1024,512]{1,0:T(8,128)(2,1)} %add_convert_fusion.1), channel_id=1, source_target_pairs={{0,8},{2,10},{4,12},{6,14},{8,16},{10,18},{12,20},{14,22},{16,24},... | collective-permute-start | bytes 3145736 | tf_op jit(solution)/shard_map/ppermute | solution.py:96
  460.4 23.2 %collective-permute-start.69 = (bf16[512,256]{1,0:T(8,128)(2,1)S(1)}, bf16[512,256]{1,0:T(8,128)(2,1)S(1)}, u32[]{:S(2)}, u32[]{:S(2)}) collective-permute-start(bf16[512,256]{1,0:T(8,128)(2,1)S(1)} %copy-done.68), channel_id=1, source_target_pairs={{0,4},{2,6},{4,0},{6,2},{8,12},{10,14},{12,8},{14,10},{16,20},{18,... | collective-permute-start | bytes 786440 | tf_op jit(solution)/shard_map/ppermute | solution.py:93
  466.8 28.6 %collective-permute-start.73 = (bf16[512,1024]{1,0:T(8,128)(2,1)S(1)}, bf16[512,1024]{1,0:T(8,128)(2,1)S(1)}, u32[]{:S(2)}, u32[]{:S(2)}) collective-permute-start(bf16[512,1024]{1,0:T(8,128)(2,1)S(1)} %copy-done.80), channel_id=1, source_target_pairs={{0,8},{2,10},{4,12},{6,14},{8,16},{10,18},{12,20},{14,22},{16,24},... | collective-permute-start | bytes 3145736 | tf_op jit(solution)/shard_map/ppermute | solution.py:96
  472.4 65.9 %collective-permute-start.84 = (bf16[256,1536]{1,0:T(8,128)(2,1)}, bf16[256,1536]{1,0:T(8,128)(2,1)}, u32[]{:S(2)}, u32[]{:S(2)}) collective-permute-start(bf16[256,1536]{1,0:T(8,128)(2,1)} %dynamic-slice_convert_fusion.2), channel_id=1, source_target_pairs={{0,4},{2,6},{4,0},{6,2},{8,12},{10,14},{12,8},{14,10},{16,20},{18,... | collective-permute-start | bytes 2359304 | tf_op jit(solution)/shard_map/ppermute | solution.py:93
  478.1 35.1 %collective-permute-start.76 = (bf16[256,1536]{1,0:T(8,128)(2,1)S(1)}, bf16[256,1536]{1,0:T(8,128)(2,1)S(1)}, u32[]{:S(2)}, u32[]{:S(2)}) collective-permute-start(bf16[256,1536]{1,0:T(8,128)(2,1)S(1)} %dynamic-slice_convert_fusion.3), channel_id=1, source_target_pairs={{0,4},{2,6},{4,0},{6,2},{8,12},{10,14},{12,8},{14,10},{16,20},{18,... | collective-permute-start | bytes 2359304 | tf_op jit(solution)/shard_map/ppermute | solution.py:93
  514.2 24.1 %collective-permute-start.85 = (bf16[256,1536]{1,0:T(8,128)(2,1)}, bf16[256,1536]{1,0:T(8,128)(2,1)}, u32[]{:S(2)}, u32[]{:S(2)}) collective-permute-start(bf16[256,1536]{1,0:T(8,128)(2,1)} %add_convert_fusion.6), channel_id=1, source_target_pairs={{0,8},{2,10},{4,12},{6,14},{8,16},{10,18},{12,20},{14,22},{16,24},... | collective-permute-start | bytes 2359304 | tf_op jit(solution)/shard_map/ppermute | solution.py:96
  514.7 22.6 %collective-permute-start.86 = (bf16[512,256]{1,0:T(8,128)(2,1)}, bf16[512,256]{1,0:T(8,128)(2,1)}, u32[]{:S(2)}, u32[]{:S(2)}) collective-permute-start(bf16[512,256]{1,0:T(8,128)(2,1)} %add_convert_fusion.21), channel_id=1, source_target_pairs={{0,8},{2,10},{4,12},{6,14},{8,16},{10,18},{12,20},{14,22},{16,24},... | collective-permute-start | bytes 786440 | tf_op jit(solution)/shard_map/ppermute | solution.py:96
  515.1 27.8 %collective-permute-start.90 = (bf16[192,2048]{1,0:T(8,128)(2,1)S(1)}, bf16[192,2048]{1,0:T(8,128)(2,1)S(1)}, u32[]{:S(2)}, u32[]{:S(2)}) collective-permute-start(bf16[192,2048]{1,0:T(8,128)(2,1)S(1)} %add_convert_fusion.7), channel_id=1, source_target_pairs={{0,1},{1,0},{2,3},{3,2},{4,5},{5,4},{6,7},{7,6},{8,9},{9,8},{10,11... | collective-permute-start | bytes 2359304 | tf_op jit(solution)/shard_map/ppermute | solution.py:99
  516.0 30.7 %collective-permute-start.89 = (bf16[192,2048]{1,0:T(8,128)(2,1)S(1)}, bf16[192,2048]{1,0:T(8,128)(2,1)S(1)}, u32[]{:S(2)}, u32[]{:S(2)}) collective-permute-start(bf16[192,2048]{1,0:T(8,128)(2,1)S(1)} %add_convert_fusion.8), channel_id=1, source_target_pairs={{0,1},{1,0},{2,3},{3,2},{4,5},{5,4},{6,7},{7,6},{8,9},{9,8},{10,11... | collective-permute-start | bytes 2359304 | tf_op jit(solution)/shard_map/ppermute | solution.py:99
  538.4 35.1 %collective-permute-start.82 = (bf16[128,1024]{1,0:T(8,128)(2,1)}, bf16[128,1024]{1,0:T(8,128)(2,1)S(1)}, u32[]{:S(2)}, u32[]{:S(2)}) collective-permute-start(bf16[128,1024]{1,0:T(8,128)(2,1)} %get-tuple-element.1308), channel_id=1, source_target_pairs={{0,6},{2,4},{4,2},{6,0},{8,14},{10,12},{12,10},{14,8},{16,22},{18,... | collective-permute-start | bytes 786440 | tf_op jit(solution)/shard_map/ppermute | solution.py:93
  538.4 35.6 %collective-permute-start.81 = (bf16[128,1024]{1,0:T(8,128)(2,1)}, bf16[128,1024]{1,0:T(8,128)(2,1)S(1)}, u32[]{:S(2)}, u32[]{:S(2)}) collective-permute-start(bf16[128,1024]{1,0:T(8,128)(2,1)} %get-tuple-element.1306), channel_id=1, source_target_pairs={{0,4},{2,6},{4,0},{6,2},{8,12},{10,14},{12,8},{14,10},{16,20},{18,... | collective-permute-start | bytes 786440 | tf_op jit(solution)/shard_map/ppermute | solution.py:93
  574.8 36.0 %collective-permute-start.64 = (bf16[192,2048]{1,0:T(8,128)(2,1)S(1)}, bf16[192,2048]{1,0:T(8,128)(2,1)S(1)}, u32[]{:S(2)}, u32[]{:S(2)}) collective-permute-start(bf16[192,2048]{1,0:T(8,128)(2,1)S(1)} %copy-done.37), channel_id=1, source_target_pairs={{0,1},{1,0},{2,3},{3,2},{4,5},{5,4},{6,7},{7,6},{8,9},{9,8},{10,11... | collective-permute-start | bytes 2359304 | tf_op jit(solution)/shard_map/ppermute | solution.py:99
  576.1 37.2 %collective-permute-start.91 = (bf16[256,1536]{1,0:T(8,128)(2,1)S(1)}, bf16[256,1536]{1,0:T(8,128)(2,1)S(1)}, u32[]{:S(2)}, u32[]{:S(2)}) collective-permute-start(bf16[256,1536]{1,0:T(8,128)(2,1)S(1)} %copy-done.52), channel_id=1, source_target_pairs={{0,4},{2,6},{4,0},{6,2},{8,12},{10,14},{12,8},{14,10},{16,20},{18,... | collective-permute-start | bytes 2359304 | tf_op jit(solution)/shard_map/ppermute | solution.py:93
  581.2 32.1 %collective-permute-start.93 = (bf16[512,256]{1,0:T(8,128)(2,1)S(1)}, bf16[512,256]{1,0:T(8,128)(2,1)S(1)}, u32[]{:S(2)}, u32[]{:S(2)}) collective-permute-start(bf16[512,256]{1,0:T(8,128)(2,1)S(1)} %add_convert_fusion.19), channel_id=1, source_target_pairs={{0,8},{2,10},{4,12},{6,14},{8,16},{10,18},{12,20},{14,22},{16,24},... | collective-permute-start | bytes 786440 | tf_op jit(solution)/shard_map/ppermute | solution.py:96
  581.2 32.1 %collective-permute-start.92 = (bf16[256,1536]{1,0:T(8,128)(2,1)S(1)}, bf16[256,1536]{1,0:T(8,128)(2,1)S(1)}, u32[]{:S(2)}, u32[]{:S(2)}) collective-permute-start(bf16[256,1536]{1,0:T(8,128)(2,1)S(1)} %add_convert_fusion.4), channel_id=1, source_target_pairs={{0,8},{2,10},{4,12},{6,14},{8,16},{10,18},{12,20},{14,22},{16,24},... | collective-permute-start | bytes 2359304 | tf_op jit(solution)/shard_map/ppermute | solution.py:96
  (142 other events, 2101.8 us)

commit v3 on v2

v3 whole, which is shorter than its diff:
```python
import functools
import math

import jax
import jax.numpy as jnp
from jax import lax
from jax.experimental import pallas as pl
from jax.experimental.pallas import tpu as pltpu
from jax.sharding import PartitionSpec as P

HEAD_DIM = 128
EPSILON = 1e-05
MASKED = -1e30
PIECE = 96
LOW = jnp.bfloat16
WIDE = jnp.float32


def plain(one, two):
    return jnp.dot(one, two, preferred_element_type=WIDE)


def inner(one, two):
    return lax.dot_general(one, two, (((0,), (0,)), ((), ())), preferred_element_type=WIDE)


def outer(one, two):
    return lax.dot_general(one, two, (((1,), (1,)), ((), ())), preferred_element_type=WIDE)


def norm_forward(values):
    centered = values - jnp.mean(values, axis=1, keepdims=True)
    inverse = lax.rsqrt(jnp.mean(centered * centered, axis=1, keepdims=True) + EPSILON)
    return centered * inverse, inverse


def norm_backward(scaled, standard, inverse):
    return (
        scaled
        - jnp.mean(scaled, axis=1, keepdims=True)
        - standard * jnp.mean(scaled * standard, axis=1, keepdims=True)
    ) * inverse


def gelu_parts(values):
    half = 0.5 * (1.0 + lax.erf(values * (1.0 / math.sqrt(2.0))))
    slope = half + values * jnp.exp(-0.5 * values * values) * (1.0 / math.sqrt(2.0 * math.pi))
    return values * half, slope


def take(values, index, size, axis):
    return lax.dynamic_slice_in_dim(values, index * size, size, axis)


def put(whole, part, index, axis):
    return lax.dynamic_update_slice_in_dim(whole, part, index * part.shape[axis], axis)


def wide(values):
    return values.astype(WIDE)


def unscaled_probs(query, key, allowed):
    scores = jnp.where(allowed, outer(query, key) * (1.0 / math.sqrt(HEAD_DIM)), MASKED)
    shifted = jnp.exp(scores - jnp.max(scores, axis=1, keepdims=True))
    return shifted, 1.0 / jnp.sum(shifted, axis=1, keepdims=True)


def head_cuts(heads):
    return [slice(i * HEAD_DIM, (i + 1) * HEAD_DIM) for i in range(heads)]


def attention_forward(query, key, value, doc_row, doc_col, frame_row, frame_col, out):
    allowed = (doc_col[0] == doc_row[0]) & (frame_row[0] <= frame_col[0])
    for cut in head_cuts(out.shape[1] // HEAD_DIM):
        shifted, inverse = unscaled_probs(query[:, cut], key[:, cut], allowed)
        out[:, cut] = plain((shifted * inverse).astype(LOW), value[:, cut]).astype(LOW)


def attention_backward(
    query, key, value, grad, doc_row, doc_col, frame_row, frame_col, to_query, to_key, to_value
):
    allowed = (doc_col[0] == doc_row[0]) & (frame_row[0] <= frame_col[0])
    factor = 1.0 / math.sqrt(HEAD_DIM)
    for cut in head_cuts(grad.shape[1] // HEAD_DIM):
        shifted, inverse = unscaled_probs(query[:, cut], key[:, cut], allowed)
        probs = shifted * inverse
        grad_probs = outer(grad[:, cut], value[:, cut])
        delta = jnp.sum(grad_probs * probs, axis=1, keepdims=True)
        grad_scores = (probs * (grad_probs - delta)).astype(LOW)
        to_query[:, cut] = (plain(grad_scores, key[:, cut]) * factor).astype(LOW)
        to_key[:, cut] = (inner(grad_scores, query[:, cut]) * factor).astype(LOW)
        to_value[:, cut] = inner(probs.astype(LOW), grad[:, cut]).astype(LOW)


def attention_call(kernel, qkv, docs, frames, *grads):
    rows, half = qkv.shape[0] // 2, qkv.shape[1] // 3
    parts = [pl.BlockSpec((rows, half), lambda g, at=at: (g, at)) for at in range(3)]
    along = pl.BlockSpec((1, 1, rows), lambda g: (g, 0, 0))
    down = pl.BlockSpec((1, rows, 1), lambda g: (g, 0, 0))
    shape = jax.ShapeDtypeStruct((2 * rows, half), LOW)
    outs = 3 if grads else 1
    return pl.pallas_call(
        kernel,
        out_shape=[shape] * outs,
        grid=(2,),
        in_specs=parts + parts[:1] * len(grads) + [along, down, along, down],
        out_specs=parts[:1] * outs,
        compiler_params=pltpu.CompilerParams(vmem_limit_bytes=32 << 20),
        cost_estimate=pl.CostEstimate(flops=0, bytes_accessed=0, transcendentals=0),
    )(
        qkv,
        qkv,
        qkv,
        *grads,
        docs[:, None, :],
        docs[:, :, None],
        frames[:, None, :],
        frames[:, :, None],
    )


class Order:
    def __init__(self, token):
        self.token = token

    def tie(self, *values):
        tied = lax.optimization_barrier((*values, self.token))[:-1]
        return tied if len(tied) > 1 else tied[0]

    def wait(self, *values):
        *values, self.token = lax.optimization_barrier((*values, self.token))
        return values if len(values) > 1 else values[0]

    def run(self, step, *values):
        values = lax.optimization_barrier((*values, self.token))[:-1]
        results = step(*values)
        if not isinstance(results, tuple):
            return self.wait(results)
        return self.wait(*results)


class Links:
    def __init__(self, count, order):
        self.order = order
        self.ring_size = count // 4
        self.to = {k: [(i, i ^ k) for i in range(count)] for k in (1, 2, 3)}
        self.next = [(i, (i + 4) % count) for i in range(count)]
        place = lax.axis_index("dp")
        self.ring_at = place // 4
        self.cell = place % 4
        self.row = self.cell // 2
        self.core = self.cell % 2

    def swap(self, values, k):
        return lax.ppermute(self.order.tie(values), "dp", self.to[k])

    def to_core(self, values):
        size = values.shape[0] // max(1, values.shape[0] // PIECE)
        return [self.swap(values[at : at + size], 1) for at in range(0, values.shape[0], size)]

    def step(self, values):
        return lax.ppermute(self.order.tie(values), "dp", self.next)

    def across(self, values):
        return lax.ppermute(self.order.tie(values), "mp", [(0, 1), (1, 0)])

    def behind(self, k):
        return lax.rem(self.ring_at - k + 2 * self.ring_size, self.ring_size)

    def by_core(self, own, other, axis):
        return jnp.where(
            self.core == 0,
            jnp.concatenate([own, other], axis=axis),
            jnp.concatenate([other, own], axis=axis),
        )

    def join(self, parts, axis):
        shape = list(parts[0].shape)
        shape[axis] *= len(parts)
        joined = jnp.zeros(shape, parts[0].dtype)
        for k, part in enumerate(parts):
            joined = put(joined, part, self.cell ^ k, axis)
        return joined

    def lay(self, blocks, axis):
        shape = list(blocks[0].shape)
        shape[axis] *= len(blocks)
        whole = jnp.zeros(shape, blocks[0].dtype)
        for k, block in enumerate(blocks):
            whole = put(whole, block, self.behind(k), axis)
        return whole

    def lay_pairs(self, near, far, axis):
        shape = list(near[0].shape)
        shape[axis] *= 2 * len(near)
        whole = jnp.zeros(shape, near[0].dtype)
        for k in range(len(near)):
            at = self.behind(k) * 2
            whole = put(whole, near[k], at + self.row, axis)
            whole = put(whole, far[k], at + 1 - self.row, axis)
        return whole


def shards(
    count,
    tokens,
    doc_ids,
    frame_ids,
    gain_attn,
    w_query,
    w_key,
    w_value,
    w_output,
    gain_mlp,
    w_up,
    w_down,
    d_out,
):
    order = Order(doc_ids)
    run, wait = order.run, order.wait
    links = Links(count, order)
    swap, step, across = links.swap, links.step, links.across
    ring = links.ring_size
    rows, width = tokens.shape
    owned = width // count
    half = w_query.shape[1] // 2
    heads = half // HEAD_DIM
    hidden_part = w_up.shape[1] // 4
    block = width // ring
    pair = block // 2
    others = range(1, ring)

    chunk = rows // 2

    def chunks(values):
        return values[:chunk], values[chunk:]

    def qkv_shard(core, gain, *weights):
        taken = [(wide(take(w, core, half, 1)) * gain[:, None]).astype(LOW) for w in weights]
        return jnp.concatenate(taken, axis=1)

    qkv_send = run(
        lambda *w: qkv_shard(1 - links.core, *w), gain_attn, w_query, w_key, w_value
    )
    qkv_other = swap(qkv_send, 1)
    out_other = swap(run(lambda w: take(w, 1 - links.core, half, 0), w_output), 1)
    qkv_own = run(lambda *w: qkv_shard(links.core, *w), gain_attn, w_query, w_key, w_value)
    qkv_other, out_other = wait(qkv_other, out_other)
    qkv_block, out_block = run(
        lambda a, b, w, o: (
            links.by_core(a, b, 0),
            links.by_core(take(w, links.core, half, 0), o, 1),
        ),
        qkv_own,
        qkv_other,
        w_output,
        out_other,
    )

    def up_shard(weight, gain):
        scaled = (wide(weight) * gain[:, None]).astype(LOW)
        return tuple(take(scaled, links.cell ^ k, hidden_part, 1) for k in (0, 2, 1, 3))

    def put_near(whole, part, k, axis):
        return put(whole, part, links.behind(k) * 2 + links.row, axis)

    def put_far(whole, part, k, axis):
        return put(whole, part, links.behind(k) * 2 + 1 - links.row, axis)

    qkv_next, out_next, qkv_far = step(qkv_block), step(out_block), swap(qkv_block, 2)
    up_own, up_row, up_core, up_last = run(up_shard, w_up, gain_mlp)
    up_row, up_core = swap(up_row, 2), swap(up_core, 1)
    normed_own = run(lambda x: norm_forward(wide(x))[0].astype(LOW), tokens)
    normed_other = swap(normed_own, 1)
    docs_other, frames_other = swap(doc_ids, 1), swap(frame_ids, 1)
    qkv_full = jnp.zeros((width, 3 * half), LOW)
    out_full = jnp.zeros((half, width), LOW)
    qkv_full, out_full = run(
        lambda q, o, a, b: (put_near(q, a, 0, 0), put_near(o, b, 0, 1)),
        qkv_full,
        out_full,
        qkv_block,
        out_block,
    )
    down_own, down_row, down_core, down_last = run(
        lambda w: tuple(take(w, links.cell ^ k, hidden_part, 0) for k in (0, 2, 1, 3)), w_down
    )
    out_blocks = [out_block]
    for k in others:
        arriving = [qkv_next, out_next, qkv_far]
        if k == 1:
            arriving += [up_row, up_core]
        if k == 2:
            arriving += [up_last]
        if k == 3:
            arriving += [out_far]
        qkv_block, out_block, far_arrived, *arrived = wait(*arriving)
        if k < ring - 1:
            qkv_next, out_next = step(qkv_block), step(out_block)
        elif ring > 2:
            up_next = step(up_block)
        qkv_far = swap(qkv_block, 2)
        out_blocks.append(out_block)
        if k == 1:
            up_row, up_core = arrived
            up_last = swap(up_last, 3)
        if k == 2:
            (up_last,) = arrived
            out_far = swap(out_blocks[0], 2)
        if k == 3:
            (out_far,) = arrived
        if k == ring - 1:
            down_row, down_core = swap(down_row, 2), swap(down_core, 1)
        qkv_full, out_full = run(
            lambda q, o, a, b, f: (
                put_far(put_near(q, a, k, 0), f, k - 1, 0),
                put_near(o, b, k, 1),
            ),
            qkv_full,
            out_full,
            qkv_block,
            out_block,
            far_arrived,
        )
        if k == min(2, ring - 1):
            if ring < 3:
                up_last = wait(up_last)
            up_block = run(lambda *p: links.join(p, 0), up_own, up_core, up_row, up_last)
            if ring < 3:
                up_next = step(up_block)
        if k == 3:
            out_full = run(lambda o, f: put_far(o, f, 0, 1), out_full, out_far)
    normed_other, docs_other, frames_other = wait(normed_other, docs_other, frames_other)
    normed_one = run(lambda a, b: jnp.concatenate([a, b], axis=0), normed_own, normed_other)
    up_full = jnp.zeros((width, hidden_part), LOW)
    up_full = run(lambda w, b: put(w, b, links.behind(0), 0), up_full, up_block)
    up_block, qkv_far, down_row, down_core = wait(up_next, qkv_far, down_row, down_core)
    if ring > 2:
        up_next = step(up_block)
    fars_from = 1 if ring > 3 else 0
    out_fars = [swap(out_blocks[k], 2) for k in range(fars_from, ring)]
    down_last = swap(down_last, 3)
    d_out_core = swap(d_out, 1)
    qkv_full = run(lambda w, f: put_far(w, f, ring - 1, 0), qkv_full, qkv_far)
    qkv = run(lambda a, b: plain(a, b).astype(LOW), normed_one, qkv_full)

    docs = jnp.concatenate([doc_ids, docs_other], axis=0)
    frames = jnp.concatenate([frame_ids, frames_other], axis=0)
    docs, frames = wait(docs, frames)
    attended = run(lambda *v: attention_call(attention_forward, *v)[0], qkv, docs, frames)
    if ring > 2:
        up_arrived, down_last, *out_fars = wait(up_next, down_last, *out_fars)
        if ring > 3:
            up_next = step(up_arrived)
    else:
        up_arrived = up_block
        down_last, *out_fars = wait(down_last, *out_fars)
    d_out_chunks = chunks(d_out)
    d_out_far = [swap(d_out_chunks[0], 2)]

    def put_fars(whole, *fars):
        for k, far in enumerate(fars):
            whole = put_far(whole, far, fars_from + k, 1)
        return whole

    out_full = run(put_fars, out_full, *out_fars)

    def part_of(product, group):
        return lambda left, weights: chunks(
            product(left[group * rows : (group + 1) * rows], weights)
        )

    def low_part_of(product, group):
        part = part_of(product, group)
        return lambda left, weights: tuple(value.astype(LOW) for value in part(left, weights))

    def add_pieces(own, *pieces):
        return own + wide(jnp.concatenate(pieces))

    def add_pieces_low(own, *pieces):
        return add_pieces(own, *pieces).astype(LOW)

    yours = [links.to_core(v) for v in run(low_part_of(plain, 1), attended, out_full)]
    mine = run(part_of(plain, 0), attended, out_full)
    out_low, out_cross = [], []
    for j in range(2):
        out_low.append(run(add_pieces_low, mine[j], *wait(*yours[j])))
        out_cross.append(across(out_low[j]))
    down_block = run(lambda *p: links.join(p, 1), down_own, down_core, down_row, down_last)
    up_full = run(
        lambda w, a, b: put(put(w, a, links.behind(1), 0), b, links.behind(min(2, ring - 1)), 0),
        up_full,
        up_block,
        up_arrived,
    )

    def put_tokens(whole, group, part, *chunk_at):
        at = group * rows + (chunk * chunk_at[0] if chunk_at else 0)
        return lax.dynamic_update_slice_in_dim(whole, part, at, 0)

    grad_plane = jnp.zeros((4 * rows, width), LOW)
    grad_plane = run(lambda w, a: put_tokens(w, 0, a), grad_plane, d_out)
    down_full = jnp.zeros((hidden_part, width), LOW)
    down_full = run(lambda w, b: put(w, b, links.behind(0), 1), down_full, down_block)
    for k in range(3, ring):
        up_block = wait(up_next)
        if k < ring - 1:
            up_next = step(up_block)
            up_full = run(lambda w, b: put(w, b, links.behind(k), 0), up_full, up_block)
    down_next = step(down_block)
    if ring > 3:
        up_full = run(lambda w, b: put(w, b, links.behind(ring - 1), 0), up_full, up_block)

    def second_norm(tokens, low, cross):
        hidden = wide(tokens) + (wide(low) + wide(cross))
        standard, inverse = norm_forward(hidden)
        return hidden, standard, inverse, standard.astype(LOW)

    token_chunks = chunks(tokens)
    seconds, far_two, core_two, last_two = [], [], [], []
    normed_two = jnp.zeros((4 * rows, width), LOW)
    for j in range(2):
        out_cross[j] = wait(out_cross[j])
        seconds.append(run(second_norm, token_chunks[j], out_low[j], out_cross[j]))
        far_two.append(swap(seconds[j][3], 2))
        core_two.append(swap(seconds[j][3], 1))
        normed_two = run(lambda w, a: put_tokens(w, 0, a, j), normed_two, seconds[j][3])
    d_out_core, d_out_far[0] = wait(d_out_core, d_out_far[0])
    down_block = wait(down_next)
    if ring > 2:
        down_next = step(down_block)
    d_out_far.append(swap(d_out_chunks[1], 2))
    d_out_last = [swap(d_out_far[0], 1)]
    down_full, grad_plane = run(
        lambda w, b, g, x, y: (
            put(w, b, links.behind(1), 1),
            put_tokens(put_tokens(g, 1, x), 2, y, 0),
        ),
        down_full,
        down_block,
        grad_plane,
        d_out_core,
        d_out_far[0],
    )
    far_two[0], core_two[0] = wait(far_two[0], core_two[0])
    last_two.append(swap(far_two[0], 1))
    normed_two = run(
        lambda w, a, b: put_tokens(put_tokens(w, 1, a, 0), 2, b, 0),
        normed_two,
        core_two[0],
        far_two[0],
    )
    for k in range(2, ring - 1):
        down_block = wait(down_next)
        down_next = step(down_block)
        down_full = run(lambda w, b: put(w, b, links.behind(k), 1), down_full, down_block)
    far_two[1], core_two[1], last_two[0] = wait(far_two[1], core_two[1], last_two[0])
    last_pieces = links.to_core(far_two[1])
    normed_two = run(
        lambda w, a, b, c: put_tokens(
            put_tokens(put_tokens(w, 1, a, 1), 2, b, 1), 3, c, 0
        ),
        normed_two,
        core_two[1],
        far_two[1],
        last_two[0],
    )
    last_pieces = wait(*last_pieces)
    normed_two = run(
        lambda w, *p: put_tokens(w, 3, jnp.concatenate(p), 1), normed_two, *last_pieces
    )
    d_out_far[1], d_out_last[0] = wait(d_out_far[1], d_out_last[0])
    d_out_pieces = links.to_core(d_out_far[1])

    def feed_up(normed, weights):
        activated, slope = gelu_parts(plain(normed, weights))
        return activated.astype(LOW), slope.astype(LOW)

    act_low, slope = run(feed_up, normed_two, up_full)

    def part_down(act, grad, k, *arrived):
        part = inner(act, take(grad, links.behind(k), block, 1))
        for total in arrived:
            part = part + wide(total)
        return part.astype(LOW) if k < ring else part

    def part_up(normed, grad, k, *arrived):
        part = inner(take(normed, links.behind(k), block, 1), grad)
        for total in arrived:
            part = part + wide(total)
        return part.astype(LOW) if k < ring else part

    def ring_down(k, *arrived):
        total = run(lambda a, g, *t: part_down(a, g, k, *t), act_low, grad_plane, *arrived)
        return step(total) if k < ring else total

    def ring_up(k, *arrived):
        total = run(lambda n, g, *t: part_up(n, g, k, *t), normed_two, grad_pre, *arrived)
        return step(total) if k < ring else total

    d_out_pieces = wait(*d_out_pieces)
    grad_plane = run(
        lambda w, a, b, *p: put_tokens(
            put_tokens(put_tokens(w, 2, a, 1), 3, b, 0), 3, jnp.concatenate(p), 1
        ),
        grad_plane,
        d_out_far[1],
        d_out_last[0],
        *d_out_pieces,
    )
    down_sum = ring_down(1)
    if ring > 2:
        down_block = wait(down_next)
        down_full = run(lambda w, b: put(w, b, links.behind(ring - 1), 1), down_full, down_block)
    grad_pre = run(
        lambda g, w, s: (outer(g, w) * wide(s)).astype(LOW), grad_plane, down_full, slope
    )

    def near_sum(near, far):
        return (near + wide(far)).astype(LOW)

    last_n = [links.to_core(v) for v in run(low_part_of(outer, 3), grad_pre, up_full)]
    far_n = run(part_of(outer, 2), grad_pre, up_full)
    far_n = [
        swap(run(add_pieces_low, far_n[j], *wait(*last_n[j])), 2) for j in range(2)
    ]
    up_sum = ring_up(1)
    down_arrived = wait(down_sum)
    down_sum = ring_down(2, down_arrived)
    core_n = [links.to_core(v) for v in run(low_part_of(outer, 1), grad_pre, up_full)]
    own_n = run(part_of(outer, 0), grad_pre, up_full)
    near_n = [run(add_pieces, own_n[j], *wait(*core_n[j])) for j in range(2)]
    last_r = [links.to_core(v) for v in run(low_part_of(plain, 3), act_low, down_full)]
    far_r = run(part_of(plain, 2), act_low, down_full)
    far_r = [run(add_pieces_low, far_r[j], *wait(*last_r[j])) for j in range(2)]
    low_n, cross_n = [], []
    far_n[0] = wait(far_n[0])
    low_n.append(run(near_sum, near_n[0], far_n[0]))
    cross_n.append(across(low_n[0]))
    up_arrived = wait(up_sum)
    up_sum = ring_up(2, up_arrived)
    far_n[1] = wait(far_n[1])
    low_n.append(run(near_sum, near_n[1], far_n[1]))
    cross_n.append(across(low_n[1]))
    far_r = [swap(part, 2) for part in far_r]
    core_r = [links.to_core(v) for v in run(low_part_of(plain, 1), act_low, down_full)]
    own_r = run(part_of(plain, 0), act_low, down_full)
    near_r = [run(add_pieces, own_r[j], *wait(*core_r[j])) for j in range(2)]
    grad_hidden, grad_low = [], jnp.zeros((2 * rows, width), LOW)
    low_r, cross_r = [], []
    for j in range(2):
        cross_n[j] = wait(cross_n[j])

        def second_back(d_out, low, cross, standard, inverse):
            scaled = wide(low) + wide(cross)
            grad_hidden = wide(d_out) + norm_backward(scaled, standard, inverse)
            return grad_hidden, grad_hidden.astype(LOW)

        grad, low = run(
            second_back, d_out_chunks[j], low_n[j], cross_n[j], seconds[j][1], seconds[j][2]
        )
        other = links.to_core(low)
        grad_hidden.append(grad)
        if j == 0 and ring > 2:
            down_arrived = wait(down_sum)
            down_sum = ring_down(3, down_arrived)
        if j == 1:
            far_r = wait(*far_r)
            for i in range(2):
                low_r.append(run(near_sum, near_r[i], far_r[i]))
                cross_r.append(across(low_r[i]))
        grad_low = run(
            lambda w, a, *p: put_tokens(put_tokens(w, 0, a, j), 1, jnp.concatenate(p), j),
            grad_low,
            low,
            *wait(*other),
        )
    if ring > 2:
        up_arrived = wait(up_sum)
        up_sum = ring_up(3, up_arrived)

    def part_qkv(normed, grad, k):
        part = inner(take(normed, links.behind(k), block, 1), grad)
        return take(part, links.row, pair, 0), take(part, 1 - links.row, pair, 0).astype(LOW)

    def part_out(attended, grad, k):
        part = inner(attended, take(grad, links.behind(k), block, 1))
        return take(part, links.row, pair, 1), take(part, 1 - links.row, pair, 1).astype(LOW)

    out_owns, out_fars = [], []
    for k in range(1, ring + 1):
        own, far = run(lambda a, g: part_out(a, g, k), attended, grad_low)
        out_owns.append(own)
        out_fars.append(swap(far, 2))

    grad_att = run(lambda g, w: outer(g, w).astype(LOW), grad_low, out_full)
    grad_qkv = run(
        lambda q, d, f, g: jnp.concatenate(attention_call(attention_backward, q, d, f, g), axis=1),
        qkv,
        docs,
        frames,
        grad_att,
    )

    def add_row(own, far, *arrived):
        total = own + wide(far)
        for part in arrived:
            total = total + wide(part)
        return total

    def add_low(*parts):
        return add_row(*parts).astype(LOW)

    def cut(total, axis, size):
        parts = [take(total, links.cell, size, axis)]
        parts += [take(total, links.cell ^ k, size, axis).astype(LOW) for k in (1, 2, 3)]
        return tuple(parts)

    def send_ends(total, axis):
        own, *parts = run(lambda t: cut(t, axis, owned), total)
        return [own] + [swap(part, k) for k, part in zip((1, 2, 3), parts)]

    def up_end(gain, weight, *parts):
        raw = links.join([wide(part) for part in parts], 1)
        return raw * gain[:, None], jnp.sum(wide(weight) * raw, axis=1)

    def first_back(tokens, grads, lows, crosses):
        standard, inverse = norm_forward(wide(tokens))
        scaled = wide(jnp.concatenate(lows)) + wide(jnp.concatenate(crosses))
        return jnp.concatenate(grads) + norm_backward(scaled, standard, inverse)

    qkv_owns, qkv_fars = [], []
    for k in range(1, ring + 1):
        own, far = run(lambda n, g: part_qkv(n, g, k), normed_one, grad_qkv)
        qkv_owns.append(own)
        qkv_fars.append(swap(far, 2) if k < 3 else far)
        if k == 2:
            out_fars = wait(*out_fars)
            out_next = step(run(add_low, out_owns[0], out_fars[0]))
    core_m = [links.to_core(v) for v in run(low_part_of(outer, 1), grad_qkv, qkv_full)]
    own_m = run(part_of(outer, 0), grad_qkv, qkv_full)
    low_m = [run(add_pieces_low, own_m[j], *wait(*core_m[j])) for j in range(2)]
    cross_m = [across(part) for part in low_m]
    qkv_far = wait(qkv_fars[0])
    qkv_next = step(run(add_low, qkv_owns[0], qkv_far))
    if ring > 2:
        qkv_fars[2] = swap(qkv_fars[2], 2)
    for k in range(2, ring + 1):
        add = add_low if k < ring else add_row
        out_arrived = wait(out_next)
        out_sum = run(add, out_owns[k - 1], out_fars[k - 1], out_arrived)
        if k < ring:
            out_next = step(out_sum)
        if k == 2:
            down_arrived = wait(down_sum)
            for i in range(4, ring + 1) if ring > 2 else (2,):
                down_sum = ring_down(i, down_arrived)
                if i < ring:
                    down_arrived = wait(down_sum)
            down_ends = send_ends(down_sum, 1)
            cross_r = wait(*cross_r)
        if k == min(3, ring):
            up_arrived = wait(up_sum)
            for i in range(4, ring + 1) if ring > 2 else (2,):
                up_sum = ring_up(i, up_arrived)
                if i < ring:
                    up_arrived = wait(up_sum)
            up_ends = send_ends(up_sum, 0)
        qkv_far = wait(qkv_fars[k - 1])
        qkv_arrived = wait(qkv_next)
        qkv_sum = run(add, qkv_owns[k - 1], qkv_far, qkv_arrived)
        if k < ring:
            qkv_next = step(qkv_sum)
        if k + 1 < ring:
            qkv_fars[k + 1] = swap(qkv_fars[k + 1], 2)
        if k == 2:
            result = run(
                lambda *p: jnp.concatenate(p[:2])
                + (wide(jnp.concatenate(p[2:4])) + wide(jnp.concatenate(p[4:]))),
                seconds[0][0],
                seconds[1][0],
                *low_r,
                *cross_r,
            )
            cross_m = wait(*cross_m)
        if k == min(3, ring):
            d_tokens = run(
                lambda t, *p: first_back(t, p[:2], p[2:4], p[4:]),
                tokens,
                *grad_hidden,
                *low_m,
                *cross_m,
            )
            down_ends = wait(*down_ends)
            d_w_down = run(lambda *p: links.join([wide(part) for part in p], 0), *down_ends)
            up_ends = wait(*up_ends)
            d_w_up, gain_mlp_own = run(up_end, gain_mlp, w_up, *up_ends)
            gain_mlp_other = across(gain_mlp_own)

    def ends(qkv, out):
        return (
            take(qkv, links.core, owned, 0),
            take(qkv, 1 - links.core, owned, 0).astype(LOW),
            take(out, links.core, owned, 1),
            take(out, 1 - links.core, owned, 1).astype(LOW),
        )

    qkv_mine, qkv_yours, out_mine, out_yours = run(ends, qkv_sum, out_sum)
    qkv_yours, out_yours = swap(qkv_yours, 1), swap(out_yours, 1)
    qkv_yours, out_yours = wait(qkv_yours, out_yours)
    d_w_output = links.by_core(out_mine, wide(out_yours), 0)
    raw = [
        links.by_core(qkv_mine[:, at : at + half], wide(qkv_yours[:, at : at + half]), 1)
        for at in (0, half, 2 * half)
    ]
    gain_attn_own = sum(
        jnp.sum(wide(weight) * part, axis=1) for weight, part in zip((w_query, w_key, w_value), raw)
    )
    d_gain_attn = gain_attn_own + across(gain_attn_own)
    d_gain_mlp = gain_mlp_own + gain_mlp_other
    d_w_query, d_w_key, d_w_value = (part * gain_attn[:, None] for part in raw)
    return (
        result,
        d_tokens,
        d_gain_attn,
        d_w_query,
        d_w_key,
        d_w_value,
        d_w_output,
        d_gain_mlp,
        d_w_up,
        d_w_down,
    )


def solution(mesh):
    return jax.shard_map(
        functools.partial(shards, mesh.shape["dp"]),
        mesh=mesh,
        in_specs=(
            P("dp", None),
            P("dp", None),
            P("dp", None),
            P("dp"),
            P("dp", "mp"),
            P("dp", "mp"),
            P("dp", "mp"),
            P("mp", "dp"),
            P("dp"),
            P("dp", "mp"),
            P("mp", "dp"),
            P("dp", None),
        ),
        out_specs=(
            P("dp", None),
            P("dp", None),
            P("dp"),
            P("dp", "mp"),
            P("dp", "mp"),
            P("dp", "mp"),
            P("mp", "dp"),
            P("dp"),
            P("dp", "mp"),
            P("mp", "dp"),
        ),
        check_vma=False,
    )
```

time: 634 us -> 612 us (0.965)
  local copies, waits for them, and re-layouts: 109 us -> 91.4 us
  Pallas kernels: 0 us -> 11.3 us
  starting transfers between devices: 70.7 us -> 61 us
    ppermute x24, waiting for transfers between devices: 70 us -> 158 us  [step(): return lax.ppermute(self.order.tie(values), 'dp', self.next)]
    ppermute x64 -> x80, waiting for transfers between devices: 163 us -> 80.2 us  [swap(): return lax.ppermute(self.order.tie(values), 'dp', self.to[k])]
    dynamic_update_slice x0 -> x14, local copies, waits for them, and re-layouts: none -> 19.7 us  [put_tokens(): return lax.dynamic_update_slice_in_dim(whole, part, at, 0)]
    dot_general x6 -> x0, matrix products: 14.6 us -> none  [the longest x1 4.22 us: attention_back(): jnp.einsum('ghqk,gqhe->gkhe', probs.astype(LOW), grad_att, preferred_elem...]
    ppermute x24, starting transfers between devices: 22.1 us -> 9.17 us  [step(): return lax.ppermute(self.order.tie(values), 'dp', self.next)]
    pallas_call x0 -> x2, Pallas kernels: none -> 11.3 us  [attention_call(): pl.pallas_call(kernel, out_shape=[shape] * outs, grid=(2,), in_specs=part...]
    dynamic_update_slice x34, local copies, waits for them, and re-layouts: 38.8 us -> 28.3 us  [put(): lax.dynamic_update_slice_in_dim(whole, part, index * part.shape[axis], axis)]
    unnamed x200 -> x157, local copies, waits for them, and re-layouts: 25.2 us -> 15.2 us
  transfers between devices with their start and end apart: 98 -> 114, of which waited for: 40 -> 54; matrix products, arithmetic and copies ran while one was open for 38% -> 36% of each run, Pallas kernels for 0% -> 2%
where the time goes in v3:
time: 612 us; the launch traced here: 606 us
  waiting for transfers between devices  294 us (48%)
  matrix products  103 us (17%)
  local copies, waits for them, and re-layouts  91.4 us (15%)
  starting transfers between devices  61 us (10%)
  other arithmetic  40.9 us (7%)
  Pallas kernels  11.3 us (2%)
    ppermute x24, waiting for transfers between devices, step(): return lax.ppermute(self.order.tie(values), 'dp', self.next)  158 us
    ppermute x80, waiting for transfers between devices, swap(): return lax.ppermute(self.order.tie(values), 'dp', self.to[k])  80.2 us
    ppermute x10, waiting for transfers between devices, across(): return lax.ppermute(self.order.tie(values), 'mp', [(0, 1), (1, 0)])  56.2 us
    ppermute x80, starting transfers between devices, swap(): return lax.ppermute(self.order.tie(values), 'dp', self.to[k])  39.4 us
    dot_general x8, matrix products, plain(): return jnp.dot(one, two, preferred_element_type=WIDE)  36.5 us
    dot_general x16, matrix products, inner(): lax.dot_general(one, two, (((0,), (0,)), ((), ())), preferred_element_typ...  36.2 us
    dot_general x8, matrix products, outer(): lax.dot_general(one, two, (((1,), (1,)), ((), ())), preferred_element_typ...  30.4 us
    dynamic_update_slice x34, local copies, waits for them, and re-layouts, put(): lax.dynamic_update_slice_in_dim(whole, part, index * part.shape[axis], axis)  28.3 us
  transfers between devices with their start and end apart: 114, of which 54 were waited for; matrix products, arithmetic and copies ran while one was open for 36% of the time, Pallas kernels for 2%

profile of v3, /device:TPU:0, one launch (start us, length us, event | category | flops | bytes accessed | tf_op | source)
XLA Modules:
  0.0 605.7 jit_solution(18010584001652153960)
XLA Ops:
  22.9 13.6 %collective-permute-done.6 = bf16[512,256]{1,0:T(8,128)(2,1)} collective-permute-done((bf16[512,256]{1,0:T(8,128)(2,1)S(1)}, bf16[512,256]{1,0:T(8,128)(2,1)}, u32[]{:S(2)}, u32[]{:S(2)}) %collective-permute-start.6) | collective-permute-done | bytes 262176 | tf_op jit(solution)/shard_map/ppermute | solution.py:163
  47.1 17.1 %collective-permute-done.11 = bf16[512,256]{1,0:T(8,128)(2,1)} collective-permute-done((bf16[512,256]{1,0:T(8,128)(2,1)}, bf16[512,256]{1,0:T(8,128)(2,1)}, u32[]{:S(2)}, u32[]{:S(2)}) %collective-permute-start.11) | collective-permute-done | bytes 262176 | tf_op jit(solution)/shard_map/ppermute | solution.py:163
  71.9 18.1 %collective-permute-done.15 = bf16[512,256]{1,0:T(8,128)(2,1)} collective-permute-done((bf16[512,256]{1,0:T(8,128)(2,1)}, bf16[512,256]{1,0:T(8,128)(2,1)}, u32[]{:S(2)}, u32[]{:S(2)}) %collective-permute-start.15) | collective-permute-done | bytes 262176 | tf_op jit(solution)/shard_map/ppermute | solution.py:163
  96.8 18.9 %collective-permute-done.20 = bf16[1024,128]{1,0:T(8,128)(2,1)S(1)} collective-permute-done((bf16[1024,128]{1,0:T(8,128)(2,1)S(1)}, bf16[1024,128]{1,0:T(8,128)(2,1)S(1)}, u32[]{:S(2)}, u32[]{:S(2)}) %collective-permute-start.20) | collective-permute-done | bytes 262176 | tf_op jit(solution)/shard_map/ppermute | solution.py:156
  122.1 8.0 %convolution_convert_fusion.query.key.value = bf16[768,1536]{1,0:T(8,128)(2,1)S(1)} fusion(bf16[768,2048]{1,0:T(8,128)(2,1)S(1)} %pad_maximum_fusion, bf16[2048,1536]{1,0:T(8,128)(2,1)} %constant_dynamic-update-slice_fusion.30), kind=kOutput, calls=%fused_computation.19 | convolution fusion | flops 4833017856 | bytes 11796480 | tf_op jit(solution)/shard_map/dot_general | solution.py:20
  132.3 4.4 shard_map.195
  138.5 5.6 collective-permute-done.26
  161.1 3.5 broadcast.157
  164.6 6.5 %copy.61 = bf16[1536,2048]{1,0:T(8,128)(2,1)} copy(bf16[1536,2048]{1,0:T(8,128)(2,1)} %broadcast.157) | data formatting | bytes 12582912
  185.5 9.5 %collective-permute-done.33 = bf16[192,2048]{1,0:T(8,128)(2,1)S(1)} collective-permute-done((bf16[192,2048]{1,0:T(8,128)(2,1)S(1)}, bf16[192,2048]{1,0:T(8,128)(2,1)S(1)}, u32[]{:S(2)}, u32[]{:S(2)}) %collective-permute-start.33) | collective-permute-done | bytes 786464 | tf_op jit(solution)/shard_map/ppermute | solution.py:166
  200.4 5.8 collective-permute-done.36
  216.7 15.3 %collective-permute-done.42 = bf16[1024,512]{1,0:T(8,128)(2,1)} collective-permute-done((bf16[1024,512]{1,0:T(8,128)(2,1)}, bf16[1024,512]{1,0:T(8,128)(2,1)}, u32[]{:S(2)}, u32[]{:S(2)}) %collective-permute-start.42) | collective-permute-done | bytes 1048608 | tf_op jit(solution)/shard_map/ppermute | solution.py:163
  244.4 10.6 %fusion.4 = (bf16[1536,1024]{1,0:T(8,128)(2,1)S(1)}, bf16[1536,1024]{1,0:T(8,128)(2,1)S(1)}) fusion(bf16[1536,2048]{1,0:T(8,128)(2,1)} %maximum_dynamic-update-slice_fusion, bf16[2048,1024]{1,0:T(8,128)(2,1)S(1)} %copy-done.26), kind=kOutput, calls=%fused_computation.5 | convolution fusion | flops 6459752448 | bytes 16777216 | tf_op jit(solution)/shard_map/dot_general | solution.py:20
  258.1 3.2 fusion.39
  261.8 8.8 %collective-permute-done.47 = bf16[1024,512]{1,0:T(8,128)(2,1)S(1)} collective-permute-done((bf16[1024,512]{1,0:T(8,128)(2,1)}, bf16[1024,512]{1,0:T(8,128)(2,1)S(1)}, u32[]{:S(2)}, u32[]{:S(2)}) %collective-permute-start.47) | collective-permute-done | bytes 1048608 | tf_op jit(solution)/shard_map/ppermute | solution.py:163
  271.7 10.1 %multiply_convert_fusion = bf16[1536,1024]{1,0:T(8,128)(2,1)S(1)} fusion(bf16[1536,1024]{1,0:T(8,128)(2,1)S(1)} %get-tuple-element.1174, bf16[1536,2048]{1,0:T(8,128)(2,1)} %maximum_dynamic-update-slice_fusion.1, bf16[1024,2048]{1,0:T(8,128)(2,1)} %constant_dynamic-update-slice_fusion.4), kind=kOutput, calls=%fused_computation.6 | convolution fusion | flops 6447169536 | bytes 16777216 | tf_op jit(solution)/shard_map/dot_general | solution.py:28
  289.6 3.2 fusion.42
  295.2 3.2 add_convert_fusion.3
  306.8 4.0 convolution_convert_fusion.2
  310.9 4.0 fusion.77
  319.5 9.8 %collective-permute-done.61 = bf16[192,2048]{1,0:T(8,128)(2,1)S(1)} collective-permute-done((bf16[192,2048]{1,0:T(8,128)(2,1)S(1)}, bf16[192,2048]{1,0:T(8,128)(2,1)S(1)}, u32[]{:S(2)}, u32[]{:S(2)}) %collective-permute-start.61) | collective-permute-done | bytes 786464 | tf_op jit(solution)/shard_map/ppermute | solution.py:156
  329.6 3.2 add_convert_fusion.2
  333.0 4.0 convolution_convert_fusion.1
  337.1 4.0 fusion.74
  348.1 15.6 %collective-permute-done.71 = bf16[192,2048]{1,0:T(8,128)(2,1)S(1)} collective-permute-done((bf16[192,2048]{1,0:T(8,128)(2,1)S(1)}, bf16[192,2048]{1,0:T(8,128)(2,1)S(1)}, u32[]{:S(2)}, u32[]{:S(2)}) %collective-permute-start.71) | collective-permute-done | bytes 786464 | tf_op jit(solution)/shard_map/ppermute | solution.py:166
  366.5 4.2 add_convert_fusion.1
  371.7 7.6 %collective-permute-done.70 = bf16[192,2048]{1,0:T(8,128)(2,1)S(1)} collective-permute-done((bf16[192,2048]{1,0:T(8,128)(2,1)S(1)}, bf16[192,2048]{1,0:T(8,128)(2,1)S(1)}, u32[]{:S(2)}, u32[]{:S(2)}) %collective-permute-start.70) | collective-permute-done | bytes 786464 | tf_op jit(solution)/shard_map/ppermute | solution.py:166
  385.3 13.3 %collective-permute-done.82 = bf16[512,1024]{1,0:T(8,128)(2,1)S(1)} collective-permute-done((bf16[512,1024]{1,0:T(8,128)(2,1)S(1)}, bf16[512,1024]{1,0:T(8,128)(2,1)S(1)}, u32[]{:S(2)}, u32[]{:S(2)}) %collective-permute-start.82) | collective-permute-done | bytes 1048608 | tf_op jit(solution)/shard_map/ppermute | solution.py:163
  398.5 4.2 add_convert_fusion
  415.1 7.0 %shard_map.196 = (bf16[768,512]{1,0:T(8,128)(2,1)S(1)}, bf16[768,512]{1,0:T(8,128)(2,1)S(1)}, bf16[768,512]{1,0:T(8,128)(2,1)S(1)}) custom-call(bf16[768,1536]{1,0:T(8,128)(2,1)S(1)} %convolution_convert_fusion.query.key.value, bf16[768,1536]{1,0:T(8,128)(2,1)S(1)} %convolution_convert_fusion.query.key.value, ...), custom_call_target="tpu_custom_call" | custom-call | tf_op jit(solution)/shard_map/pallas_call | solution.py:103
  432.1 3.5 collective-permute-done.83
  437.1 4.1 collective-permute-done.84
  442.0 4.9 collective-permute-done.85
  446.8 5.6 collective-permute-done.86
  455.8 5.4 convolution_convert_fusion.5
  461.4 5.0 fusion.55
  472.7 9.4 %collective-permute-done.87 = bf16[512,256]{1,0:T(8,128)(2,1)S(1)} collective-permute-done((bf16[512,256]{1,0:T(8,128)(2,1)S(1)}, bf16[512,256]{1,0:T(8,128)(2,1)S(1)}, u32[]{:S(2)}, u32[]{:S(2)}) %collective-permute-start.87) | collective-permute-done | bytes 262176 | tf_op jit(solution)/shard_map/ppermute | solution.py:163
  482.3 3.5 convert_add_fusion.2
  487.1 3.5 collective-permute-done.78
  492.6 11.8 %collective-permute-done.94 = bf16[256,1536]{1,0:T(8,128)(2,1)S(1)} collective-permute-done((bf16[256,1536]{1,0:T(8,128)(2,1)S(1)}, bf16[256,1536]{1,0:T(8,128)(2,1)S(1)}, u32[]{:S(2)}, u32[]{:S(2)}) %collective-permute-start.94) | collective-permute-done | bytes 786464 | tf_op jit(solution)/shard_map/ppermute | solution.py:163
  507.5 16.0 %collective-permute-done.96 = bf16[192,2048]{1,0:T(8,128)(2,1)S(1)} collective-permute-done((bf16[192,2048]{1,0:T(8,128)(2,1)S(1)}, bf16[192,2048]{1,0:T(8,128)(2,1)S(1)}, u32[]{:S(2)}, u32[]{:S(2)}) %collective-permute-start.96) | collective-permute-done | bytes 786464 | tf_op jit(solution)/shard_map/ppermute | solution.py:166
  524.3 5.8 collective-permute-done.99
  530.3 3.2 convert_add_fusion.1
  535.3 13.8 %collective-permute-done.100 = bf16[256,1536]{1,0:T(8,128)(2,1)S(1)} collective-permute-done((bf16[256,1536]{1,0:T(8,128)(2,1)S(1)}, bf16[256,1536]{1,0:T(8,128)(2,1)S(1)}, u32[]{:S(2)}, u32[]{:S(2)}) %collective-permute-start.100) | collective-permute-done | bytes 786464 | tf_op jit(solution)/shard_map/ppermute | solution.py:163
  552.2 4.5 fusion.14
  559.0 6.9 %collective-permute-done.104 = bf16[128,1024]{1,0:T(8,128)(2,1)S(1)} collective-permute-done((bf16[128,1024]{1,0:T(8,128)(2,1)S(1)}, bf16[128,1024]{1,0:T(8,128)(2,1)S(1)}, u32[]{:S(2)}, u32[]{:S(2)}) %collective-permute-start.104) | collective-permute-done | bytes 262176 | tf_op jit(solution)/shard_map/ppermute | solution.py:156
  565.9 4.7 collective-permute-done.105
  572.8 19.6 %collective-permute-done.109 = bf16[256,1536]{1,0:T(8,128)(2,1)S(1)} collective-permute-done((bf16[256,1536]{1,0:T(8,128)(2,1)S(1)}, bf16[256,1536]{1,0:T(8,128)(2,1)S(1)}, u32[]{:S(2)}, u32[]{:S(2)}) %collective-permute-start.109) | collective-permute-done | bytes 786464 | tf_op jit(solution)/shard_map/ppermute | solution.py:163
  (582 shorter events, 224.8 us)
Async XLA Ops:
  8.0 28.6 %collective-permute-start.5 = (bf16[256,1536]{1,0:T(8,128)(2,1)S(1)}, bf16[256,1536]{1,0:T(8,128)(2,1)}, u32[]{:S(2)}, u32[]{:S(2)}) collective-permute-start(bf16[256,1536]{1,0:T(8,128)(2,1)S(1)} %maximum_select_fusion), channel_id=1, source_target_pairs={{0,8},{2,10},{4,12},{6,14},{8,16},{10,18},{12,20},{14,22},{16,24},... | collective-permute-start | bytes 2359304 | tf_op jit(solution)/shard_map/ppermute | solution.py:163
  11.1 25.5 %collective-permute-start.7 = (bf16[256,1536]{1,0:T(8,128)(2,1)S(1)}, bf16[256,1536]{1,0:T(8,128)(2,1)S(1)}, u32[]{:S(2)}, u32[]{:S(2)}) collective-permute-start(bf16[256,1536]{1,0:T(8,128)(2,1)S(1)} %maximum_select_fusion), channel_id=1, source_target_pairs={{0,4},{2,6},{4,0},{6,2},{8,12},{10,14},{12,8},{14,10},{16,20},{18,... | collective-permute-start | bytes 2359304 | tf_op jit(solution)/shard_map/ppermute | solution.py:156
  37.5 26.7 %collective-permute-start.10 = (bf16[256,1536]{1,0:T(8,128)(2,1)}, bf16[256,1536]{1,0:T(8,128)(2,1)}, u32[]{:S(2)}, u32[]{:S(2)}) collective-permute-start(bf16[256,1536]{1,0:T(8,128)(2,1)} %collective-permute-done.5), channel_id=1, source_target_pairs={{0,8},{2,10},{4,12},{6,14},{8,16},{10,18},{12,20},{14,22},{16,24},... | collective-permute-start | bytes 2359304 | tf_op jit(solution)/shard_map/ppermute | solution.py:163
  38.4 25.8 %collective-permute-start.12 = (bf16[256,1536]{1,0:T(8,128)(2,1)}, bf16[256,1536]{1,0:T(8,128)(2,1)}, u32[]{:S(2)}, u32[]{:S(2)}) collective-permute-start(bf16[256,1536]{1,0:T(8,128)(2,1)} %collective-permute-done.5), channel_id=1, source_target_pairs={{0,4},{2,6},{4,0},{6,2},{8,12},{10,14},{12,8},{14,10},{16,20},{18,... | collective-permute-start | bytes 2359304 | tf_op jit(solution)/shard_map/ppermute | solution.py:156
  41.2 53.6 %collective-permute-start.2 = (bf16[384,2048]{1,0:T(8,128)(2,1)}, bf16[384,2048]{1,0:T(8,128)(2,1)S(1)}, u32[]{:S(2)}, u32[]{:S(2)}) collective-permute-start(bf16[384,2048]{1,0:T(8,128)(2,1)} %fusion.17), channel_id=1, source_target_pairs={{0,2},{2,0},{4,6},{6,4},{8,10},{10,8},{12,14},{14,12},{16,18},{18,... | collective-permute-start | bytes 4718600 | tf_op jit(solution)/shard_map/ppermute | solution.py:156
  41.2 23.0 %collective-permute-start.11 = (bf16[512,256]{1,0:T(8,128)(2,1)}, bf16[512,256]{1,0:T(8,128)(2,1)}, u32[]{:S(2)}, u32[]{:S(2)}) collective-permute-start(bf16[512,256]{1,0:T(8,128)(2,1)} %collective-permute-done.6), channel_id=1, source_target_pairs={{0,8},{2,10},{4,12},{6,14},{8,16},{10,18},{12,20},{14,22},{16,24},... | collective-permute-start | bytes 786440 | tf_op jit(solution)/shard_map/ppermute | solution.py:163
  64.2 26.3 %collective-permute-start.14 = (bf16[256,1536]{1,0:T(8,128)(2,1)}, bf16[256,1536]{1,0:T(8,128)(2,1)S(1)}, u32[]{:S(2)}, u32[]{:S(2)}) collective-permute-start(bf16[256,1536]{1,0:T(8,128)(2,1)} %collective-permute-done.10), channel_id=1, source_target_pairs={{0,8},{2,10},{4,12},{6,14},{8,16},{10,18},{12,20},{14,22},{16,24},... | collective-permute-start | bytes 2359304 | tf_op jit(solution)/shard_map/ppermute | solution.py:163
  64.2 26.2 %collective-permute-start.16 = (bf16[256,1536]{1,0:T(8,128)(2,1)}, bf16[256,1536]{1,0:T(8,128)(2,1)S(1)}, u32[]{:S(2)}, u32[]{:S(2)}) collective-permute-start(bf16[256,1536]{1,0:T(8,128)(2,1)} %collective-permute-done.10), channel_id=1, source_target_pairs={{0,4},{2,6},{4,0},{6,2},{8,12},{10,14},{12,8},{14,10},{16,20},{18,... | collective-permute-start | bytes 2359304 | tf_op jit(solution)/shard_map/ppermute | solution.py:156
  90.5 27.1 %collective-permute-start.18 = (bf16[512,1024]{1,0:T(8,128)(2,1)S(1)}, bf16[512,1024]{1,0:T(8,128)(2,1)}, u32[]{:S(2)}, u32[]{:S(2)}) collective-permute-start(bf16[512,1024]{1,0:T(8,128)(2,1)S(1)} %constant_dynamic-update-slice_fusion.36), channel_id=1, source_target_pairs={{0,8},{2,10},{4,12},{6,14},{8,16},{10,18},{12,20},{14,22},{16,24},... | collective-permute-start | bytes 3145736 | tf_op jit(solution)/shard_map/ppermute | solution.py:163
  90.5 25.2 %collective-permute-start.19 = (bf16[256,1536]{1,0:T(8,128)(2,1)S(1)}, bf16[256,1536]{1,0:T(8,128)(2,1)S(1)}, u32[]{:S(2)}, u32[]{:S(2)}) collective-permute-start(bf16[256,1536]{1,0:T(8,128)(2,1)S(1)} %collective-permute-done.14), channel_id=1, source_target_pairs={{0,4},{2,6},{4,0},{6,2},{8,12},{10,14},{12,8},{14,10},{16,20},{18,... | collective-permute-start | bytes 2359304 | tf_op jit(solution)/shard_map/ppermute | solution.py:156
  118.5 26.6 %collective-permute-start.22 = (bf16[512,1024]{1,0:T(8,128)(2,1)}, bf16[512,1024]{1,0:T(8,128)(2,1)}, u32[]{:S(2)}, u32[]{:S(2)}) collective-permute-start(bf16[512,1024]{1,0:T(8,128)(2,1)} %collective-permute-done.18), channel_id=1, source_target_pairs={{0,8},{2,10},{4,12},{6,14},{8,16},{10,18},{12,20},{14,22},{16,24},... | collective-permute-start | bytes 3145736 | tf_op jit(solution)/shard_map/ppermute | solution.py:163
  120.9 23.3 %collective-permute-start.26 = (bf16[512,256]{1,0:T(8,128)(2,1)}, bf16[512,256]{1,0:T(8,128)(2,1)}, u32[]{:S(2)}, u32[]{:S(2)}) collective-permute-start(bf16[512,256]{1,0:T(8,128)(2,1)} %collective-permute-done.15), channel_id=1, source_target_pairs={{0,4},{2,6},{4,0},{6,2},{8,12},{10,14},{12,8},{14,10},{16,20},{18,... | collective-permute-start | bytes 786440 | tf_op jit(solution)/shard_map/ppermute | solution.py:156
  136.7 62.9 %collective-permute-start.37 = (bf16[384,2048]{1,0:T(8,128)(2,1)S(1)}, bf16[384,2048]{1,0:T(8,128)(2,1)S(1)}, u32[]{:S(2)}, u32[]{:S(2)}) collective-permute-start(bf16[384,2048]{1,0:T(8,128)(2,1)S(1)} %copy-done.19), channel_id=1, source_target_pairs={{0,2},{2,0},{4,6},{6,4},{8,10},{10,8},{12,14},{14,12},{16,18},{18,... | collective-permute-start | bytes 4718600 | tf_op jit(solution)/shard_map/ppermute | solution.py:156
  152.6 27.2 %collective-permute-start.32 = (bf16[512,1024]{1,0:T(8,128)(2,1)}, bf16[512,1024]{1,0:T(8,128)(2,1)S(1)}, u32[]{:S(2)}, u32[]{:S(2)}) collective-permute-start(bf16[512,1024]{1,0:T(8,128)(2,1)} %collective-permute-done.22), channel_id=1, source_target_pairs={{0,8},{2,10},{4,12},{6,14},{8,16},{10,18},{12,20},{14,22},{16,24},... | collective-permute-start | bytes 3145736 | tf_op jit(solution)/shard_map/ppermute | solution.py:163
  153.1 47.1 %collective-permute-start.38 = (bf16[192,2048]{1,0:T(8,128)(2,1)S(1)}, bf16[192,2048]{1,0:T(8,128)(2,1)S(1)}, u32[]{:S(2)}, u32[]{:S(2)}) collective-permute-start(bf16[192,2048]{1,0:T(8,128)(2,1)S(1)} %copy-done.30), channel_id=1, source_target_pairs={{0,4},{2,6},{4,0},{6,2},{8,12},{10,14},{12,8},{14,10},{16,20},{18,... | collective-permute-start | bytes 2359304 | tf_op jit(solution)/shard_map/ppermute | solution.py:156
  154.6 25.4 %collective-permute-start.29 = (bf16[192,2048]{1,0:T(8,128)(2,1)S(1)}, bf16[192,2048]{1,0:T(8,128)(2,1)S(1)}, u32[]{:S(2)}, u32[]{:S(2)}) collective-permute-start(bf16[192,2048]{1,0:T(8,128)(2,1)S(1)} %add_convert_fusion.18), channel_id=1, source_target_pairs={{0,1},{1,0},{2,3},{3,2},{4,5},{5,4},{6,7},{7,6},{8,9},{9,8},{10,11... | collective-permute-start | bytes 2359304 | tf_op jit(solution)/shard_map/ppermute | solution.py:166
  179.9 26.3 %collective-permute-start.36 = (bf16[1024,512]{1,0:T(8,128)(2,1)S(1)}, bf16[1024,512]{1,0:T(8,128)(2,1)}, u32[]{:S(2)}, u32[]{:S(2)}) collective-permute-start(bf16[1024,512]{1,0:T(8,128)(2,1)S(1)} %constant_dynamic-update-slice_fusion.23), channel_id=1, source_target_pairs={{0,8},{2,10},{4,12},{6,14},{8,16},{10,18},{12,20},{14,22},{16,24},... | collective-permute-start | bytes 3145736 | tf_op jit(solution)/shard_map/ppermute | solution.py:163
  184.3 26.7 %collective-permute-start.34 = (bf16[192,2048]{1,0:T(8,128)(2,1)S(1)}, bf16[192,2048]{1,0:T(8,128)(2,1)}, u32[]{:S(2)}, u32[]{:S(2)}) collective-permute-start(bf16[192,2048]{1,0:T(8,128)(2,1)S(1)} %get-tuple-element.1084), channel_id=1, source_target_pairs={{0,4},{2,6},{4,0},{6,2},{8,12},{10,14},{12,8},{14,10},{16,20},{18,... | collective-permute-start | bytes 2359304 | tf_op jit(solution)/shard_map/ppermute | solution.py:156
  199.6 34.6 %collective-permute-start.39 = (bf16[192,2048]{1,0:T(8,128)(2,1)}, bf16[192,2048]{1,0:T(8,128)(2,1)}, u32[]{:S(2)}, u32[]{:S(2)}) collective-permute-start(bf16[192,2048]{1,0:T(8,128)(2,1)} %get-tuple-element.1109), channel_id=1, source_target_pairs={{0,4},{2,6},{4,0},{6,2},{8,12},{10,14},{12,8},{14,10},{16,20},{18,... | collective-permute-start | bytes 2359304 | tf_op jit(solution)/shard_map/ppermute | solution.py:156
  200.2 34.1 %collective-permute-start.40 = (bf16[192,2048]{1,0:T(8,128)(2,1)}, bf16[192,2048]{1,0:T(8,128)(2,1)}, u32[]{:S(2)}, u32[]{:S(2)}) collective-permute-start(bf16[192,2048]{1,0:T(8,128)(2,1)} %get-tuple-element.1109), channel_id=1, source_target_pairs={{0,2},{2,0},{4,6},{6,4},{8,10},{10,8},{12,14},{14,12},{16,18},{18,... | collective-permute-start | bytes 2359304 | tf_op jit(solution)/shard_map/ppermute | solution.py:156
  206.2 25.8 %collective-permute-start.42 = (bf16[1024,512]{1,0:T(8,128)(2,1)}, bf16[1024,512]{1,0:T(8,128)(2,1)}, u32[]{:S(2)}, u32[]{:S(2)}) collective-permute-start(bf16[1024,512]{1,0:T(8,128)(2,1)} %collective-permute-done.36), channel_id=1, source_target_pairs={{0,8},{2,10},{4,12},{6,14},{8,16},{10,18},{12,20},{14,22},{16,24},... | collective-permute-start | bytes 3145736 | tf_op jit(solution)/shard_map/ppermute | solution.py:163
  211.0 23.3 %collective-permute-start.41 = (bf16[192,2048]{1,0:T(8,128)(2,1)}, bf16[192,2048]{1,0:T(8,128)(2,1)}, u32[]{:S(2)}, u32[]{:S(2)}) collective-permute-start(bf16[192,2048]{1,0:T(8,128)(2,1)} %collective-permute-done.34), channel_id=1, source_target_pairs={{0,2},{2,0},{4,6},{6,4},{8,10},{10,8},{12,14},{14,12},{16,18},{18,... | collective-permute-start | bytes 2359304 | tf_op jit(solution)/shard_map/ppermute | solution.py:156
  215.4 28.3 %collective-permute-start.45 = (bf16[192,2048]{1,0:T(8,128)(2,1)S(1)}, bf16[192,2048]{1,0:T(8,128)(2,1)S(1)}, u32[]{:S(2)}, u32[]{:S(2)}) collective-permute-start(bf16[192,2048]{1,0:T(8,128)(2,1)S(1)} %copy-done.29), channel_id=1, source_target_pairs={{0,4},{2,6},{4,0},{6,2},{8,12},{10,14},{12,8},{14,10},{16,20},{18,... | collective-permute-start | bytes 2359304 | tf_op jit(solution)/shard_map/ppermute | solution.py:156
  242.7 28.0 %collective-permute-start.47 = (bf16[1024,512]{1,0:T(8,128)(2,1)}, bf16[1024,512]{1,0:T(8,128)(2,1)S(1)}, u32[]{:S(2)}, u32[]{:S(2)}) collective-permute-start(bf16[1024,512]{1,0:T(8,128)(2,1)} %collective-permute-done.42), channel_id=1, source_target_pairs={{0,8},{2,10},{4,12},{6,14},{8,16},{10,18},{12,20},{14,22},{16,24},... | collective-permute-start | bytes 3145736 | tf_op jit(solution)/shard_map/ppermute | solution.py:163
  261.4 33.8 %collective-permute-start.50 = (bf16[1024,512]{1,0:T(8,128)(2,1)S(1)}, bf16[1024,512]{1,0:T(8,128)(2,1)S(1)}, u32[]{:S(2)}, u32[]{:S(2)}) collective-permute-start(bf16[1024,512]{1,0:T(8,128)(2,1)S(1)} %fusion.39), channel_id=1, source_target_pairs={{0,8},{2,10},{4,12},{6,14},{8,16},{10,18},{12,20},{14,22},{16,24},... | collective-permute-start | bytes 3145736 | tf_op jit(solution)/shard_map/ppermute | solution.py:163
  292.8 40.0 %collective-permute-start.59 = (bf16[192,2048]{1,0:T(8,128)(2,1)S(1)}, bf16[192,2048]{1,0:T(8,128)(2,1)S(1)}, u32[]{:S(2)}, u32[]{:S(2)}) collective-permute-start(bf16[192,2048]{1,0:T(8,128)(2,1)S(1)} %add_convert_fusion.15), channel_id=1, source_target_pairs={{0,4},{2,6},{4,0},{6,2},{8,12},{10,14},{12,8},{14,10},{16,20},{18,... | collective-permute-start | bytes 2359304 | tf_op jit(solution)/shard_map/ppermute | solution.py:156
  294.2 35.4 %collective-permute-start.60 = (bf16[512,1024]{1,0:T(8,128)(2,1)S(1)}, bf16[512,1024]{1,0:T(8,128)(2,1)S(1)}, u32[]{:S(2)}, u32[]{:S(2)}) collective-permute-start(bf16[512,1024]{1,0:T(8,128)(2,1)S(1)} %fusion.42), channel_id=1, source_target_pairs={{0,8},{2,10},{4,12},{6,14},{8,16},{10,18},{12,20},{14,22},{16,24},... | collective-permute-start | bytes 3145736 | tf_op jit(solution)/shard_map/ppermute | solution.py:163
  294.3 35.0 %collective-permute-start.61 = (bf16[192,2048]{1,0:T(8,128)(2,1)S(1)}, bf16[192,2048]{1,0:T(8,128)(2,1)S(1)}, u32[]{:S(2)}, u32[]{:S(2)}) collective-permute-start(bf16[192,2048]{1,0:T(8,128)(2,1)S(1)} %add_convert_fusion.16), channel_id=1, source_target_pairs={{0,4},{2,6},{4,0},{6,2},{8,12},{10,14},{12,8},{14,10},{16,20},{18,... | collective-permute-start | bytes 2359304 | tf_op jit(solution)/shard_map/ppermute | solution.py:156
  318.8 47.2 %collective-permute-start.76 = (bf16[1024,512]{1,0:T(8,128)(2,1)S(1)}, bf16[1024,512]{1,0:T(8,128)(2,1)S(1)}, u32[]{:S(2)}, u32[]{:S(2)}) collective-permute-start(bf16[1024,512]{1,0:T(8,128)(2,1)S(1)} %add_convert_fusion.3), channel_id=1, source_target_pairs={{0,8},{2,10},{4,12},{6,14},{8,16},{10,18},{12,20},{14,22},{16,24},... | collective-permute-start | bytes 3145736 | tf_op jit(solution)/shard_map/ppermute | solution.py:163
  342.0 39.6 %collective-permute-start.68 = (bf16[192,2048]{1,0:T(8,128)(2,1)S(1)}, bf16[192,2048]{1,0:T(8,128)(2,1)S(1)}, u32[]{:S(2)}, u32[]{:S(2)}) collective-permute-start(bf16[192,2048]{1,0:T(8,128)(2,1)S(1)} %add_convert_fusion.14), channel_id=1, source_target_pairs={{0,4},{2,6},{4,0},{6,2},{8,12},{10,14},{12,8},{14,10},{16,20},{18,... | collective-permute-start | bytes 2359304 | tf_op jit(solution)/shard_map/ppermute | solution.py:156
  346.6 35.0 %collective-permute-start.69 = (bf16[192,2048]{1,0:T(8,128)(2,1)S(1)}, bf16[192,2048]{1,0:T(8,128)(2,1)S(1)}, u32[]{:S(2)}, u32[]{:S(2)}) collective-permute-start(bf16[192,2048]{1,0:T(8,128)(2,1)S(1)} %add_convert_fusion.13), channel_id=1, source_target_pairs={{0,4},{2,6},{4,0},{6,2},{8,12},{10,14},{12,8},{14,10},{16,20},{18,... | collective-permute-start | bytes 2359304 | tf_op jit(solution)/shard_map/ppermute | solution.py:156
  347.2 32.2 %collective-permute-start.70 = (bf16[192,2048]{1,0:T(8,128)(2,1)S(1)}, bf16[192,2048]{1,0:T(8,128)(2,1)S(1)}, u32[]{:S(2)}, u32[]{:S(2)}) collective-permute-start(bf16[192,2048]{1,0:T(8,128)(2,1)S(1)} %add_convert_fusion.11), channel_id=1, source_target_pairs={{0,1},{1,0},{2,3},{3,2},{4,5},{5,4},{6,7},{7,6},{8,9},{9,8},{10,11... | collective-permute-start | bytes 2359304 | tf_op jit(solution)/shard_map/ppermute | solution.py:166
  370.7 27.8 %collective-permute-start.82 = (bf16[512,1024]{1,0:T(8,128)(2,1)S(1)}, bf16[512,1024]{1,0:T(8,128)(2,1)S(1)}, u32[]{:S(2)}, u32[]{:S(2)}) collective-permute-start(bf16[512,1024]{1,0:T(8,128)(2,1)S(1)} %add_convert_fusion.2), channel_id=1, source_target_pairs={{0,8},{2,10},{4,12},{6,14},{8,16},{10,18},{12,20},{14,22},{16,24},... | collective-permute-start | bytes 3145736 | tf_op jit(solution)/shard_map/ppermute | solution.py:163
  370.7 111.5 %collective-permute-start.79 = (bf16[1024,512]{1,0:T(8,128)(2,1)}, bf16[1024,512]{1,0:T(8,128)(2,1)}, u32[]{:S(2)}, u32[]{:S(2)}) collective-permute-start(bf16[1024,512]{1,0:T(8,128)(2,1)} %add_convert_fusion.1), channel_id=1, source_target_pairs={{0,8},{2,10},{4,12},{6,14},{8,16},{10,18},{12,20},{14,22},{16,24},... | collective-permute-start | bytes 3145736 | tf_op jit(solution)/shard_map/ppermute | solution.py:163
  429.1 23.3 %collective-permute-start.86 = (bf16[512,256]{1,0:T(8,128)(2,1)S(1)}, bf16[512,256]{1,0:T(8,128)(2,1)S(1)}, u32[]{:S(2)}, u32[]{:S(2)}) collective-permute-start(bf16[512,256]{1,0:T(8,128)(2,1)S(1)} %copy-done.60), channel_id=1, source_target_pairs={{0,4},{2,6},{4,0},{6,2},{8,12},{10,14},{12,8},{14,10},{16,20},{18,... | collective-permute-start | bytes 786440 | tf_op jit(solution)/shard_map/ppermute | solution.py:156
  435.6 50.6 %collective-permute-start.77 = (bf16[192,2048]{1,0:T(8,128)(2,1)S(1)}, bf16[192,2048]{1,0:T(8,128)(2,1)S(1)}, u32[]{:S(2)}, u32[]{:S(2)}) collective-permute-start(bf16[192,2048]{1,0:T(8,128)(2,1)S(1)} %copy-done.32), channel_id=1, source_target_pairs={{0,1},{1,0},{2,3},{3,2},{4,5},{5,4},{6,7},{7,6},{8,9},{9,8},{10,11... | collective-permute-start | bytes 2359304 | tf_op jit(solution)/shard_map/ppermute | solution.py:166
  441.2 31.3 %collective-permute-start.88 = (bf16[256,1536]{1,0:T(8,128)(2,1)S(1)}, bf16[256,1536]{1,0:T(8,128)(2,1)S(1)}, u32[]{:S(2)}, u32[]{:S(2)}) collective-permute-start(bf16[256,1536]{1,0:T(8,128)(2,1)S(1)} %dynamic-slice_convert_fusion.3), channel_id=1, source_target_pairs={{0,4},{2,6},{4,0},{6,2},{8,12},{10,14},{12,8},{14,10},{16,20},{18,... | collective-permute-start | bytes 2359304 | tf_op jit(solution)/shard_map/ppermute | solution.py:156
  482.1 22.3 %collective-permute-start.94 = (bf16[256,1536]{1,0:T(8,128)(2,1)S(1)}, bf16[256,1536]{1,0:T(8,128)(2,1)S(1)}, u32[]{:S(2)}, u32[]{:S(2)}) collective-permute-start(bf16[256,1536]{1,0:T(8,128)(2,1)S(1)} %add_convert_fusion.6), channel_id=1, source_target_pairs={{0,8},{2,10},{4,12},{6,14},{8,16},{10,18},{12,20},{14,22},{16,24},... | collective-permute-start | bytes 2359304 | tf_op jit(solution)/shard_map/ppermute | solution.py:163
  482.2 48.0 %collective-permute-start.98 = (bf16[512,1024]{1,0:T(8,128)(2,1)S(1)}, bf16[512,1024]{1,0:T(8,128)(2,1)S(1)}, u32[]{:S(2)}, u32[]{:S(2)}) collective-permute-start(bf16[512,1024]{1,0:T(8,128)(2,1)S(1)} %copy-done.73), channel_id=1, source_target_pairs={{0,8},{2,10},{4,12},{6,14},{8,16},{10,18},{12,20},{14,22},{16,24},... | collective-permute-start | bytes 3145736 | tf_op jit(solution)/shard_map/ppermute | solution.py:163
  490.6 32.9 %collective-permute-start.96 = (bf16[192,2048]{1,0:T(8,128)(2,1)S(1)}, bf16[192,2048]{1,0:T(8,128)(2,1)S(1)}, u32[]{:S(2)}, u32[]{:S(2)}) collective-permute-start(bf16[192,2048]{1,0:T(8,128)(2,1)S(1)} %add_convert_fusion.7), channel_id=1, source_target_pairs={{0,1},{1,0},{2,3},{3,2},{4,5},{5,4},{6,7},{7,6},{8,9},{9,8},{10,11... | collective-permute-start | bytes 2359304 | tf_op jit(solution)/shard_map/ppermute | solution.py:166
  492.1 41.6 %collective-permute-start.97 = (bf16[256,1536]{1,0:T(8,128)(2,1)S(1)}, bf16[256,1536]{1,0:T(8,128)(2,1)S(1)}, u32[]{:S(2)}, u32[]{:S(2)}) collective-permute-start(bf16[256,1536]{1,0:T(8,128)(2,1)S(1)} %dynamic-slice_convert_fusion.1), channel_id=1, source_target_pairs={{0,4},{2,6},{4,0},{6,2},{8,12},{10,14},{12,8},{14,10},{16,20},{18,... | collective-permute-start | bytes 2359304 | tf_op jit(solution)/shard_map/ppermute | solution.py:156
  504.4 25.7 %collective-permute-start.99 = (bf16[512,256]{1,0:T(8,128)(2,1)S(1)}, bf16[512,256]{1,0:T(8,128)(2,1)S(1)}, u32[]{:S(2)}, u32[]{:S(2)}) collective-permute-start(bf16[512,256]{1,0:T(8,128)(2,1)S(1)} %add_convert_fusion.20), channel_id=1, source_target_pairs={{0,8},{2,10},{4,12},{6,14},{8,16},{10,18},{12,20},{14,22},{16,24},... | collective-permute-start | bytes 786440 | tf_op jit(solution)/shard_map/ppermute | solution.py:163
  507.5 49.3 %collective-permute-start.106 = (bf16[1024,128]{1,0:T(8,128)(2,1)S(1)}, bf16[1024,128]{1,0:T(8,128)(2,1)S(1)}, u32[]{:S(2)}, u32[]{:S(2)}) collective-permute-start(bf16[1024,128]{1,0:T(8,128)(2,1)S(1)} %get-tuple-element.1586), channel_id=1, source_target_pairs={{0,2},{2,0},{4,6},{6,4},{8,10},{10,8},{12,14},{14,12},{16,18},{18,... | collective-permute-start | bytes 786440 | tf_op jit(solution)/shard_map/ppermute | solution.py:156
  523.5 33.2 %collective-permute-start.107 = (bf16[1024,128]{1,0:T(8,128)(2,1)S(1)}, bf16[1024,128]{1,0:T(8,128)(2,1)S(1)}, u32[]{:S(2)}, u32[]{:S(2)}) collective-permute-start(bf16[1024,128]{1,0:T(8,128)(2,1)S(1)} %get-tuple-element.1588), channel_id=1, source_target_pairs={{0,4},{2,6},{4,0},{6,2},{8,12},{10,14},{12,8},{14,10},{16,20},{18,... | collective-permute-start | bytes 786440 | tf_op jit(solution)/shard_map/ppermute | solution.py:156
  530.2 28.1 %collective-permute-start.108 = (bf16[1024,128]{1,0:T(8,128)(2,1)S(1)}, bf16[1024,128]{1,0:T(8,128)(2,1)S(1)}, u32[]{:S(2)}, u32[]{:S(2)}) collective-permute-start(bf16[1024,128]{1,0:T(8,128)(2,1)S(1)} %get-tuple-element.1590), channel_id=1, source_target_pairs={{0,6},{2,4},{4,2},{6,0},{8,14},{10,12},{12,10},{14,8},{16,22},{18,... | collective-permute-start | bytes 786440 | tf_op jit(solution)/shard_map/ppermute | solution.py:156
  533.7 39.1 %collective-permute-start.101 = (bf16[256,1536]{1,0:T(8,128)(2,1)S(1)}, bf16[256,1536]{1,0:T(8,128)(2,1)S(1)}, u32[]{:S(2)}, u32[]{:S(2)}) collective-permute-start(bf16[256,1536]{1,0:T(8,128)(2,1)S(1)} %dynamic-slice_convert_fusion), channel_id=1, source_target_pairs={{0,4},{2,6},{4,0},{6,2},{8,12},{10,14},{12,8},{14,10},{16,20},{18,... | collective-permute-start | bytes 2359304 | tf_op jit(solution)/shard_map/ppermute | solution.py:156
  549.1 23.6 %collective-permute-start.102 = (bf16[512,256]{1,0:T(8,128)(2,1)S(1)}, bf16[512,256]{1,0:T(8,128)(2,1)S(1)}, u32[]{:S(2)}, u32[]{:S(2)}) collective-permute-start(bf16[512,256]{1,0:T(8,128)(2,1)S(1)} %add_convert_fusion.19), channel_id=1, source_target_pairs={{0,8},{2,10},{4,12},{6,14},{8,16},{10,18},{12,20},{14,22},{16,24},... | collective-permute-start | bytes 786440 | tf_op jit(solution)/shard_map/ppermute | solution.py:163
  570.6 21.8 %collective-permute-start.109 = (bf16[256,1536]{1,0:T(8,128)(2,1)S(1)}, bf16[256,1536]{1,0:T(8,128)(2,1)S(1)}, u32[]{:S(2)}, u32[]{:S(2)}) collective-permute-start(bf16[256,1536]{1,0:T(8,128)(2,1)S(1)} %add_convert_fusion.4), channel_id=1, source_target_pairs={{0,8},{2,10},{4,12},{6,14},{8,16},{10,18},{12,20},{14,22},{16,24},... | collective-permute-start | bytes 2359304 | tf_op jit(solution)/shard_map/ppermute | solution.py:163
  (144 other events, 1492.3 us)

commit v4 on v3

--- a/solution.py
+++ b/solution.py
@@ -522,63 +522,48 @@
 
     last_n = [links.to_core(v) for v in run(low_part_of(outer, 3), grad_pre, up_full)]
     far_n = run(part_of(outer, 2), grad_pre, up_full)
-    far_n = [
-        swap(run(add_pieces_low, far_n[j], *wait(*last_n[j])), 2) for j in range(2)
-    ]
+    far_a = run(add_pieces_low, far_n[0], *wait(*last_n[0]))
+    far_b = run(add_pieces_low, far_n[1], *wait(*last_n[1]))
+    far_a = swap(far_a, 2)
     up_sum = ring_up(1)
     down_arrived = wait(down_sum)
     down_sum = ring_down(2, down_arrived)
+    far_n = [far_a, swap(far_b, 2)]
     core_n = [links.to_core(v) for v in run(low_part_of(outer, 1), grad_pre, up_full)]
     own_n = run(part_of(outer, 0), grad_pre, up_full)
     near_n = [run(add_pieces, own_n[j], *wait(*core_n[j])) for j in range(2)]
-    last_r = [links.to_core(v) for v in run(low_part_of(plain, 3), act_low, down_full)]
-    far_r = run(part_of(plain, 2), act_low, down_full)
-    far_r = [run(add_pieces_low, far_r[j], *wait(*last_r[j])) for j in range(2)]
-    low_n, cross_n = [], []
-    far_n[0] = wait(far_n[0])
-    low_n.append(run(near_sum, near_n[0], far_n[0]))
-    cross_n.append(across(low_n[0]))
-    up_arrived = wait(up_sum)
-    up_sum = ring_up(2, up_arrived)
-    far_n[1] = wait(far_n[1])
-    low_n.append(run(near_sum, near_n[1], far_n[1]))
-    cross_n.append(across(low_n[1]))
-    far_r = [swap(part, 2) for part in far_r]
-    core_r = [links.to_core(v) for v in run(low_part_of(plain, 1), act_low, down_full)]
-    own_r = run(part_of(plain, 0), act_low, down_full)
-    near_r = [run(add_pieces, own_r[j], *wait(*core_r[j])) for j in range(2)]
-    grad_hidden, grad_low = [], jnp.zeros((2 * rows, width), LOW)
-    low_r, cross_r = [], []
-    for j in range(2):
-        cross_n[j] = wait(cross_n[j])
-
-        def second_back(d_out, low, cross, standard, inverse):
-            scaled = wide(low) + wide(cross)
-            grad_hidden = wide(d_out) + norm_backward(scaled, standard, inverse)
-            return grad_hidden, grad_hidden.astype(LOW)
-
+    def second_back(d_out, low, cross, standard, inverse):
+        scaled = wide(low) + wide(cross)
+        grad_hidden = wide(d_out) + norm_backward(scaled, standard, inverse)
+        return grad_hidden, grad_hidden.astype(LOW)
+
+    def back_chunk(j):
         grad, low = run(
             second_back, d_out_chunks[j], low_n[j], cross_n[j], seconds[j][1], seconds[j][2]
         )
-        other = links.to_core(low)
-        grad_hidden.append(grad)
-        if j == 0 and ring > 2:
-            down_arrived = wait(down_sum)
-            down_sum = ring_down(3, down_arrived)
-        if j == 1:
-            far_r = wait(*far_r)
-            for i in range(2):
-                low_r.append(run(near_sum, near_r[i], far_r[i]))
-                cross_r.append(across(low_r[i]))
-        grad_low = run(
-            lambda w, a, *p: put_tokens(put_tokens(w, 0, a, j), 1, jnp.concatenate(p), j),
-            grad_low,
-            low,
-            *wait(*other),
-        )
-    if ring > 2:
-        up_arrived = wait(up_sum)
-        up_sum = ring_up(3, up_arrived)
+        return grad, low, links.to_core(low)
+
+    low_n, cross_n = [], []
+    for j in range(2):
+        low_n.append(run(near_sum, near_n[j], wait(far_n[j])))
+        cross_n.append(across(low_n[j]))
+    cross_n[0] = wait(cross_n[0])
+    backs = [back_chunk(0)]
+    up_arrived = wait(up_sum)
+    up_sum = ring_up(2, up_arrived)
+    last_r = [links.to_core(v) for v in run(low_part_of(plain, 3), act_low, down_full)]
+    core_r = [links.to_core(v) for v in run(low_part_of(plain, 1), act_low, down_full)]
+    far_r = run(part_of(plain, 2), act_low, down_full)
+    own_r = run(part_of(plain, 0), act_low, down_full)
+    far_r = [swap(run(add_pieces_low, far_r[j], *wait(*last_r[j])), 2) for j in range(2)]
+    near_r = [run(add_pieces, own_r[j], *wait(*core_r[j])) for j in range(2)]
+    cross_n[1] = wait(cross_n[1])
+    backs.append(back_chunk(1))
+    grad_hidden = [backs[0][0], backs[1][0]]
+    down_arrived = wait(down_sum)
+    down_sum = ring_down(3, down_arrived)
+    pieces = wait(*backs[0][2], *backs[1][2])
+    grad_low = run(lambda *p: jnp.concatenate(p, axis=0), backs[0][1], backs[1][1], *pieces)
 
     def part_qkv(normed, grad, k):
         part = inner(take(normed, links.behind(k), block, 1), grad)
@@ -594,6 +579,8 @@
         out_owns.append(own)
         out_fars.append(swap(far, 2))
 
+    up_arrived = wait(up_sum)
+    up_sum = ring_up(3, up_arrived)
     grad_att = run(lambda g, w: outer(g, w).astype(LOW), grad_low, out_full)
     grad_qkv = run(
         lambda q, d, f, g: jnp.concatenate(attention_call(attention_backward, q, d, f, g), axis=1),
@@ -617,10 +604,6 @@
         parts += [take(total, links.cell ^ k, size, axis).astype(LOW) for k in (1, 2, 3)]
         return tuple(parts)
 
-    def send_ends(total, axis):
-        own, *parts = run(lambda t: cut(t, axis, owned), total)
-        return [own] + [swap(part, k) for k, part in zip((1, 2, 3), parts)]
-
     def up_end(gain, weight, *parts):
         raw = links.join([wide(part) for part in parts], 1)
         return raw * gain[:, None], jnp.sum(wide(weight) * raw, axis=1)
@@ -634,47 +617,45 @@
     for k in range(1, ring + 1):
         own, far = run(lambda n, g: part_qkv(n, g, k), normed_one, grad_qkv)
         qkv_owns.append(own)
-        qkv_fars.append(swap(far, 2) if k < 3 else far)
-        if k == 2:
-            out_fars = wait(*out_fars)
-            out_next = step(run(add_low, out_owns[0], out_fars[0]))
+        qkv_fars.append(swap(far, 2) if k == 1 else far)
+    *out_fars, far_r[0], far_r[1] = wait(*out_fars, *far_r)
+    low_r = [run(near_sum, near_r[j], far_r[j]) for j in range(2)]
+    cross_r = [across(part) for part in low_r]
     core_m = [links.to_core(v) for v in run(low_part_of(outer, 1), grad_qkv, qkv_full)]
     own_m = run(part_of(outer, 0), grad_qkv, qkv_full)
     low_m = [run(add_pieces_low, own_m[j], *wait(*core_m[j])) for j in range(2)]
-    cross_m = [across(part) for part in low_m]
-    qkv_far = wait(qkv_fars[0])
-    qkv_next = step(run(add_low, qkv_owns[0], qkv_far))
-    if ring > 2:
-        qkv_fars[2] = swap(qkv_fars[2], 2)
+    down_arrived = wait(down_sum)
+    for k in range(4, ring + 1):
+        down_sum = ring_down(k, down_arrived)
+        if k < ring:
+            down_arrived = wait(down_sum)
+    down_ends = list(run(lambda t: cut(t, 1, owned), down_sum))
+    down_ends[1], down_ends[2] = swap(down_ends[1], 1), swap(down_ends[2], 2)
+    up_arrived = wait(up_sum)
+    for k in range(4, ring + 1):
+        up_sum = ring_up(k, up_arrived)
+        if k < ring:
+            up_arrived = wait(up_sum)
+    up_ends = list(run(lambda t: cut(t, 0, owned), up_sum))
+
+    qkv_fars[0], down_ends[1], down_ends[2], cross_r[0] = wait(
+        qkv_fars[0], down_ends[1], down_ends[2], cross_r[0]
+    )
+    qkv_sum, out_sum = run(
+        lambda a, b, c, d: (add_low(a, b), add_low(c, d)),
+        qkv_owns[0],
+        qkv_fars[0],
+        out_owns[0],
+        out_fars[0],
+    )
     for k in range(2, ring + 1):
-        add = add_low if k < ring else add_row
-        out_arrived = wait(out_next)
-        out_sum = run(add, out_owns[k - 1], out_fars[k - 1], out_arrived)
-        if k < ring:
-            out_next = step(out_sum)
+        sent = [step(qkv_sum), step(out_sum), swap(qkv_fars[k - 1], 2)]
         if k == 2:
-            down_arrived = wait(down_sum)
-            for i in range(4, ring + 1) if ring > 2 else (2,):
-                down_sum = ring_down(i, down_arrived)
-                if i < ring:
-                    down_arrived = wait(down_sum)
-            down_ends = send_ends(down_sum, 1)
-            cross_r = wait(*cross_r)
-        if k == min(3, ring):
-            up_arrived = wait(up_sum)
-            for i in range(4, ring + 1) if ring > 2 else (2,):
-                up_sum = ring_up(i, up_arrived)
-                if i < ring:
-                    up_arrived = wait(up_sum)
-            up_ends = send_ends(up_sum, 0)
-        qkv_far = wait(qkv_fars[k - 1])
-        qkv_arrived = wait(qkv_next)
-        qkv_sum = run(add, qkv_owns[k - 1], qkv_far, qkv_arrived)
-        if k < ring:
-            qkv_next = step(qkv_sum)
-        if k + 1 < ring:
-            qkv_fars[k + 1] = swap(qkv_fars[k + 1], 2)
-        if k == 2:
+            down_ends[3] = swap(down_ends[3], 3)
+            cross_m = [across(part) for part in low_m]
+            *sent, down_ends[3], cross_r[1] = wait(*sent, down_ends[3], cross_r[1])
+        elif k == 3:
+            up_ends[1], up_ends[2] = swap(up_ends[1], 1), swap(up_ends[2], 2)
             result = run(
                 lambda *p: jnp.concatenate(p[:2])
                 + (wide(jnp.concatenate(p[2:4])) + wide(jnp.concatenate(p[4:]))),
@@ -683,8 +664,12 @@
                 *low_r,
                 *cross_r,
             )
-            cross_m = wait(*cross_m)
-        if k == min(3, ring):
+            d_w_down = run(lambda *p: links.join([wide(part) for part in p], 0), *down_ends)
+            *sent, up_ends[1], up_ends[2], cross_m[0], cross_m[1] = wait(
+                *sent, up_ends[1], up_ends[2], *cross_m
+            )
+        elif k == 4:
+            up_ends[3] = swap(up_ends[3], 3)
             d_tokens = run(
                 lambda t, *p: first_back(t, p[:2], p[2:4], p[4:]),
                 tokens,
@@ -692,11 +677,19 @@
                 *low_m,
                 *cross_m,
             )
-            down_ends = wait(*down_ends)
-            d_w_down = run(lambda *p: links.join([wide(part) for part in p], 0), *down_ends)
-            up_ends = wait(*up_ends)
-            d_w_up, gain_mlp_own = run(up_end, gain_mlp, w_up, *up_ends)
-            gain_mlp_other = across(gain_mlp_own)
+            *sent, up_ends[3] = wait(*sent, up_ends[3])
+        else:
+            sent = wait(*sent)
+        add = add_low if k < ring else add_row
+        qkv_sum, out_sum = run(
+            lambda *p: (add(*p[:3]), add(*p[3:])),
+            qkv_owns[k - 1],
+            sent[2],
+            sent[0],
+            out_owns[k - 1],
+            out_fars[k - 1],
+            sent[1],
+        )
 
     def ends(qkv, out):
         return (
@@ -708,6 +701,8 @@
 
     qkv_mine, qkv_yours, out_mine, out_yours = run(ends, qkv_sum, out_sum)
     qkv_yours, out_yours = swap(qkv_yours, 1), swap(out_yours, 1)
+    d_w_up, gain_mlp_own = run(up_end, gain_mlp, w_up, *up_ends)
+    gain_mlp_other = across(gain_mlp_own)
     qkv_yours, out_yours = wait(qkv_yours, out_yours)
     d_w_output = links.by_core(out_mine, wide(out_yours), 0)
     raw = [
@@ -717,7 +712,8 @@
     gain_attn_own = sum(
         jnp.sum(wide(weight) * part, axis=1) for weight, part in zip((w_query, w_key, w_value), raw)
     )
-    d_gain_attn = gain_attn_own + across(gain_attn_own)
+    gain_attn_other = across(gain_attn_own)
+    d_gain_attn = gain_attn_own + gain_attn_other
     d_gain_mlp = gain_mlp_own + gain_mlp_other
     d_w_query, d_w_key, d_w_value = (part * gain_attn[:, None] for part in raw)
     return (

time: 612 us -> 586 us (0.958)
  waiting for transfers between devices: 294 us -> 253 us
  other arithmetic: 40.9 us -> 63.8 us
  local copies, waits for them, and re-layouts: 91.4 us -> 80 us
    ppermute x10, waiting for transfers between devices: 56.2 us -> 26 us  [across(): return lax.ppermute(self.order.tie(values), 'mp', [(0, 1), (1, 0)])]
    ppermute x80, waiting for transfers between devices: 80.2 us -> 61.9 us  [swap(): return lax.ppermute(self.order.tie(values), 'dp', self.to[k])]
    dynamic_update_slice x14 -> x12, local copies, waits for them, and re-layouts: 19.7 us -> 3.47 us  [put_tokens(): return lax.dynamic_update_slice_in_dim(whole, part, at, 0)]
    dot_general x8, matrix products: 30.4 us -> 39.7 us  [outer(): lax.dot_general(one, two, (((1,), (1,)), ((), ())), preferred_element_typ...]
    dot_general x8, matrix products: 36.5 us -> 29.3 us  [plain(): return jnp.dot(one, two, preferred_element_type=WIDE)]
    ppermute x24, waiting for transfers between devices: 158 us -> 165 us  [step(): return lax.ppermute(self.order.tie(values), 'dp', self.next)]
    unnamed x157 -> x192, local copies, waits for them, and re-layouts: 15.2 us -> 11.8 us
  transfers between devices with their start and end apart: 114 -> 114, of which waited for: 54 -> 47; matrix products, arithmetic and copies ran while one was open for 36% -> 39% of each run, Pallas kernels for 2% -> 2%
where the time goes in v4:
time: 586 us; the launch traced here: 579 us
  waiting for transfers between devices  253 us (43%)
  matrix products  104 us (18%)
  local copies, waits for them, and re-layouts  80 us (14%)
  other arithmetic  63.8 us (11%)
  starting transfers between devices  63.1 us (11%)
  Pallas kernels  11.4 us (2%)
    ppermute x24, waiting for transfers between devices, step(): return lax.ppermute(self.order.tie(values), 'dp', self.next)  165 us
    ppermute x80, waiting for transfers between devices, swap(): return lax.ppermute(self.order.tie(values), 'dp', self.to[k])  61.9 us
    ppermute x80, starting transfers between devices, swap(): return lax.ppermute(self.order.tie(values), 'dp', self.to[k])  43.5 us
    dot_general x8, matrix products, outer(): lax.dot_general(one, two, (((1,), (1,)), ((), ())), preferred_element_typ...  39.7 us
    dot_general x16, matrix products, inner(): lax.dot_general(one, two, (((0,), (0,)), ((), ())), preferred_element_typ...  35.2 us
    dynamic_update_slice x34, local copies, waits for them, and re-layouts, put(): lax.dynamic_update_slice_in_dim(whole, part, index * part.shape[axis], axis)  30.9 us
    dot_general x8, matrix products, plain(): return jnp.dot(one, two, preferred_element_type=WIDE)  29.3 us
    ppermute x10, waiting for transfers between devices, across(): return lax.ppermute(self.order.tie(values), 'mp', [(0, 1), (1, 0)])  26 us
  transfers between devices with their start and end apart: 114, of which 47 were waited for; matrix products, arithmetic and copies ran while one was open for 39% of the time, Pallas kernels for 2%

profile of v4, /device:TPU:0, one launch (start us, length us, event | category | flops | bytes accessed | tf_op | source)
XLA Modules:
  0.0 579.2 jit_solution(8881674210774723059)
XLA Ops:
  8.0 3.1 collective-permute-start.5
  17.5 3.0 broadcast_in_dim.32
  22.9 13.6 %collective-permute-done.6 = bf16[512,256]{1,0:T(8,128)(2,1)} collective-permute-done((bf16[512,256]{1,0:T(8,128)(2,1)S(1)}, bf16[512,256]{1,0:T(8,128)(2,1)}, u32[]{:S(2)}, u32[]{:S(2)}) %collective-permute-start.6) | collective-permute-done | bytes 262176 | tf_op jit(solution)/shard_map/ppermute | solution.py:163
  47.1 17.1 %collective-permute-done.11 = bf16[512,256]{1,0:T(8,128)(2,1)} collective-permute-done((bf16[512,256]{1,0:T(8,128)(2,1)}, bf16[512,256]{1,0:T(8,128)(2,1)}, u32[]{:S(2)}, u32[]{:S(2)}) %collective-permute-start.11) | collective-permute-done | bytes 262176 | tf_op jit(solution)/shard_map/ppermute | solution.py:163
  71.9 18.1 %collective-permute-done.15 = bf16[512,256]{1,0:T(8,128)(2,1)} collective-permute-done((bf16[512,256]{1,0:T(8,128)(2,1)}, bf16[512,256]{1,0:T(8,128)(2,1)}, u32[]{:S(2)}, u32[]{:S(2)}) %collective-permute-start.15) | collective-permute-done | bytes 262176 | tf_op jit(solution)/shard_map/ppermute | solution.py:163
  96.1 2.9 broadcast_in_dim.35
  100.0 15.7 %collective-permute-done.20 = bf16[1024,128]{1,0:T(8,128)(2,1)S(1)} collective-permute-done((bf16[1024,128]{1,0:T(8,128)(2,1)S(1)}, bf16[1024,128]{1,0:T(8,128)(2,1)S(1)}, u32[]{:S(2)}, u32[]{:S(2)}) %collective-permute-start.20) | collective-permute-done | bytes 262176 | tf_op jit(solution)/shard_map/ppermute | solution.py:156
  122.5 8.0 %convolution_convert_fusion.query.key.value = bf16[768,1536]{1,0:T(8,128)(2,1)S(1)} fusion(bf16[768,2048]{1,0:T(8,128)(2,1)S(1)} %pad_maximum_fusion, bf16[2048,1536]{1,0:T(8,128)(2,1)} %constant_dynamic-update-slice_fusion.28), kind=kOutput, calls=%fused_computation.19 | convolution fusion | flops 4833017856 | bytes 11796480 | tf_op jit(solution)/shard_map/dot_general | solution.py:20
  132.7 4.4 shard_map.195
  138.9 5.6 collective-permute-done.26
  171.9 8.3 %collective-permute-done.32 = bf16[512,1024]{1,0:T(8,128)(2,1)} collective-permute-done((bf16[512,1024]{1,0:T(8,128)(2,1)}, bf16[512,1024]{1,0:T(8,128)(2,1)}, u32[]{:S(2)}, u32[]{:S(2)}) %collective-permute-start.32) | collective-permute-done | bytes 1048608 | tf_op jit(solution)/shard_map/ppermute | solution.py:163
  188.1 3.1 collective-permute-done.33
  195.6 13.2 %collective-permute-done.36 = bf16[1024,512]{1,0:T(8,128)(2,1)S(1)} collective-permute-done((bf16[1024,512]{1,0:T(8,128)(2,1)}, bf16[1024,512]{1,0:T(8,128)(2,1)S(1)}, u32[]{:S(2)}, u32[]{:S(2)}) %collective-permute-start.36) | collective-permute-done | bytes 1048608 | tf_op jit(solution)/shard_map/ppermute | solution.py:163
  213.6 20.7 %collective-permute-done.42 = bf16[1024,512]{1,0:T(8,128)(2,1)S(1)} collective-permute-done((bf16[1024,512]{1,0:T(8,128)(2,1)S(1)}, bf16[1024,512]{1,0:T(8,128)(2,1)S(1)}, u32[]{:S(2)}, u32[]{:S(2)}) %collective-permute-start.42) | collective-permute-done | bytes 1048608 | tf_op jit(solution)/shard_map/ppermute | solution.py:163
  239.9 12.0 %fusion.4 = (bf16[1536,1024]{1,0:T(8,128)(2,1)}, bf16[1536,1024]{1,0:T(8,128)(2,1)S(1)}) fusion(bf16[1536,2048]{1,0:T(8,128)(2,1)S(1)} %maximum_dynamic-update-slice_fusion, bf16[2048,1024]{1,0:T(8,128)(2,1)} %constant_dynamic-update-slice_fusion.16), kind=kOutput, calls=%fused_computation.5 | convolution fusion | flops 6459752448 | bytes 16777216 | tf_op jit(solution)/shard_map/dot_general | solution.py:20
  253.6 3.0 fusion.39
  256.6 6.6 %collective-permute-done.47 = bf16[1024,512]{1,0:T(8,128)(2,1)S(1)} collective-permute-done((bf16[1024,512]{1,0:T(8,128)(2,1)S(1)}, bf16[1024,512]{1,0:T(8,128)(2,1)S(1)}, u32[]{:S(2)}, u32[]{:S(2)}) %collective-permute-start.47) | collective-permute-done | bytes 1048608 | tf_op jit(solution)/shard_map/ppermute | solution.py:163
  263.4 10.3 %multiply_convert_fusion = bf16[1536,1024]{1,0:T(8,128)(2,1)} fusion(bf16[1536,1024]{1,0:T(8,128)(2,1)} %get-tuple-element.1150, bf16[1536,2048]{1,0:T(8,128)(2,1)S(1)} %maximum_dynamic-update-slice_fusion.1, bf16[1024,2048]{1,0:T(8,128)(2,1)S(1)} %constant_dynamic-update-slice_fusion.2), kind=kOutput, calls=%fused_computation.6 | convolution fusion | flops 6447169536 | bytes 16777216 | tf_op jit(solution)/shard_map/dot_general | solution.py:28
  273.7 4.3 convolution_convert_fusion.4
  279.9 4.0 fusion.83
  288.8 2.8 fusion.42
  292.9 2.8 add_convert_fusion.3
  295.7 4.0 convolution_convert_fusion.3
  299.9 4.0 fusion.80
  309.0 2.9 collective-permute-done.58
  314.7 13.4 %collective-permute-done.62 = bf16[192,2048]{1,0:T(8,128)(2,1)} collective-permute-done((bf16[192,2048]{1,0:T(8,128)(2,1)}, bf16[192,2048]{1,0:T(8,128)(2,1)}, u32[]{:S(2)}, u32[]{:S(2)}) %collective-permute-start.62) | collective-permute-done | bytes 786464 | tf_op jit(solution)/shard_map/ppermute | solution.py:156
  333.2 3.4 fusion.109
  336.6 5.7 collective-permute-done.54
  342.4 3.2 add_convert_fusion.2
  367.2 4.3 add_convert_fusion.1
  384.6 4.7 collective-permute-done.83
  390.8 4.3 add_convert_fusion
  399.4 7.0 %shard_map.196 = (bf16[768,512]{1,0:T(8,128)(2,1)S(1)}, bf16[768,512]{1,0:T(8,128)(2,1)S(1)}, bf16[768,512]{1,0:T(8,128)(2,1)S(1)}) custom-call(bf16[768,1536]{1,0:T(8,128)(2,1)S(1)} %convolution_convert_fusion.query.key.value, bf16[768,1536]{1,0:T(8,128)(2,1)S(1)} %convolution_convert_fusion.query.key.value, ...), custom_call_target="tpu_custom_call" | custom-call | tf_op jit(solution)/shard_map/pallas_call | solution.py:103
  420.4 5.4 collective-permute-done.79
  427.3 4.1 collective-permute-done.80
  435.4 5.4 convolution_convert_fusion.5
  441.0 5.0 fusion.55
  452.1 3.4 convert_add_fusion.2
  457.2 11.2 %collective-permute-done.93 = bf16[512,1024]{1,0:T(8,128)(2,1)S(1)} collective-permute-done((bf16[512,1024]{1,0:T(8,128)(2,1)S(1)}, bf16[512,1024]{1,0:T(8,128)(2,1)S(1)}, u32[]{:S(2)}, u32[]{:S(2)}) %collective-permute-start.93) | collective-permute-done | bytes 1048608 | tf_op jit(solution)/shard_map/ppermute | solution.py:163
  470.0 3.2 convert_add_fusion.1
  479.6 6.8 %collective-permute-done.98 = bf16[192,2048]{1,0:T(8,128)(2,1)} collective-permute-done((bf16[192,2048]{1,0:T(8,128)(2,1)}, bf16[192,2048]{1,0:T(8,128)(2,1)}, u32[]{:S(2)}, u32[]{:S(2)}) %collective-permute-start.98) | collective-permute-done | bytes 786464 | tf_op jit(solution)/shard_map/ppermute | solution.py:166
  487.1 15.7 %collective-permute-done.95 = bf16[512,256]{1,0:T(8,128)(2,1)} collective-permute-done((bf16[512,256]{1,0:T(8,128)(2,1)}, bf16[512,256]{1,0:T(8,128)(2,1)}, u32[]{:S(2)}, u32[]{:S(2)}) %collective-permute-start.95) | collective-permute-done | bytes 262176 | tf_op jit(solution)/shard_map/ppermute | solution.py:163
  506.9 3.9 maximum_add_fusion
  512.1 9.9 %collective-permute-done.105 = bf16[192,2048]{1,0:T(8,128)(2,1)S(1)} collective-permute-done((bf16[192,2048]{1,0:T(8,128)(2,1)S(1)}, bf16[192,2048]{1,0:T(8,128)(2,1)S(1)}, u32[]{:S(2)}, u32[]{:S(2)}) %collective-permute-start.105) | collective-permute-done | bytes 786464 | tf_op jit(solution)/shard_map/ppermute | solution.py:166
  524.6 10.9 %collective-permute-done.100 = bf16[512,256]{1,0:T(8,128)(2,1)S(1)} collective-permute-done((bf16[512,256]{1,0:T(8,128)(2,1)S(1)}, bf16[512,256]{1,0:T(8,128)(2,1)S(1)}, u32[]{:S(2)}, u32[]{:S(2)}) %collective-permute-start.100) | collective-permute-done | bytes 262176 | tf_op jit(solution)/shard_map/ppermute | solution.py:163
  541.4 4.8 fusion.14
  546.2 16.4 %collective-permute-done.107 = bf16[512,256]{1,0:T(8,128)(2,1)S(1)} collective-permute-done((bf16[512,256]{1,0:T(8,128)(2,1)S(1)}, bf16[512,256]{1,0:T(8,128)(2,1)S(1)}, u32[]{:S(2)}, u32[]{:S(2)}) %collective-permute-start.107) | collective-permute-done | bytes 262176 | tf_op jit(solution)/shard_map/ppermute | solution.py:163
  567.8 3.4 collective-permute-done.113
  (613 shorter events, 226.2 us)
Async XLA Ops:
  8.0 28.6 %collective-permute-start.5 = (bf16[256,1536]{1,0:T(8,128)(2,1)S(1)}, bf16[256,1536]{1,0:T(8,128)(2,1)}, u32[]{:S(2)}, u32[]{:S(2)}) collective-permute-start(bf16[256,1536]{1,0:T(8,128)(2,1)S(1)} %maximum_select_fusion), channel_id=1, source_target_pairs={{0,8},{2,10},{4,12},{6,14},{8,16},{10,18},{12,20},{14,22},{16,24},... | collective-permute-start | bytes 2359304 | tf_op jit(solution)/shard_map/ppermute | solution.py:163
  11.1 25.5 %collective-permute-start.7 = (bf16[256,1536]{1,0:T(8,128)(2,1)S(1)}, bf16[256,1536]{1,0:T(8,128)(2,1)S(1)}, u32[]{:S(2)}, u32[]{:S(2)}) collective-permute-start(bf16[256,1536]{1,0:T(8,128)(2,1)S(1)} %maximum_select_fusion), channel_id=1, source_target_pairs={{0,4},{2,6},{4,0},{6,2},{8,12},{10,14},{12,8},{14,10},{16,20},{18,... | collective-permute-start | bytes 2359304 | tf_op jit(solution)/shard_map/ppermute | solution.py:156
  37.5 26.7 %collective-permute-start.10 = (bf16[256,1536]{1,0:T(8,128)(2,1)}, bf16[256,1536]{1,0:T(8,128)(2,1)}, u32[]{:S(2)}, u32[]{:S(2)}) collective-permute-start(bf16[256,1536]{1,0:T(8,128)(2,1)} %collective-permute-done.5), channel_id=1, source_target_pairs={{0,8},{2,10},{4,12},{6,14},{8,16},{10,18},{12,20},{14,22},{16,24},... | collective-permute-start | bytes 2359304 | tf_op jit(solution)/shard_map/ppermute | solution.py:163
  38.4 25.8 %collective-permute-start.12 = (bf16[256,1536]{1,0:T(8,128)(2,1)}, bf16[256,1536]{1,0:T(8,128)(2,1)}, u32[]{:S(2)}, u32[]{:S(2)}) collective-permute-start(bf16[256,1536]{1,0:T(8,128)(2,1)} %collective-permute-done.5), channel_id=1, source_target_pairs={{0,4},{2,6},{4,0},{6,2},{8,12},{10,14},{12,8},{14,10},{16,20},{18,... | collective-permute-start | bytes 2359304 | tf_op jit(solution)/shard_map/ppermute | solution.py:156
  41.2 53.6 %collective-permute-start.2 = (bf16[384,2048]{1,0:T(8,128)(2,1)}, bf16[384,2048]{1,0:T(8,128)(2,1)S(1)}, u32[]{:S(2)}, u32[]{:S(2)}) collective-permute-start(bf16[384,2048]{1,0:T(8,128)(2,1)} %fusion.17), channel_id=1, source_target_pairs={{0,2},{2,0},{4,6},{6,4},{8,10},{10,8},{12,14},{14,12},{16,18},{18,... | collective-permute-start | bytes 4718600 | tf_op jit(solution)/shard_map/ppermute | solution.py:156
  41.2 23.0 %collective-permute-start.11 = (bf16[512,256]{1,0:T(8,128)(2,1)}, bf16[512,256]{1,0:T(8,128)(2,1)}, u32[]{:S(2)}, u32[]{:S(2)}) collective-permute-start(bf16[512,256]{1,0:T(8,128)(2,1)} %collective-permute-done.6), channel_id=1, source_target_pairs={{0,8},{2,10},{4,12},{6,14},{8,16},{10,18},{12,20},{14,22},{16,24},... | collective-permute-start | bytes 786440 | tf_op jit(solution)/shard_map/ppermute | solution.py:163
  64.2 26.3 %collective-permute-start.14 = (bf16[256,1536]{1,0:T(8,128)(2,1)}, bf16[256,1536]{1,0:T(8,128)(2,1)S(1)}, u32[]{:S(2)}, u32[]{:S(2)}) collective-permute-start(bf16[256,1536]{1,0:T(8,128)(2,1)} %collective-permute-done.10), channel_id=1, source_target_pairs={{0,8},{2,10},{4,12},{6,14},{8,16},{10,18},{12,20},{14,22},{16,24},... | collective-permute-start | bytes 2359304 | tf_op jit(solution)/shard_map/ppermute | solution.py:163
  64.3 26.2 %collective-permute-start.16 = (bf16[256,1536]{1,0:T(8,128)(2,1)}, bf16[256,1536]{1,0:T(8,128)(2,1)S(1)}, u32[]{:S(2)}, u32[]{:S(2)}) collective-permute-start(bf16[256,1536]{1,0:T(8,128)(2,1)} %collective-permute-done.10), channel_id=1, source_target_pairs={{0,4},{2,6},{4,0},{6,2},{8,12},{10,14},{12,8},{14,10},{16,20},{18,... | collective-permute-start | bytes 2359304 | tf_op jit(solution)/shard_map/ppermute | solution.py:156
  90.5 27.1 %collective-permute-start.18 = (bf16[512,1024]{1,0:T(8,128)(2,1)S(1)}, bf16[512,1024]{1,0:T(8,128)(2,1)}, u32[]{:S(2)}, u32[]{:S(2)}) collective-permute-start(bf16[512,1024]{1,0:T(8,128)(2,1)S(1)} %constant_dynamic-update-slice_fusion.34), channel_id=1, source_target_pairs={{0,8},{2,10},{4,12},{6,14},{8,16},{10,18},{12,20},{14,22},{16,24},... | collective-permute-start | bytes 3145736 | tf_op jit(solution)/shard_map/ppermute | solution.py:163
  90.5 25.2 %collective-permute-start.19 = (bf16[256,1536]{1,0:T(8,128)(2,1)S(1)}, bf16[256,1536]{1,0:T(8,128)(2,1)S(1)}, u32[]{:S(2)}, u32[]{:S(2)}) collective-permute-start(bf16[256,1536]{1,0:T(8,128)(2,1)S(1)} %collective-permute-done.14), channel_id=1, source_target_pairs={{0,4},{2,6},{4,0},{6,2},{8,12},{10,14},{12,8},{14,10},{16,20},{18,... | collective-permute-start | bytes 2359304 | tf_op jit(solution)/shard_map/ppermute | solution.py:156
  118.5 26.9 %collective-permute-start.22 = (bf16[512,1024]{1,0:T(8,128)(2,1)}, bf16[512,1024]{1,0:T(8,128)(2,1)}, u32[]{:S(2)}, u32[]{:S(2)}) collective-permute-start(bf16[512,1024]{1,0:T(8,128)(2,1)} %collective-permute-done.18), channel_id=1, source_target_pairs={{0,8},{2,10},{4,12},{6,14},{8,16},{10,18},{12,20},{14,22},{16,24},... | collective-permute-start | bytes 3145736 | tf_op jit(solution)/shard_map/ppermute | solution.py:163
  121.2 23.3 %collective-permute-start.26 = (bf16[512,256]{1,0:T(8,128)(2,1)}, bf16[512,256]{1,0:T(8,128)(2,1)}, u32[]{:S(2)}, u32[]{:S(2)}) collective-permute-start(bf16[512,256]{1,0:T(8,128)(2,1)} %collective-permute-done.15), channel_id=1, source_target_pairs={{0,4},{2,6},{4,0},{6,2},{8,12},{10,14},{12,8},{14,10},{16,20},{18,... | collective-permute-start | bytes 786440 | tf_op jit(solution)/shard_map/ppermute | solution.py:156
  137.1 57.5 %collective-permute-start.37 = (bf16[384,2048]{1,0:T(8,128)(2,1)S(1)}, bf16[384,2048]{1,0:T(8,128)(2,1)}, u32[]{:S(2)}, u32[]{:S(2)}) collective-permute-start(bf16[384,2048]{1,0:T(8,128)(2,1)S(1)} %copy-done.21), channel_id=1, source_target_pairs={{0,2},{2,0},{4,6},{6,4},{8,10},{10,8},{12,14},{14,12},{16,18},{18,... | collective-permute-start | bytes 4718600 | tf_op jit(solution)/shard_map/ppermute | solution.py:156
  152.9 27.3 %collective-permute-start.32 = (bf16[512,1024]{1,0:T(8,128)(2,1)}, bf16[512,1024]{1,0:T(8,128)(2,1)}, u32[]{:S(2)}, u32[]{:S(2)}) collective-permute-start(bf16[512,1024]{1,0:T(8,128)(2,1)} %collective-permute-done.22), channel_id=1, source_target_pairs={{0,8},{2,10},{4,12},{6,14},{8,16},{10,18},{12,20},{14,22},{16,24},... | collective-permute-start | bytes 3145736 | tf_op jit(solution)/shard_map/ppermute | solution.py:163
  153.4 41.9 %collective-permute-start.38 = (bf16[192,2048]{1,0:T(8,128)(2,1)}, bf16[192,2048]{1,0:T(8,128)(2,1)}, u32[]{:S(2)}, u32[]{:S(2)}) collective-permute-start(bf16[192,2048]{1,0:T(8,128)(2,1)} %get-tuple-element.1241), channel_id=1, source_target_pairs={{0,4},{2,6},{4,0},{6,2},{8,12},{10,14},{12,8},{14,10},{16,20},{18,... | collective-permute-start | bytes 2359304 | tf_op jit(solution)/shard_map/ppermute | solution.py:156
  155.0 27.5 %collective-permute-start.29 = (bf16[192,2048]{1,0:T(8,128)(2,1)S(1)}, bf16[192,2048]{1,0:T(8,128)(2,1)S(1)}, u32[]{:S(2)}, u32[]{:S(2)}) collective-permute-start(bf16[192,2048]{1,0:T(8,128)(2,1)S(1)} %add_convert_fusion.18), channel_id=1, source_target_pairs={{0,1},{1,0},{2,3},{3,2},{4,5},{5,4},{6,7},{7,6},{8,9},{9,8},{10,11... | collective-permute-start | bytes 2359304 | tf_op jit(solution)/shard_map/ppermute | solution.py:166
  182.5 26.4 %collective-permute-start.36 = (bf16[1024,512]{1,0:T(8,128)(2,1)}, bf16[1024,512]{1,0:T(8,128)(2,1)S(1)}, u32[]{:S(2)}, u32[]{:S(2)}) collective-permute-start(bf16[1024,512]{1,0:T(8,128)(2,1)} %constant_dynamic-update-slice_fusion.21), channel_id=1, source_target_pairs={{0,8},{2,10},{4,12},{6,14},{8,16},{10,18},{12,20},{14,22},{16,24},... | collective-permute-start | bytes 3145736 | tf_op jit(solution)/shard_map/ppermute | solution.py:163
  186.8 25.2 %collective-permute-start.34 = (bf16[192,2048]{1,0:T(8,128)(2,1)S(1)}, bf16[192,2048]{1,0:T(8,128)(2,1)S(1)}, u32[]{:S(2)}, u32[]{:S(2)}) collective-permute-start(bf16[192,2048]{1,0:T(8,128)(2,1)S(1)} %get-tuple-element.1060), channel_id=1, source_target_pairs={{0,4},{2,6},{4,0},{6,2},{8,12},{10,14},{12,8},{14,10},{16,20},{18,... | collective-permute-start | bytes 2359304 | tf_op jit(solution)/shard_map/ppermute | solution.py:156
  194.6 39.9 %collective-permute-start.39 = (bf16[192,2048]{1,0:T(8,128)(2,1)S(1)}, bf16[192,2048]{1,0:T(8,128)(2,1)S(1)}, u32[]{:S(2)}, u32[]{:S(2)}) collective-permute-start(bf16[192,2048]{1,0:T(8,128)(2,1)S(1)} %get-tuple-element.1085), channel_id=1, source_target_pairs={{0,4},{2,6},{4,0},{6,2},{8,12},{10,14},{12,8},{14,10},{16,20},{18,... | collective-permute-start | bytes 2359304 | tf_op jit(solution)/shard_map/ppermute | solution.py:156
  195.4 39.1 %collective-permute-start.40 = (bf16[192,2048]{1,0:T(8,128)(2,1)S(1)}, bf16[192,2048]{1,0:T(8,128)(2,1)S(1)}, u32[]{:S(2)}, u32[]{:S(2)}) collective-permute-start(bf16[192,2048]{1,0:T(8,128)(2,1)S(1)} %get-tuple-element.1085), channel_id=1, source_target_pairs={{0,2},{2,0},{4,6},{6,4},{8,10},{10,8},{12,14},{14,12},{16,18},{18,... | collective-permute-start | bytes 2359304 | tf_op jit(solution)/shard_map/ppermute | solution.py:156
  208.9 25.4 %collective-permute-start.42 = (bf16[1024,512]{1,0:T(8,128)(2,1)S(1)}, bf16[1024,512]{1,0:T(8,128)(2,1)S(1)}, u32[]{:S(2)}, u32[]{:S(2)}) collective-permute-start(bf16[1024,512]{1,0:T(8,128)(2,1)S(1)} %collective-permute-done.36), channel_id=1, source_target_pairs={{0,8},{2,10},{4,12},{6,14},{8,16},{10,18},{12,20},{14,22},{16,24},... | collective-permute-start | bytes 3145736 | tf_op jit(solution)/shard_map/ppermute | solution.py:163
  212.2 27.1 %collective-permute-start.45 = (bf16[192,2048]{1,0:T(8,128)(2,1)S(1)}, bf16[192,2048]{1,0:T(8,128)(2,1)S(1)}, u32[]{:S(2)}, u32[]{:S(2)}) collective-permute-start(bf16[192,2048]{1,0:T(8,128)(2,1)S(1)} %copy-done.32), channel_id=1, source_target_pairs={{0,4},{2,6},{4,0},{6,2},{8,12},{10,14},{12,8},{14,10},{16,20},{18,... | collective-permute-start | bytes 2359304 | tf_op jit(solution)/shard_map/ppermute | solution.py:156
  235.4 27.8 %collective-permute-start.47 = (bf16[1024,512]{1,0:T(8,128)(2,1)S(1)}, bf16[1024,512]{1,0:T(8,128)(2,1)S(1)}, u32[]{:S(2)}, u32[]{:S(2)}) collective-permute-start(bf16[1024,512]{1,0:T(8,128)(2,1)S(1)} %collective-permute-done.42), channel_id=1, source_target_pairs={{0,8},{2,10},{4,12},{6,14},{8,16},{10,18},{12,20},{14,22},{16,24},... | collective-permute-start | bytes 3145736 | tf_op jit(solution)/shard_map/ppermute | solution.py:163
  256.6 36.2 %collective-permute-start.55 = (bf16[1024,512]{1,0:T(8,128)(2,1)}, bf16[1024,512]{1,0:T(8,128)(2,1)S(1)}, u32[]{:S(2)}, u32[]{:S(2)}) collective-permute-start(bf16[1024,512]{1,0:T(8,128)(2,1)} %fusion.39), channel_id=1, source_target_pairs={{0,8},{2,10},{4,12},{6,14},{8,16},{10,18},{12,20},{14,22},{16,24},... | collective-permute-start | bytes 3145736 | tf_op jit(solution)/shard_map/ppermute | solution.py:163
  314.3 28.1 %collective-permute-start.54 = (bf16[512,1024]{1,0:T(8,128)(2,1)}, bf16[512,1024]{1,0:T(8,128)(2,1)S(1)}, u32[]{:S(2)}, u32[]{:S(2)}) collective-permute-start(bf16[512,1024]{1,0:T(8,128)(2,1)} %fusion.42), channel_id=1, source_target_pairs={{0,8},{2,10},{4,12},{6,14},{8,16},{10,18},{12,20},{14,22},{16,24},... | collective-permute-start | bytes 3145736 | tf_op jit(solution)/shard_map/ppermute | solution.py:163
  314.3 52.5 %collective-permute-start.76 = (bf16[1024,512]{1,0:T(8,128)(2,1)}, bf16[1024,512]{1,0:T(8,128)(2,1)S(1)}, u32[]{:S(2)}, u32[]{:S(2)}) collective-permute-start(bf16[1024,512]{1,0:T(8,128)(2,1)} %add_convert_fusion.3), channel_id=1, source_target_pairs={{0,8},{2,10},{4,12},{6,14},{8,16},{10,18},{12,20},{14,22},{16,24},... | collective-permute-start | bytes 3145736 | tf_op jit(solution)/shard_map/ppermute | solution.py:163
  329.9 33.8 %collective-permute-start.69 = (bf16[192,2048]{1,0:T(8,128)(2,1)S(1)}, bf16[192,2048]{1,0:T(8,128)(2,1)S(1)}, u32[]{:S(2)}, u32[]{:S(2)}) collective-permute-start(bf16[192,2048]{1,0:T(8,128)(2,1)S(1)} %add_convert_fusion.13), channel_id=1, source_target_pairs={{0,1},{1,0},{2,3},{3,2},{4,5},{5,4},{6,7},{7,6},{8,9},{9,8},{10,11... | collective-permute-start | bytes 2359304 | tf_op jit(solution)/shard_map/ppermute | solution.py:166
  362.1 27.2 %collective-permute-start.83 = (bf16[512,1024]{1,0:T(8,128)(2,1)S(1)}, bf16[512,1024]{1,0:T(8,128)(2,1)S(1)}, u32[]{:S(2)}, u32[]{:S(2)}) collective-permute-start(bf16[512,1024]{1,0:T(8,128)(2,1)S(1)} %add_convert_fusion.2), channel_id=1, source_target_pairs={{0,8},{2,10},{4,12},{6,14},{8,16},{10,18},{12,20},{14,22},{16,24},... | collective-permute-start | bytes 3145736 | tf_op jit(solution)/shard_map/ppermute | solution.py:163
  371.5 59.9 %collective-permute-start.81 = (bf16[192,2048]{1,0:T(8,128)(2,1)}, bf16[192,2048]{1,0:T(8,128)(2,1)}, u32[]{:S(2)}, u32[]{:S(2)}) collective-permute-start(bf16[192,2048]{1,0:T(8,128)(2,1)} %add_convert_fusion.12), channel_id=1, source_target_pairs={{0,4},{2,6},{4,0},{6,2},{8,12},{10,14},{12,8},{14,10},{16,20},{18,... | collective-permute-start | bytes 2359304 | tf_op jit(solution)/shard_map/ppermute | solution.py:156
  373.0 58.4 %collective-permute-start.82 = (bf16[192,2048]{1,0:T(8,128)(2,1)}, bf16[192,2048]{1,0:T(8,128)(2,1)}, u32[]{:S(2)}, u32[]{:S(2)}) collective-permute-start(bf16[192,2048]{1,0:T(8,128)(2,1)} %add_convert_fusion.11), channel_id=1, source_target_pairs={{0,4},{2,6},{4,0},{6,2},{8,12},{10,14},{12,8},{14,10},{16,20},{18,... | collective-permute-start | bytes 2359304 | tf_op jit(solution)/shard_map/ppermute | solution.py:156
  378.2 40.6 %collective-permute-start.77 = (bf16[512,256]{1,0:T(8,128)(2,1)}, bf16[512,256]{1,0:T(8,128)(2,1)}, u32[]{:S(2)}, u32[]{:S(2)}) collective-permute-start(bf16[512,256]{1,0:T(8,128)(2,1)} %dynamic-slice_convert_fusion.14), channel_id=1, source_target_pairs={{0,4},{2,6},{4,0},{6,2},{8,12},{10,14},{12,8},{14,10},{16,20},{18,... | collective-permute-start | bytes 786440 | tf_op jit(solution)/shard_map/ppermute | solution.py:156
  379.7 40.7 %collective-permute-start.78 = (bf16[512,256]{1,0:T(8,128)(2,1)}, bf16[512,256]{1,0:T(8,128)(2,1)}, u32[]{:S(2)}, u32[]{:S(2)}) collective-permute-start(bf16[512,256]{1,0:T(8,128)(2,1)} %dynamic-slice_convert_fusion.13), channel_id=1, source_target_pairs={{0,4},{2,6},{4,0},{6,2},{8,12},{10,14},{12,8},{14,10},{16,20},{18,... | collective-permute-start | bytes 786440 | tf_op jit(solution)/shard_map/ppermute | solution.py:156
  389.3 36.5 %collective-permute-start.79 = (bf16[512,256]{1,0:T(8,128)(2,1)}, bf16[512,256]{1,0:T(8,128)(2,1)S(1)}, u32[]{:S(2)}, u32[]{:S(2)}) collective-permute-start(bf16[512,256]{1,0:T(8,128)(2,1)} %dynamic-slice_convert_fusion.12), channel_id=1, source_target_pairs={{0,4},{2,6},{4,0},{6,2},{8,12},{10,14},{12,8},{14,10},{16,20},{18,... | collective-permute-start | bytes 786440 | tf_op jit(solution)/shard_map/ppermute | solution.py:156
  420.4 31.6 %collective-permute-start.85 = (bf16[1024,512]{1,0:T(8,128)(2,1)S(1)}, bf16[1024,512]{1,0:T(8,128)(2,1)S(1)}, u32[]{:S(2)}, u32[]{:S(2)}) collective-permute-start(bf16[1024,512]{1,0:T(8,128)(2,1)S(1)} %copy-done.84), channel_id=1, source_target_pairs={{0,8},{2,10},{4,12},{6,14},{8,16},{10,18},{12,20},{14,22},{16,24},... | collective-permute-start | bytes 3145736 | tf_op jit(solution)/shard_map/ppermute | solution.py:163
  425.8 49.3 %collective-permute-start.84 = (bf16[256,1536]{1,0:T(8,128)(2,1)S(1)}, bf16[256,1536]{1,0:T(8,128)(2,1)S(1)}, u32[]{:S(2)}, u32[]{:S(2)}) collective-permute-start(bf16[256,1536]{1,0:T(8,128)(2,1)S(1)} %dynamic-slice_convert_fusion.3), channel_id=1, source_target_pairs={{0,4},{2,6},{4,0},{6,2},{8,12},{10,14},{12,8},{14,10},{16,20},{18,... | collective-permute-start | bytes 2359304 | tf_op jit(solution)/shard_map/ppermute | solution.py:156
  431.4 37.1 %collective-permute-start.93 = (bf16[512,1024]{1,0:T(8,128)(2,1)S(1)}, bf16[512,1024]{1,0:T(8,128)(2,1)S(1)}, u32[]{:S(2)}, u32[]{:S(2)}) collective-permute-start(bf16[512,1024]{1,0:T(8,128)(2,1)S(1)} %copy-done.85), channel_id=1, source_target_pairs={{0,8},{2,10},{4,12},{6,14},{8,16},{10,18},{12,20},{14,22},{16,24},... | collective-permute-start | bytes 3145736 | tf_op jit(solution)/shard_map/ppermute | solution.py:163
  449.8 25.3 %collective-permute-start.92 = (bf16[192,2048]{1,0:T(8,128)(2,1)S(1)}, bf16[192,2048]{1,0:T(8,128)(2,1)S(1)}, u32[]{:S(2)}, u32[]{:S(2)}) collective-permute-start(bf16[192,2048]{1,0:T(8,128)(2,1)S(1)} %add_convert_fusion.10), channel_id=1, source_target_pairs={{0,1},{1,0},{2,3},{3,2},{4,5},{5,4},{6,7},{7,6},{8,9},{9,8},{10,11... | collective-permute-start | bytes 2359304 | tf_op jit(solution)/shard_map/ppermute | solution.py:166
  450.6 35.7 %collective-permute-start.98 = (bf16[192,2048]{1,0:T(8,128)(2,1)}, bf16[192,2048]{1,0:T(8,128)(2,1)}, u32[]{:S(2)}, u32[]{:S(2)}) collective-permute-start(bf16[192,2048]{1,0:T(8,128)(2,1)} %add_convert_fusion.9), channel_id=1, source_target_pairs={{0,1},{1,0},{2,3},{3,2},{4,5},{5,4},{6,7},{7,6},{8,9},{9,8},{10,11... | collective-permute-start | bytes 2359304 | tf_op jit(solution)/shard_map/ppermute | solution.py:166
  478.2 25.3 %collective-permute-start.94 = (bf16[256,1536]{1,0:T(8,128)(2,1)}, bf16[256,1536]{1,0:T(8,128)(2,1)}, u32[]{:S(2)}, u32[]{:S(2)}) collective-permute-start(bf16[256,1536]{1,0:T(8,128)(2,1)} %add_convert_fusion.6), channel_id=1, source_target_pairs={{0,8},{2,10},{4,12},{6,14},{8,16},{10,18},{12,20},{14,22},{16,24},... | collective-permute-start | bytes 2359304 | tf_op jit(solution)/shard_map/ppermute | solution.py:163
  478.2 25.3 %collective-permute-start.96 = (bf16[256,1536]{1,0:T(8,128)(2,1)}, bf16[256,1536]{1,0:T(8,128)(2,1)}, u32[]{:S(2)}, u32[]{:S(2)}) collective-permute-start(bf16[256,1536]{1,0:T(8,128)(2,1)} %dynamic-slice_convert_fusion.2), channel_id=1, source_target_pairs={{0,4},{2,6},{4,0},{6,2},{8,12},{10,14},{12,8},{14,10},{16,20},{18,... | collective-permute-start | bytes 2359304 | tf_op jit(solution)/shard_map/ppermute | solution.py:156
  479.4 23.5 %collective-permute-start.95 = (bf16[512,256]{1,0:T(8,128)(2,1)}, bf16[512,256]{1,0:T(8,128)(2,1)}, u32[]{:S(2)}, u32[]{:S(2)}) collective-permute-start(bf16[512,256]{1,0:T(8,128)(2,1)} %add_convert_fusion.21), channel_id=1, source_target_pairs={{0,8},{2,10},{4,12},{6,14},{8,16},{10,18},{12,20},{14,22},{16,24},... | collective-permute-start | bytes 786440 | tf_op jit(solution)/shard_map/ppermute | solution.py:163
  479.5 23.9 %collective-permute-start.97 = (bf16[1024,128]{1,0:T(8,128)(2,1)}, bf16[1024,128]{1,0:T(8,128)(2,1)}, u32[]{:S(2)}, u32[]{:S(2)}) collective-permute-start(bf16[1024,128]{1,0:T(8,128)(2,1)} %get-tuple-element.1484), channel_id=1, source_target_pairs={{0,6},{2,4},{4,2},{6,0},{8,14},{10,12},{12,10},{14,8},{16,22},{18,... | collective-permute-start | bytes 786440 | tf_op jit(solution)/shard_map/ppermute | solution.py:156
  486.3 25.6 %collective-permute-start.104 = (bf16[192,2048]{1,0:T(8,128)(2,1)S(1)}, bf16[192,2048]{1,0:T(8,128)(2,1)S(1)}, u32[]{:S(2)}, u32[]{:S(2)}) collective-permute-start(bf16[192,2048]{1,0:T(8,128)(2,1)S(1)} %add_convert_fusion.8), channel_id=1, source_target_pairs={{0,1},{1,0},{2,3},{3,2},{4,5},{5,4},{6,7},{7,6},{8,9},{9,8},{10,11... | collective-permute-start | bytes 2359304 | tf_op jit(solution)/shard_map/ppermute | solution.py:166
  510.8 24.8 %collective-permute-start.99 = (bf16[256,1536]{1,0:T(8,128)(2,1)S(1)}, bf16[256,1536]{1,0:T(8,128)(2,1)S(1)}, u32[]{:S(2)}, u32[]{:S(2)}) collective-permute-start(bf16[256,1536]{1,0:T(8,128)(2,1)S(1)} %add_convert_fusion.5), channel_id=1, source_target_pairs={{0,8},{2,10},{4,12},{6,14},{8,16},{10,18},{12,20},{14,22},{16,24},... | collective-permute-start | bytes 2359304 | tf_op jit(solution)/shard_map/ppermute | solution.py:163
  510.9 24.7 %collective-permute-start.100 = (bf16[512,256]{1,0:T(8,128)(2,1)S(1)}, bf16[512,256]{1,0:T(8,128)(2,1)S(1)}, u32[]{:S(2)}, u32[]{:S(2)}) collective-permute-start(bf16[512,256]{1,0:T(8,128)(2,1)S(1)} %add_convert_fusion.20), channel_id=1, source_target_pairs={{0,8},{2,10},{4,12},{6,14},{8,16},{10,18},{12,20},{14,22},{16,24},... | collective-permute-start | bytes 786440 | tf_op jit(solution)/shard_map/ppermute | solution.py:163
  510.9 24.6 %collective-permute-start.101 = (bf16[256,1536]{1,0:T(8,128)(2,1)S(1)}, bf16[256,1536]{1,0:T(8,128)(2,1)S(1)}, u32[]{:S(2)}, u32[]{:S(2)}) collective-permute-start(bf16[256,1536]{1,0:T(8,128)(2,1)S(1)} %copy-done.56), channel_id=1, source_target_pairs={{0,4},{2,6},{4,0},{6,2},{8,12},{10,14},{12,8},{14,10},{16,20},{18,... | collective-permute-start | bytes 2359304 | tf_op jit(solution)/shard_map/ppermute | solution.py:156
  512.0 23.5 %collective-permute-start.102 = (bf16[128,1024]{1,0:T(8,128)(2,1)S(1)}, bf16[128,1024]{1,0:T(8,128)(2,1)S(1)}, u32[]{:S(2)}, u32[]{:S(2)}) collective-permute-start(bf16[128,1024]{1,0:T(8,128)(2,1)S(1)} %copy-done.62), channel_id=1, source_target_pairs={{0,2},{2,0},{4,6},{6,4},{8,10},{10,8},{12,14},{14,12},{16,18},{18,... | collective-permute-start | bytes 786440 | tf_op jit(solution)/shard_map/ppermute | solution.py:156
  538.0 25.0 %collective-permute-start.106 = (bf16[256,1536]{1,0:T(8,128)(2,1)S(1)}, bf16[256,1536]{1,0:T(8,128)(2,1)S(1)}, u32[]{:S(2)}, u32[]{:S(2)}) collective-permute-start(bf16[256,1536]{1,0:T(8,128)(2,1)S(1)} %add_convert_fusion.4), channel_id=1, source_target_pairs={{0,8},{2,10},{4,12},{6,14},{8,16},{10,18},{12,20},{14,22},{16,24},... | collective-permute-start | bytes 2359304 | tf_op jit(solution)/shard_map/ppermute | solution.py:163
  (159 other events, 1479.6 us)

commit v5 on v4

--- a/solution.py
+++ b/solution.py
@@ -613,6 +613,7 @@
         scaled = wide(jnp.concatenate(lows)) + wide(jnp.concatenate(crosses))
         return jnp.concatenate(grads) + norm_backward(scaled, standard, inverse)
 
+    down_arrived = wait(down_sum)
     qkv_owns, qkv_fars = [], []
     for k in range(1, ring + 1):
         own, far = run(lambda n, g: part_qkv(n, g, k), normed_one, grad_qkv)
@@ -621,10 +622,6 @@
     *out_fars, far_r[0], far_r[1] = wait(*out_fars, *far_r)
     low_r = [run(near_sum, near_r[j], far_r[j]) for j in range(2)]
     cross_r = [across(part) for part in low_r]
-    core_m = [links.to_core(v) for v in run(low_part_of(outer, 1), grad_qkv, qkv_full)]
-    own_m = run(part_of(outer, 0), grad_qkv, qkv_full)
-    low_m = [run(add_pieces_low, own_m[j], *wait(*core_m[j])) for j in range(2)]
-    down_arrived = wait(down_sum)
     for k in range(4, ring + 1):
         down_sum = ring_down(k, down_arrived)
         if k < ring:
@@ -638,9 +635,7 @@
             up_arrived = wait(up_sum)
     up_ends = list(run(lambda t: cut(t, 0, owned), up_sum))
 
-    qkv_fars[0], down_ends[1], down_ends[2], cross_r[0] = wait(
-        qkv_fars[0], down_ends[1], down_ends[2], cross_r[0]
-    )
+    qkv_fars[0], down_ends[1], down_ends[2] = wait(qkv_fars[0], down_ends[1], down_ends[2])
     qkv_sum, out_sum = run(
         lambda a, b, c, d: (add_low(a, b), add_low(c, d)),
         qkv_owns[0],
@@ -652,8 +647,11 @@
         sent = [step(qkv_sum), step(out_sum), swap(qkv_fars[k - 1], 2)]
         if k == 2:
             down_ends[3] = swap(down_ends[3], 3)
+            core_m = [links.to_core(v) for v in run(low_part_of(outer, 1), grad_qkv, qkv_full)]
+            own_m = run(part_of(outer, 0), grad_qkv, qkv_full)
+            low_m = [run(add_pieces_low, own_m[j], *wait(*core_m[j])) for j in range(2)]
             cross_m = [across(part) for part in low_m]
-            *sent, down_ends[3], cross_r[1] = wait(*sent, down_ends[3], cross_r[1])
+            *sent, down_ends[3], cross_r[0], cross_r[1] = wait(*sent, down_ends[3], *cross_r)
         elif k == 3:
             up_ends[1], up_ends[2] = swap(up_ends[1], 1), swap(up_ends[2], 2)
             result = run(

time: 586 us -> 578 us (0.986)
  local copies, waits for them, and re-layouts: 80 us -> 70.7 us
  other arithmetic: 63.8 us -> 55.1 us
  waiting for transfers between devices: 253 us -> 260 us
    ppermute x80, waiting for transfers between devices: 61.9 us -> 83.2 us  [swap(): return lax.ppermute(self.order.tie(values), 'dp', self.to[k])]
    ppermute x10, waiting for transfers between devices: 26 us -> 9.41 us  [across(): return lax.ppermute(self.order.tie(values), 'mp', [(0, 1), (1, 0)])]
    unnamed x192 -> x158, local copies, waits for them, and re-layouts: 11.8 us -> 10.5 us
  transfers between devices with their start and end apart: 114 -> 114, of which waited for: 47 -> 47; matrix products, arithmetic and copies ran while one was open for 39% -> 37% of each run, Pallas kernels for 2% -> 2%
where the time goes in v5:
time: 578 us; the launch traced here: 572 us
  waiting for transfers between devices  260 us (45%)
  matrix products  104 us (18%)
  local copies, waits for them, and re-layouts  70.7 us (12%)
  starting transfers between devices  66.3 us (11%)
  other arithmetic  55.1 us (10%)
  Pallas kernels  11.4 us (2%)
    ppermute x24, waiting for transfers between devices, step(): return lax.ppermute(self.order.tie(values), 'dp', self.next)  168 us
    ppermute x80, waiting for transfers between devices, swap(): return lax.ppermute(self.order.tie(values), 'dp', self.to[k])  83.2 us
    ppermute x80, starting transfers between devices, swap(): return lax.ppermute(self.order.tie(values), 'dp', self.to[k])  43.4 us
    dot_general x8, matrix products, outer(): lax.dot_general(one, two, (((1,), (1,)), ((), ())), preferred_element_typ...  39.4 us
    dot_general x16, matrix products, inner(): lax.dot_general(one, two, (((0,), (0,)), ((), ())), preferred_element_typ...  35.4 us
    dynamic_update_slice x34, local copies, waits for them, and re-layouts, put(): lax.dynamic_update_slice_in_dim(whole, part, index * part.shape[axis], axis)  31 us
    dot_general x8, matrix products, plain(): return jnp.dot(one, two, preferred_element_type=WIDE)  29.3 us
    ppermute x24, starting transfers between devices, step(): return lax.ppermute(self.order.tie(values), 'dp', self.next)  13.8 us
  transfers between devices with their start and end apart: 114, of which 47 were waited for; matrix products, arithmetic and copies ran while one was open for 37% of the time, Pallas kernels for 2%

profile of v5, /device:TPU:0, one launch (start us, length us, event | category | flops | bytes accessed | tf_op | source)
XLA Modules:
  0.0 571.6 jit_solution(2280372175088861681)
XLA Ops:
  8.0 3.1 collective-permute-start.5
  17.5 3.0 broadcast_in_dim.32
  22.9 13.6 %collective-permute-done.6 = bf16[512,256]{1,0:T(8,128)(2,1)} collective-permute-done((bf16[512,256]{1,0:T(8,128)(2,1)S(1)}, bf16[512,256]{1,0:T(8,128)(2,1)}, u32[]{:S(2)}, u32[]{:S(2)}) %collective-permute-start.6) | collective-permute-done | bytes 262176 | tf_op jit(solution)/shard_map/ppermute | solution.py:163
  47.1 17.1 %collective-permute-done.11 = bf16[512,256]{1,0:T(8,128)(2,1)} collective-permute-done((bf16[512,256]{1,0:T(8,128)(2,1)}, bf16[512,256]{1,0:T(8,128)(2,1)}, u32[]{:S(2)}, u32[]{:S(2)}) %collective-permute-start.11) | collective-permute-done | bytes 262176 | tf_op jit(solution)/shard_map/ppermute | solution.py:163
  71.9 18.0 %collective-permute-done.15 = bf16[512,256]{1,0:T(8,128)(2,1)} collective-permute-done((bf16[512,256]{1,0:T(8,128)(2,1)}, bf16[512,256]{1,0:T(8,128)(2,1)}, u32[]{:S(2)}, u32[]{:S(2)}) %collective-permute-start.15) | collective-permute-done | bytes 262176 | tf_op jit(solution)/shard_map/ppermute | solution.py:163
  96.1 2.9 broadcast_in_dim.35
  100.1 15.6 %collective-permute-done.20 = bf16[1024,128]{1,0:T(8,128)(2,1)S(1)} collective-permute-done((bf16[1024,128]{1,0:T(8,128)(2,1)S(1)}, bf16[1024,128]{1,0:T(8,128)(2,1)S(1)}, u32[]{:S(2)}, u32[]{:S(2)}) %collective-permute-start.20) | collective-permute-done | bytes 262176 | tf_op jit(solution)/shard_map/ppermute | solution.py:156
  122.5 8.0 %convolution_convert_fusion.query.key.value = bf16[768,1536]{1,0:T(8,128)(2,1)S(1)} fusion(bf16[768,2048]{1,0:T(8,128)(2,1)S(1)} %pad_maximum_fusion, bf16[2048,1536]{1,0:T(8,128)(2,1)} %constant_dynamic-update-slice_fusion.28), kind=kOutput, calls=%fused_computation.19 | convolution fusion | flops 4833017856 | bytes 11796480 | tf_op jit(solution)/shard_map/dot_general | solution.py:20
  132.7 4.4 shard_map.195
  138.9 5.6 collective-permute-done.26
  171.9 8.4 %collective-permute-done.32 = bf16[512,1024]{1,0:T(8,128)(2,1)} collective-permute-done((bf16[512,1024]{1,0:T(8,128)(2,1)}, bf16[512,1024]{1,0:T(8,128)(2,1)}, u32[]{:S(2)}, u32[]{:S(2)}) %collective-permute-start.32) | collective-permute-done | bytes 1048608 | tf_op jit(solution)/shard_map/ppermute | solution.py:163
  188.1 3.1 collective-permute-done.33
  195.7 13.2 %collective-permute-done.36 = bf16[1024,512]{1,0:T(8,128)(2,1)S(1)} collective-permute-done((bf16[1024,512]{1,0:T(8,128)(2,1)}, bf16[1024,512]{1,0:T(8,128)(2,1)S(1)}, u32[]{:S(2)}, u32[]{:S(2)}) %collective-permute-start.36) | collective-permute-done | bytes 1048608 | tf_op jit(solution)/shard_map/ppermute | solution.py:163
  213.6 20.7 %collective-permute-done.42 = bf16[1024,512]{1,0:T(8,128)(2,1)S(1)} collective-permute-done((bf16[1024,512]{1,0:T(8,128)(2,1)S(1)}, bf16[1024,512]{1,0:T(8,128)(2,1)S(1)}, u32[]{:S(2)}, u32[]{:S(2)}) %collective-permute-start.42) | collective-permute-done | bytes 1048608 | tf_op jit(solution)/shard_map/ppermute | solution.py:163
  240.0 12.0 %fusion.4 = (bf16[1536,1024]{1,0:T(8,128)(2,1)}, bf16[1536,1024]{1,0:T(8,128)(2,1)S(1)}) fusion(bf16[1536,2048]{1,0:T(8,128)(2,1)S(1)} %maximum_dynamic-update-slice_fusion, bf16[2048,1024]{1,0:T(8,128)(2,1)} %constant_dynamic-update-slice_fusion.16), kind=kOutput, calls=%fused_computation.5 | convolution fusion | flops 6459752448 | bytes 16777216 | tf_op jit(solution)/shard_map/dot_general | solution.py:20
  253.7 3.0 fusion.39
  256.7 6.6 %collective-permute-done.47 = bf16[1024,512]{1,0:T(8,128)(2,1)S(1)} collective-permute-done((bf16[1024,512]{1,0:T(8,128)(2,1)S(1)}, bf16[1024,512]{1,0:T(8,128)(2,1)S(1)}, u32[]{:S(2)}, u32[]{:S(2)}) %collective-permute-start.47) | collective-permute-done | bytes 1048608 | tf_op jit(solution)/shard_map/ppermute | solution.py:163
  263.4 10.3 %multiply_convert_fusion = bf16[1536,1024]{1,0:T(8,128)(2,1)} fusion(bf16[1536,1024]{1,0:T(8,128)(2,1)} %get-tuple-element.1150, bf16[1536,2048]{1,0:T(8,128)(2,1)S(1)} %maximum_dynamic-update-slice_fusion.1, bf16[1024,2048]{1,0:T(8,128)(2,1)S(1)} %constant_dynamic-update-slice_fusion.2), kind=kOutput, calls=%fused_computation.6 | convolution fusion | flops 6447169536 | bytes 16777216 | tf_op jit(solution)/shard_map/dot_general | solution.py:28
  273.8 4.3 convolution_convert_fusion.4
  279.9 4.0 fusion.83
  288.8 2.8 fusion.42
  292.9 2.9 add_convert_fusion.3
  295.7 4.0 convolution_convert_fusion.3
  299.9 4.0 fusion.80
  309.1 2.9 collective-permute-done.58
  314.8 13.4 %collective-permute-done.62 = bf16[192,2048]{1,0:T(8,128)(2,1)} collective-permute-done((bf16[192,2048]{1,0:T(8,128)(2,1)}, bf16[192,2048]{1,0:T(8,128)(2,1)}, u32[]{:S(2)}, u32[]{:S(2)}) %collective-permute-start.62) | collective-permute-done | bytes 786464 | tf_op jit(solution)/shard_map/ppermute | solution.py:156
  333.3 3.5 fusion.109
  336.8 5.7 %collective-permute-done.54 = bf16[512,1024]{1,0:T(8,128)(2,1)S(1)} collective-permute-done((bf16[512,1024]{1,0:T(8,128)(2,1)}, bf16[512,1024]{1,0:T(8,128)(2,1)S(1)}, u32[]{:S(2)}, u32[]{:S(2)}) %collective-permute-start.54) | collective-permute-done | bytes 1048608 | tf_op jit(solution)/shard_map/ppermute | solution.py:163
  342.5 3.2 add_convert_fusion.2
  367.2 4.3 add_convert_fusion.1
  384.1 6.0 %collective-permute-done.83 = bf16[512,1024]{1,0:T(8,128)(2,1)S(1)} collective-permute-done((bf16[512,1024]{1,0:T(8,128)(2,1)S(1)}, bf16[512,1024]{1,0:T(8,128)(2,1)S(1)}, u32[]{:S(2)}, u32[]{:S(2)}) %collective-permute-start.83) | collective-permute-done | bytes 1048608 | tf_op jit(solution)/shard_map/ppermute | solution.py:163
  391.6 4.2 add_convert_fusion
  400.1 7.0 %shard_map.196 = (bf16[768,512]{1,0:T(8,128)(2,1)S(1)}, bf16[768,512]{1,0:T(8,128)(2,1)S(1)}, bf16[768,512]{1,0:T(8,128)(2,1)S(1)}) custom-call(bf16[768,1536]{1,0:T(8,128)(2,1)S(1)} %convolution_convert_fusion.query.key.value, bf16[768,1536]{1,0:T(8,128)(2,1)S(1)} %convolution_convert_fusion.query.key.value, ...), custom_call_target="tpu_custom_call" | custom-call | tf_op jit(solution)/shard_map/pallas_call | solution.py:103
  407.3 4.6 collective-permute-done.84
  421.2 4.6 collective-permute-done.79
  425.8 4.8 collective-permute-done.80
  435.0 3.7 convert_add_fusion.2
  440.5 6.7 %collective-permute-done.88 = bf16[512,1024]{1,0:T(8,128)(2,1)S(1)} collective-permute-done((bf16[512,1024]{1,0:T(8,128)(2,1)S(1)}, bf16[512,1024]{1,0:T(8,128)(2,1)S(1)}, u32[]{:S(2)}, u32[]{:S(2)}) %collective-permute-start.88) | collective-permute-done | bytes 1048608 | tf_op jit(solution)/shard_map/ppermute | solution.py:163
  447.7 3.2 convert_add_fusion.1
  451.1 6.8 %collective-permute-done.87 = bf16[1024,128]{1,0:T(8,128)(2,1)S(1)} collective-permute-done((bf16[1024,128]{1,0:T(8,128)(2,1)S(1)}, bf16[1024,128]{1,0:T(8,128)(2,1)S(1)}, u32[]{:S(2)}, u32[]{:S(2)}) %collective-permute-start.87) | collective-permute-done | bytes 262176 | tf_op jit(solution)/shard_map/ppermute | solution.py:156
  459.1 5.4 convolution_convert_fusion.5
  465.5 4.7 fusion.55
  476.9 21.1 %collective-permute-done.90 = bf16[512,256]{1,0:T(8,128)(2,1)S(1)} collective-permute-done((bf16[512,256]{1,0:T(8,128)(2,1)S(1)}, bf16[512,256]{1,0:T(8,128)(2,1)S(1)}, u32[]{:S(2)}, u32[]{:S(2)}) %collective-permute-start.90) | collective-permute-done | bytes 262176 | tf_op jit(solution)/shard_map/ppermute | solution.py:163
  504.5 5.9 %collective-permute-done.100 = bf16[512,256]{1,0:T(8,128)(2,1)S(1)} collective-permute-done((bf16[512,256]{1,0:T(8,128)(2,1)S(1)}, bf16[512,256]{1,0:T(8,128)(2,1)S(1)}, u32[]{:S(2)}, u32[]{:S(2)}) %collective-permute-start.100) | collective-permute-done | bytes 262176 | tf_op jit(solution)/shard_map/ppermute | solution.py:163
  513.2 14.9 %collective-permute-done.103 = bf16[128,1024]{1,0:T(8,128)(2,1)S(1)} collective-permute-done((bf16[128,1024]{1,0:T(8,128)(2,1)S(1)}, bf16[128,1024]{1,0:T(8,128)(2,1)S(1)}, u32[]{:S(2)}, u32[]{:S(2)}) %collective-permute-start.103) | collective-permute-done | bytes 262176 | tf_op jit(solution)/shard_map/ppermute | solution.py:156
  534.7 4.6 fusion.14
  539.2 17.4 %collective-permute-done.107 = bf16[512,256]{1,0:T(8,128)(2,1)S(1)} collective-permute-done((bf16[512,256]{1,0:T(8,128)(2,1)S(1)}, bf16[512,256]{1,0:T(8,128)(2,1)S(1)}, u32[]{:S(2)}, u32[]{:S(2)}) %collective-permute-start.107) | collective-permute-done | bytes 262176 | tf_op jit(solution)/shard_map/ppermute | solution.py:163
  561.0 2.7 collective-permute-done.113
  (579 shorter events, 216.1 us)
Async XLA Ops:
  8.0 28.6 %collective-permute-start.5 = (bf16[256,1536]{1,0:T(8,128)(2,1)S(1)}, bf16[256,1536]{1,0:T(8,128)(2,1)}, u32[]{:S(2)}, u32[]{:S(2)}) collective-permute-start(bf16[256,1536]{1,0:T(8,128)(2,1)S(1)} %maximum_select_fusion), channel_id=1, source_target_pairs={{0,8},{2,10},{4,12},{6,14},{8,16},{10,18},{12,20},{14,22},{16,24},... | collective-permute-start | bytes 2359304 | tf_op jit(solution)/shard_map/ppermute | solution.py:163
  11.1 25.5 %collective-permute-start.7 = (bf16[256,1536]{1,0:T(8,128)(2,1)S(1)}, bf16[256,1536]{1,0:T(8,128)(2,1)S(1)}, u32[]{:S(2)}, u32[]{:S(2)}) collective-permute-start(bf16[256,1536]{1,0:T(8,128)(2,1)S(1)} %maximum_select_fusion), channel_id=1, source_target_pairs={{0,4},{2,6},{4,0},{6,2},{8,12},{10,14},{12,8},{14,10},{16,20},{18,... | collective-permute-start | bytes 2359304 | tf_op jit(solution)/shard_map/ppermute | solution.py:156
  37.5 26.7 %collective-permute-start.10 = (bf16[256,1536]{1,0:T(8,128)(2,1)}, bf16[256,1536]{1,0:T(8,128)(2,1)}, u32[]{:S(2)}, u32[]{:S(2)}) collective-permute-start(bf16[256,1536]{1,0:T(8,128)(2,1)} %collective-permute-done.5), channel_id=1, source_target_pairs={{0,8},{2,10},{4,12},{6,14},{8,16},{10,18},{12,20},{14,22},{16,24},... | collective-permute-start | bytes 2359304 | tf_op jit(solution)/shard_map/ppermute | solution.py:163
  38.4 25.8 %collective-permute-start.12 = (bf16[256,1536]{1,0:T(8,128)(2,1)}, bf16[256,1536]{1,0:T(8,128)(2,1)}, u32[]{:S(2)}, u32[]{:S(2)}) collective-permute-start(bf16[256,1536]{1,0:T(8,128)(2,1)} %collective-permute-done.5), channel_id=1, source_target_pairs={{0,4},{2,6},{4,0},{6,2},{8,12},{10,14},{12,8},{14,10},{16,20},{18,... | collective-permute-start | bytes 2359304 | tf_op jit(solution)/shard_map/ppermute | solution.py:156
  41.2 53.6 %collective-permute-start.2 = (bf16[384,2048]{1,0:T(8,128)(2,1)}, bf16[384,2048]{1,0:T(8,128)(2,1)S(1)}, u32[]{:S(2)}, u32[]{:S(2)}) collective-permute-start(bf16[384,2048]{1,0:T(8,128)(2,1)} %fusion.17), channel_id=1, source_target_pairs={{0,2},{2,0},{4,6},{6,4},{8,10},{10,8},{12,14},{14,12},{16,18},{18,... | collective-permute-start | bytes 4718600 | tf_op jit(solution)/shard_map/ppermute | solution.py:156
  41.2 23.0 %collective-permute-start.11 = (bf16[512,256]{1,0:T(8,128)(2,1)}, bf16[512,256]{1,0:T(8,128)(2,1)}, u32[]{:S(2)}, u32[]{:S(2)}) collective-permute-start(bf16[512,256]{1,0:T(8,128)(2,1)} %collective-permute-done.6), channel_id=1, source_target_pairs={{0,8},{2,10},{4,12},{6,14},{8,16},{10,18},{12,20},{14,22},{16,24},... | collective-permute-start | bytes 786440 | tf_op jit(solution)/shard_map/ppermute | solution.py:163
  64.2 26.3 %collective-permute-start.14 = (bf16[256,1536]{1,0:T(8,128)(2,1)}, bf16[256,1536]{1,0:T(8,128)(2,1)S(1)}, u32[]{:S(2)}, u32[]{:S(2)}) collective-permute-start(bf16[256,1536]{1,0:T(8,128)(2,1)} %collective-permute-done.10), channel_id=1, source_target_pairs={{0,8},{2,10},{4,12},{6,14},{8,16},{10,18},{12,20},{14,22},{16,24},... | collective-permute-start | bytes 2359304 | tf_op jit(solution)/shard_map/ppermute | solution.py:163
  64.2 26.2 %collective-permute-start.16 = (bf16[256,1536]{1,0:T(8,128)(2,1)}, bf16[256,1536]{1,0:T(8,128)(2,1)S(1)}, u32[]{:S(2)}, u32[]{:S(2)}) collective-permute-start(bf16[256,1536]{1,0:T(8,128)(2,1)} %collective-permute-done.10), channel_id=1, source_target_pairs={{0,4},{2,6},{4,0},{6,2},{8,12},{10,14},{12,8},{14,10},{16,20},{18,... | collective-permute-start | bytes 2359304 | tf_op jit(solution)/shard_map/ppermute | solution.py:156
  90.5 27.1 %collective-permute-start.18 = (bf16[512,1024]{1,0:T(8,128)(2,1)S(1)}, bf16[512,1024]{1,0:T(8,128)(2,1)}, u32[]{:S(2)}, u32[]{:S(2)}) collective-permute-start(bf16[512,1024]{1,0:T(8,128)(2,1)S(1)} %constant_dynamic-update-slice_fusion.34), channel_id=1, source_target_pairs={{0,8},{2,10},{4,12},{6,14},{8,16},{10,18},{12,20},{14,22},{16,24},... | collective-permute-start | bytes 3145736 | tf_op jit(solution)/shard_map/ppermute | solution.py:163
  90.5 25.2 %collective-permute-start.19 = (bf16[256,1536]{1,0:T(8,128)(2,1)S(1)}, bf16[256,1536]{1,0:T(8,128)(2,1)S(1)}, u32[]{:S(2)}, u32[]{:S(2)}) collective-permute-start(bf16[256,1536]{1,0:T(8,128)(2,1)S(1)} %collective-permute-done.14), channel_id=1, source_target_pairs={{0,4},{2,6},{4,0},{6,2},{8,12},{10,14},{12,8},{14,10},{16,20},{18,... | collective-permute-start | bytes 2359304 | tf_op jit(solution)/shard_map/ppermute | solution.py:156
  118.5 26.9 %collective-permute-start.22 = (bf16[512,1024]{1,0:T(8,128)(2,1)}, bf16[512,1024]{1,0:T(8,128)(2,1)}, u32[]{:S(2)}, u32[]{:S(2)}) collective-permute-start(bf16[512,1024]{1,0:T(8,128)(2,1)} %collective-permute-done.18), channel_id=1, source_target_pairs={{0,8},{2,10},{4,12},{6,14},{8,16},{10,18},{12,20},{14,22},{16,24},... | collective-permute-start | bytes 3145736 | tf_op jit(solution)/shard_map/ppermute | solution.py:163
  121.2 23.2 %collective-permute-start.26 = (bf16[512,256]{1,0:T(8,128)(2,1)}, bf16[512,256]{1,0:T(8,128)(2,1)}, u32[]{:S(2)}, u32[]{:S(2)}) collective-permute-start(bf16[512,256]{1,0:T(8,128)(2,1)} %collective-permute-done.15), channel_id=1, source_target_pairs={{0,4},{2,6},{4,0},{6,2},{8,12},{10,14},{12,8},{14,10},{16,20},{18,... | collective-permute-start | bytes 786440 | tf_op jit(solution)/shard_map/ppermute | solution.py:156
  137.1 57.5 %collective-permute-start.37 = (bf16[384,2048]{1,0:T(8,128)(2,1)S(1)}, bf16[384,2048]{1,0:T(8,128)(2,1)}, u32[]{:S(2)}, u32[]{:S(2)}) collective-permute-start(bf16[384,2048]{1,0:T(8,128)(2,1)S(1)} %copy-done.21), channel_id=1, source_target_pairs={{0,2},{2,0},{4,6},{6,4},{8,10},{10,8},{12,14},{14,12},{16,18},{18,... | collective-permute-start | bytes 4718600 | tf_op jit(solution)/shard_map/ppermute | solution.py:156
  152.9 27.3 %collective-permute-start.32 = (bf16[512,1024]{1,0:T(8,128)(2,1)}, bf16[512,1024]{1,0:T(8,128)(2,1)}, u32[]{:S(2)}, u32[]{:S(2)}) collective-permute-start(bf16[512,1024]{1,0:T(8,128)(2,1)} %collective-permute-done.22), channel_id=1, source_target_pairs={{0,8},{2,10},{4,12},{6,14},{8,16},{10,18},{12,20},{14,22},{16,24},... | collective-permute-start | bytes 3145736 | tf_op jit(solution)/shard_map/ppermute | solution.py:163
  153.5 42.0 %collective-permute-start.38 = (bf16[192,2048]{1,0:T(8,128)(2,1)}, bf16[192,2048]{1,0:T(8,128)(2,1)}, u32[]{:S(2)}, u32[]{:S(2)}) collective-permute-start(bf16[192,2048]{1,0:T(8,128)(2,1)} %get-tuple-element.1241), channel_id=1, source_target_pairs={{0,4},{2,6},{4,0},{6,2},{8,12},{10,14},{12,8},{14,10},{16,20},{18,... | collective-permute-start | bytes 2359304 | tf_op jit(solution)/shard_map/ppermute | solution.py:156
  155.0 27.5 %collective-permute-start.29 = (bf16[192,2048]{1,0:T(8,128)(2,1)S(1)}, bf16[192,2048]{1,0:T(8,128)(2,1)S(1)}, u32[]{:S(2)}, u32[]{:S(2)}) collective-permute-start(bf16[192,2048]{1,0:T(8,128)(2,1)S(1)} %add_convert_fusion.18), channel_id=1, source_target_pairs={{0,1},{1,0},{2,3},{3,2},{4,5},{5,4},{6,7},{7,6},{8,9},{9,8},{10,11... | collective-permute-start | bytes 2359304 | tf_op jit(solution)/shard_map/ppermute | solution.py:166
  182.5 26.4 %collective-permute-start.36 = (bf16[1024,512]{1,0:T(8,128)(2,1)}, bf16[1024,512]{1,0:T(8,128)(2,1)S(1)}, u32[]{:S(2)}, u32[]{:S(2)}) collective-permute-start(bf16[1024,512]{1,0:T(8,128)(2,1)} %constant_dynamic-update-slice_fusion.21), channel_id=1, source_target_pairs={{0,8},{2,10},{4,12},{6,14},{8,16},{10,18},{12,20},{14,22},{16,24},... | collective-permute-start | bytes 3145736 | tf_op jit(solution)/shard_map/ppermute | solution.py:163
  186.8 25.2 %collective-permute-start.34 = (bf16[192,2048]{1,0:T(8,128)(2,1)S(1)}, bf16[192,2048]{1,0:T(8,128)(2,1)S(1)}, u32[]{:S(2)}, u32[]{:S(2)}) collective-permute-start(bf16[192,2048]{1,0:T(8,128)(2,1)S(1)} %get-tuple-element.1060), channel_id=1, source_target_pairs={{0,4},{2,6},{4,0},{6,2},{8,12},{10,14},{12,8},{14,10},{16,20},{18,... | collective-permute-start | bytes 2359304 | tf_op jit(solution)/shard_map/ppermute | solution.py:156
  194.6 39.9 %collective-permute-start.39 = (bf16[192,2048]{1,0:T(8,128)(2,1)S(1)}, bf16[192,2048]{1,0:T(8,128)(2,1)S(1)}, u32[]{:S(2)}, u32[]{:S(2)}) collective-permute-start(bf16[192,2048]{1,0:T(8,128)(2,1)S(1)} %get-tuple-element.1085), channel_id=1, source_target_pairs={{0,4},{2,6},{4,0},{6,2},{8,12},{10,14},{12,8},{14,10},{16,20},{18,... | collective-permute-start | bytes 2359304 | tf_op jit(solution)/shard_map/ppermute | solution.py:156
  195.5 39.0 %collective-permute-start.40 = (bf16[192,2048]{1,0:T(8,128)(2,1)S(1)}, bf16[192,2048]{1,0:T(8,128)(2,1)S(1)}, u32[]{:S(2)}, u32[]{:S(2)}) collective-permute-start(bf16[192,2048]{1,0:T(8,128)(2,1)S(1)} %get-tuple-element.1085), channel_id=1, source_target_pairs={{0,2},{2,0},{4,6},{6,4},{8,10},{10,8},{12,14},{14,12},{16,18},{18,... | collective-permute-start | bytes 2359304 | tf_op jit(solution)/shard_map/ppermute | solution.py:156
  208.9 25.4 %collective-permute-start.42 = (bf16[1024,512]{1,0:T(8,128)(2,1)S(1)}, bf16[1024,512]{1,0:T(8,128)(2,1)S(1)}, u32[]{:S(2)}, u32[]{:S(2)}) collective-permute-start(bf16[1024,512]{1,0:T(8,128)(2,1)S(1)} %collective-permute-done.36), channel_id=1, source_target_pairs={{0,8},{2,10},{4,12},{6,14},{8,16},{10,18},{12,20},{14,22},{16,24},... | collective-permute-start | bytes 3145736 | tf_op jit(solution)/shard_map/ppermute | solution.py:163
  212.3 27.1 %collective-permute-start.45 = (bf16[192,2048]{1,0:T(8,128)(2,1)S(1)}, bf16[192,2048]{1,0:T(8,128)(2,1)S(1)}, u32[]{:S(2)}, u32[]{:S(2)}) collective-permute-start(bf16[192,2048]{1,0:T(8,128)(2,1)S(1)} %copy-done.31), channel_id=1, source_target_pairs={{0,4},{2,6},{4,0},{6,2},{8,12},{10,14},{12,8},{14,10},{16,20},{18,... | collective-permute-start | bytes 2359304 | tf_op jit(solution)/shard_map/ppermute | solution.py:156
  235.4 27.8 %collective-permute-start.47 = (bf16[1024,512]{1,0:T(8,128)(2,1)S(1)}, bf16[1024,512]{1,0:T(8,128)(2,1)S(1)}, u32[]{:S(2)}, u32[]{:S(2)}) collective-permute-start(bf16[1024,512]{1,0:T(8,128)(2,1)S(1)} %collective-permute-done.42), channel_id=1, source_target_pairs={{0,8},{2,10},{4,12},{6,14},{8,16},{10,18},{12,20},{14,22},{16,24},... | collective-permute-start | bytes 3145736 | tf_op jit(solution)/shard_map/ppermute | solution.py:163
  256.7 36.2 %collective-permute-start.55 = (bf16[1024,512]{1,0:T(8,128)(2,1)}, bf16[1024,512]{1,0:T(8,128)(2,1)S(1)}, u32[]{:S(2)}, u32[]{:S(2)}) collective-permute-start(bf16[1024,512]{1,0:T(8,128)(2,1)} %fusion.39), channel_id=1, source_target_pairs={{0,8},{2,10},{4,12},{6,14},{8,16},{10,18},{12,20},{14,22},{16,24},... | collective-permute-start | bytes 3145736 | tf_op jit(solution)/shard_map/ppermute | solution.py:163
  314.4 28.1 %collective-permute-start.54 = (bf16[512,1024]{1,0:T(8,128)(2,1)}, bf16[512,1024]{1,0:T(8,128)(2,1)S(1)}, u32[]{:S(2)}, u32[]{:S(2)}) collective-permute-start(bf16[512,1024]{1,0:T(8,128)(2,1)} %fusion.42), channel_id=1, source_target_pairs={{0,8},{2,10},{4,12},{6,14},{8,16},{10,18},{12,20},{14,22},{16,24},... | collective-permute-start | bytes 3145736 | tf_op jit(solution)/shard_map/ppermute | solution.py:163
  314.4 52.4 %collective-permute-start.76 = (bf16[1024,512]{1,0:T(8,128)(2,1)}, bf16[1024,512]{1,0:T(8,128)(2,1)S(1)}, u32[]{:S(2)}, u32[]{:S(2)}) collective-permute-start(bf16[1024,512]{1,0:T(8,128)(2,1)} %add_convert_fusion.3), channel_id=1, source_target_pairs={{0,8},{2,10},{4,12},{6,14},{8,16},{10,18},{12,20},{14,22},{16,24},... | collective-permute-start | bytes 3145736 | tf_op jit(solution)/shard_map/ppermute | solution.py:163
  330.0 33.8 %collective-permute-start.69 = (bf16[192,2048]{1,0:T(8,128)(2,1)S(1)}, bf16[192,2048]{1,0:T(8,128)(2,1)S(1)}, u32[]{:S(2)}, u32[]{:S(2)}) collective-permute-start(bf16[192,2048]{1,0:T(8,128)(2,1)S(1)} %add_convert_fusion.13), channel_id=1, source_target_pairs={{0,1},{1,0},{2,3},{3,2},{4,5},{5,4},{6,7},{7,6},{8,9},{9,8},{10,11... | collective-permute-start | bytes 2359304 | tf_op jit(solution)/shard_map/ppermute | solution.py:166
  362.2 28.0 %collective-permute-start.83 = (bf16[512,1024]{1,0:T(8,128)(2,1)S(1)}, bf16[512,1024]{1,0:T(8,128)(2,1)S(1)}, u32[]{:S(2)}, u32[]{:S(2)}) collective-permute-start(bf16[512,1024]{1,0:T(8,128)(2,1)S(1)} %add_convert_fusion.2), channel_id=1, source_target_pairs={{0,8},{2,10},{4,12},{6,14},{8,16},{10,18},{12,20},{14,22},{16,24},... | collective-permute-start | bytes 3145736 | tf_op jit(solution)/shard_map/ppermute | solution.py:163
  371.5 59.1 %collective-permute-start.81 = (bf16[192,2048]{1,0:T(8,128)(2,1)}, bf16[192,2048]{1,0:T(8,128)(2,1)}, u32[]{:S(2)}, u32[]{:S(2)}) collective-permute-start(bf16[192,2048]{1,0:T(8,128)(2,1)} %add_convert_fusion.12), channel_id=1, source_target_pairs={{0,4},{2,6},{4,0},{6,2},{8,12},{10,14},{12,8},{14,10},{16,20},{18,... | collective-permute-start | bytes 2359304 | tf_op jit(solution)/shard_map/ppermute | solution.py:156
  373.0 57.6 %collective-permute-start.82 = (bf16[192,2048]{1,0:T(8,128)(2,1)}, bf16[192,2048]{1,0:T(8,128)(2,1)}, u32[]{:S(2)}, u32[]{:S(2)}) collective-permute-start(bf16[192,2048]{1,0:T(8,128)(2,1)} %add_convert_fusion.11), channel_id=1, source_target_pairs={{0,4},{2,6},{4,0},{6,2},{8,12},{10,14},{12,8},{14,10},{16,20},{18,... | collective-permute-start | bytes 2359304 | tf_op jit(solution)/shard_map/ppermute | solution.py:156
  373.6 38.4 %collective-permute-start.84 = (bf16[1024,512]{1,0:T(8,128)(2,1)}, bf16[1024,512]{1,0:T(8,128)(2,1)}, u32[]{:S(2)}, u32[]{:S(2)}) collective-permute-start(bf16[1024,512]{1,0:T(8,128)(2,1)} %add_convert_fusion.1), channel_id=1, source_target_pairs={{0,8},{2,10},{4,12},{6,14},{8,16},{10,18},{12,20},{14,22},{16,24},... | collective-permute-start | bytes 3145736 | tf_op jit(solution)/shard_map/ppermute | solution.py:163
  378.3 41.5 %collective-permute-start.77 = (bf16[512,256]{1,0:T(8,128)(2,1)}, bf16[512,256]{1,0:T(8,128)(2,1)}, u32[]{:S(2)}, u32[]{:S(2)}) collective-permute-start(bf16[512,256]{1,0:T(8,128)(2,1)} %dynamic-slice_convert_fusion.14), channel_id=1, source_target_pairs={{0,4},{2,6},{4,0},{6,2},{8,12},{10,14},{12,8},{14,10},{16,20},{18,... | collective-permute-start | bytes 786440 | tf_op jit(solution)/shard_map/ppermute | solution.py:156
  390.1 30.5 %collective-permute-start.78 = (bf16[512,256]{1,0:T(8,128)(2,1)}, bf16[512,256]{1,0:T(8,128)(2,1)S(1)}, u32[]{:S(2)}, u32[]{:S(2)}) collective-permute-start(bf16[512,256]{1,0:T(8,128)(2,1)} %dynamic-slice_convert_fusion.13), channel_id=1, source_target_pairs={{0,4},{2,6},{4,0},{6,2},{8,12},{10,14},{12,8},{14,10},{16,20},{18,... | collective-permute-start | bytes 786440 | tf_op jit(solution)/shard_map/ppermute | solution.py:156
  421.0 26.1 %collective-permute-start.88 = (bf16[512,1024]{1,0:T(8,128)(2,1)S(1)}, bf16[512,1024]{1,0:T(8,128)(2,1)S(1)}, u32[]{:S(2)}, u32[]{:S(2)}) collective-permute-start(bf16[512,1024]{1,0:T(8,128)(2,1)S(1)} %copy-done.68), channel_id=1, source_target_pairs={{0,8},{2,10},{4,12},{6,14},{8,16},{10,18},{12,20},{14,22},{16,24},... | collective-permute-start | bytes 3145736 | tf_op jit(solution)/shard_map/ppermute | solution.py:163
  433.4 24.4 %collective-permute-start.85 = (bf16[256,1536]{1,0:T(8,128)(2,1)S(1)}, bf16[256,1536]{1,0:T(8,128)(2,1)S(1)}, u32[]{:S(2)}, u32[]{:S(2)}) collective-permute-start(bf16[256,1536]{1,0:T(8,128)(2,1)S(1)} %dynamic-slice_convert_fusion.3), channel_id=1, source_target_pairs={{0,4},{2,6},{4,0},{6,2},{8,12},{10,14},{12,8},{14,10},{16,20},{18,... | collective-permute-start | bytes 2359304 | tf_op jit(solution)/shard_map/ppermute | solution.py:156
  439.7 34.7 %collective-permute-start.93 = (bf16[192,2048]{1,0:T(8,128)(2,1)S(1)}, bf16[192,2048]{1,0:T(8,128)(2,1)S(1)}, u32[]{:S(2)}, u32[]{:S(2)}) collective-permute-start(bf16[192,2048]{1,0:T(8,128)(2,1)S(1)} %add_convert_fusion.10), channel_id=1, source_target_pairs={{0,1},{1,0},{2,3},{3,2},{4,5},{5,4},{6,7},{7,6},{8,9},{9,8},{10,11... | collective-permute-start | bytes 2359304 | tf_op jit(solution)/shard_map/ppermute | solution.py:166
  447.1 29.1 %collective-permute-start.94 = (bf16[192,2048]{1,0:T(8,128)(2,1)S(1)}, bf16[192,2048]{1,0:T(8,128)(2,1)S(1)}, u32[]{:S(2)}, u32[]{:S(2)}) collective-permute-start(bf16[192,2048]{1,0:T(8,128)(2,1)S(1)} %add_convert_fusion.9), channel_id=1, source_target_pairs={{0,1},{1,0},{2,3},{3,2},{4,5},{5,4},{6,7},{7,6},{8,9},{9,8},{10,11... | collective-permute-start | bytes 2359304 | tf_op jit(solution)/shard_map/ppermute | solution.py:166
  470.5 28.3 %collective-permute-start.89 = (bf16[256,1536]{1,0:T(8,128)(2,1)S(1)}, bf16[256,1536]{1,0:T(8,128)(2,1)S(1)}, u32[]{:S(2)}, u32[]{:S(2)}) collective-permute-start(bf16[256,1536]{1,0:T(8,128)(2,1)S(1)} %add_convert_fusion.8), channel_id=1, source_target_pairs={{0,8},{2,10},{4,12},{6,14},{8,16},{10,18},{12,20},{14,22},{16,24},... | collective-permute-start | bytes 2359304 | tf_op jit(solution)/shard_map/ppermute | solution.py:163
  470.6 28.2 %collective-permute-start.91 = (bf16[256,1536]{1,0:T(8,128)(2,1)S(1)}, bf16[256,1536]{1,0:T(8,128)(2,1)S(1)}, u32[]{:S(2)}, u32[]{:S(2)}) collective-permute-start(bf16[256,1536]{1,0:T(8,128)(2,1)S(1)} %dynamic-slice_convert_fusion.2), channel_id=1, source_target_pairs={{0,4},{2,6},{4,0},{6,2},{8,12},{10,14},{12,8},{14,10},{16,20},{18,... | collective-permute-start | bytes 2359304 | tf_op jit(solution)/shard_map/ppermute | solution.py:156
  473.8 24.2 %collective-permute-start.90 = (bf16[512,256]{1,0:T(8,128)(2,1)S(1)}, bf16[512,256]{1,0:T(8,128)(2,1)S(1)}, u32[]{:S(2)}, u32[]{:S(2)}) collective-permute-start(bf16[512,256]{1,0:T(8,128)(2,1)S(1)} %add_convert_fusion.21), channel_id=1, source_target_pairs={{0,8},{2,10},{4,12},{6,14},{8,16},{10,18},{12,20},{14,22},{16,24},... | collective-permute-start | bytes 786440 | tf_op jit(solution)/shard_map/ppermute | solution.py:163
  474.4 24.4 %collective-permute-start.92 = (bf16[1024,128]{1,0:T(8,128)(2,1)S(1)}, bf16[1024,128]{1,0:T(8,128)(2,1)S(1)}, u32[]{:S(2)}, u32[]{:S(2)}) collective-permute-start(bf16[1024,128]{1,0:T(8,128)(2,1)S(1)} %get-tuple-element.1454), channel_id=1, source_target_pairs={{0,6},{2,4},{4,2},{6,0},{8,14},{10,12},{12,10},{14,8},{16,22},{18,... | collective-permute-start | bytes 786440 | tf_op jit(solution)/shard_map/ppermute | solution.py:156
  476.2 51.9 %collective-permute-start.104 = (bf16[192,2048]{1,0:T(8,128)(2,1)S(1)}, bf16[192,2048]{1,0:T(8,128)(2,1)S(1)}, u32[]{:S(2)}, u32[]{:S(2)}) collective-permute-start(bf16[192,2048]{1,0:T(8,128)(2,1)S(1)} %add_convert_fusion.7), channel_id=1, source_target_pairs={{0,1},{1,0},{2,3},{3,2},{4,5},{5,4},{6,7},{7,6},{8,9},{9,8},{10,11... | collective-permute-start | bytes 2359304 | tf_op jit(solution)/shard_map/ppermute | solution.py:166
  498.0 30.1 %collective-permute-start.105 = (bf16[192,2048]{1,0:T(8,128)(2,1)S(1)}, bf16[192,2048]{1,0:T(8,128)(2,1)S(1)}, u32[]{:S(2)}, u32[]{:S(2)}) collective-permute-start(bf16[192,2048]{1,0:T(8,128)(2,1)S(1)} %add_convert_fusion.6), channel_id=1, source_target_pairs={{0,1},{1,0},{2,3},{3,2},{4,5},{5,4},{6,7},{7,6},{8,9},{9,8},{10,11... | collective-permute-start | bytes 2359304 | tf_op jit(solution)/shard_map/ppermute | solution.py:166
  501.7 26.4 %collective-permute-start.99 = (bf16[256,1536]{1,0:T(8,128)(2,1)S(1)}, bf16[256,1536]{1,0:T(8,128)(2,1)S(1)}, u32[]{:S(2)}, u32[]{:S(2)}) collective-permute-start(bf16[256,1536]{1,0:T(8,128)(2,1)S(1)} %add_convert_fusion.5), channel_id=1, source_target_pairs={{0,8},{2,10},{4,12},{6,14},{8,16},{10,18},{12,20},{14,22},{16,24},... | collective-permute-start | bytes 2359304 | tf_op jit(solution)/shard_map/ppermute | solution.py:163
  503.0 25.1 %collective-permute-start.101 = (bf16[256,1536]{1,0:T(8,128)(2,1)S(1)}, bf16[256,1536]{1,0:T(8,128)(2,1)S(1)}, u32[]{:S(2)}, u32[]{:S(2)}) collective-permute-start(bf16[256,1536]{1,0:T(8,128)(2,1)S(1)} %dynamic-slice_convert_fusion.1), channel_id=1, source_target_pairs={{0,4},{2,6},{4,0},{6,2},{8,12},{10,14},{12,8},{14,10},{16,20},{18,... | collective-permute-start | bytes 2359304 | tf_op jit(solution)/shard_map/ppermute | solution.py:156
  530.5 26.1 %collective-permute-start.106 = (bf16[256,1536]{1,0:T(8,128)(2,1)S(1)}, bf16[256,1536]{1,0:T(8,128)(2,1)S(1)}, u32[]{:S(2)}, u32[]{:S(2)}) collective-permute-start(bf16[256,1536]{1,0:T(8,128)(2,1)S(1)} %add_convert_fusion.4), channel_id=1, source_target_pairs={{0,8},{2,10},{4,12},{6,14},{8,16},{10,18},{12,20},{14,22},{16,24},... | collective-permute-start | bytes 2359304 | tf_op jit(solution)/shard_map/ppermute | solution.py:163
  531.1 25.4 %collective-permute-start.107 = (bf16[512,256]{1,0:T(8,128)(2,1)S(1)}, bf16[512,256]{1,0:T(8,128)(2,1)S(1)}, u32[]{:S(2)}, u32[]{:S(2)}) collective-permute-start(bf16[512,256]{1,0:T(8,128)(2,1)S(1)} %add_convert_fusion.19), channel_id=1, source_target_pairs={{0,8},{2,10},{4,12},{6,14},{8,16},{10,18},{12,20},{14,22},{16,24},... | collective-permute-start | bytes 786440 | tf_op jit(solution)/shard_map/ppermute | solution.py:163
  533.4 23.2 %collective-permute-start.108 = (bf16[256,1536]{1,0:T(8,128)(2,1)S(1)}, bf16[256,1536]{1,0:T(8,128)(2,1)S(1)}, u32[]{:S(2)}, u32[]{:S(2)}) collective-permute-start(bf16[256,1536]{1,0:T(8,128)(2,1)S(1)} %dynamic-slice_convert_fusion), channel_id=1, source_target_pairs={{0,4},{2,6},{4,0},{6,2},{8,12},{10,14},{12,8},{14,10},{16,20},{18,... | collective-permute-start | bytes 2359304 | tf_op jit(solution)/shard_map/ppermute | solution.py:156
  (142 other events, 1313.8 us)

commit v6 on v5

--- a/solution.py
+++ b/solution.py
@@ -619,6 +619,9 @@
         own, far = run(lambda n, g: part_qkv(n, g, k), normed_one, grad_qkv)
         qkv_owns.append(own)
         qkv_fars.append(swap(far, 2) if k == 1 else far)
+    core_m = [links.to_core(v) for v in run(low_part_of(outer, 1), grad_qkv, qkv_full)]
+    own_m = run(part_of(outer, 0), grad_qkv, qkv_full)
+    low_m = [run(add_pieces_low, own_m[j], *wait(*core_m[j])) for j in range(2)]
     *out_fars, far_r[0], far_r[1] = wait(*out_fars, *far_r)
     low_r = [run(near_sum, near_r[j], far_r[j]) for j in range(2)]
     cross_r = [across(part) for part in low_r]
@@ -647,9 +650,6 @@
         sent = [step(qkv_sum), step(out_sum), swap(qkv_fars[k - 1], 2)]
         if k == 2:
             down_ends[3] = swap(down_ends[3], 3)
-            core_m = [links.to_core(v) for v in run(low_part_of(outer, 1), grad_qkv, qkv_full)]
-            own_m = run(part_of(outer, 0), grad_qkv, qkv_full)
-            low_m = [run(add_pieces_low, own_m[j], *wait(*core_m[j])) for j in range(2)]
             cross_m = [across(part) for part in low_m]
             *sent, down_ends[3], cross_r[0], cross_r[1] = wait(*sent, down_ends[3], *cross_r)
         elif k == 3:

time: 578 us -> 611 us (1.057)
  waiting for transfers between devices: 260 us -> 283 us
  other arithmetic: 55.1 us -> 64 us
  local copies, waits for them, and re-layouts: 70.7 us -> 79.4 us
  starting transfers between devices: 66.3 us -> 58.8 us
    ppermute x10, waiting for transfers between devices: 9.41 us -> 34.6 us  [across(): return lax.ppermute(self.order.tie(values), 'mp', [(0, 1), (1, 0)])]
  transfers between devices with their start and end apart: 114 -> 114, of which waited for: 47 -> 50; matrix products, arithmetic and copies ran while one was open for 37% -> 38% of each run, Pallas kernels for 2% -> 2%
where the time goes in v6:
time: 611 us; the launch traced here: 604 us
  waiting for transfers between devices  283 us (46%)
  matrix products  104 us (17%)
  local copies, waits for them, and re-layouts  79.4 us (13%)
  other arithmetic  64 us (10%)
  starting transfers between devices  58.8 us (10%)
  Pallas kernels  11.4 us (2%)
    ppermute x24, waiting for transfers between devices, step(): return lax.ppermute(self.order.tie(values), 'dp', self.next)  164 us
    ppermute x80, waiting for transfers between devices, swap(): return lax.ppermute(self.order.tie(values), 'dp', self.to[k])  84.1 us
    ppermute x80, starting transfers between devices, swap(): return lax.ppermute(self.order.tie(values), 'dp', self.to[k])  41.4 us
    dot_general x8, matrix products, outer(): lax.dot_general(one, two, (((1,), (1,)), ((), ())), preferred_element_typ...  39.7 us
    dot_general x16, matrix products, inner(): lax.dot_general(one, two, (((0,), (0,)), ((), ())), preferred_element_typ...  35.4 us
    ppermute x10, waiting for transfers between devices, across(): return lax.ppermute(self.order.tie(values), 'mp', [(0, 1), (1, 0)])  34.6 us
    dynamic_update_slice x34, local copies, waits for them, and re-layouts, put(): lax.dynamic_update_slice_in_dim(whole, part, index * part.shape[axis], axis)  31 us
    dot_general x8, matrix products, plain(): return jnp.dot(one, two, preferred_element_type=WIDE)  29.3 us
  transfers between devices with their start and end apart: 114, of which 50 were waited for; matrix products, arithmetic and copies ran while one was open for 38% of the time, Pallas kernels for 2%

profile of v6, /device:TPU:0, one launch (start us, length us, event | category | flops | bytes accessed | tf_op | source)
XLA Modules:
  0.0 604.5 jit_solution(14384444772192193611)
XLA Ops:
  8.0 3.1 collective-permute-start.5
  17.5 3.1 broadcast_in_dim.32
  23.0 13.6 %collective-permute-done.6 = bf16[512,256]{1,0:T(8,128)(2,1)} collective-permute-done((bf16[512,256]{1,0:T(8,128)(2,1)S(1)}, bf16[512,256]{1,0:T(8,128)(2,1)}, u32[]{:S(2)}, u32[]{:S(2)}) %collective-permute-start.6) | collective-permute-done | bytes 262176 | tf_op jit(solution)/shard_map/ppermute | solution.py:163
  47.2 17.0 %collective-permute-done.11 = bf16[512,256]{1,0:T(8,128)(2,1)} collective-permute-done((bf16[512,256]{1,0:T(8,128)(2,1)}, bf16[512,256]{1,0:T(8,128)(2,1)}, u32[]{:S(2)}, u32[]{:S(2)}) %collective-permute-start.11) | collective-permute-done | bytes 262176 | tf_op jit(solution)/shard_map/ppermute | solution.py:163
  72.0 18.0 %collective-permute-done.15 = bf16[512,256]{1,0:T(8,128)(2,1)} collective-permute-done((bf16[512,256]{1,0:T(8,128)(2,1)}, bf16[512,256]{1,0:T(8,128)(2,1)}, u32[]{:S(2)}, u32[]{:S(2)}) %collective-permute-start.15) | collective-permute-done | bytes 262176 | tf_op jit(solution)/shard_map/ppermute | solution.py:163
  100.0 15.8 %collective-permute-done.20 = bf16[1024,128]{1,0:T(8,128)(2,1)S(1)} collective-permute-done((bf16[1024,128]{1,0:T(8,128)(2,1)S(1)}, bf16[1024,128]{1,0:T(8,128)(2,1)S(1)}, u32[]{:S(2)}, u32[]{:S(2)}) %collective-permute-start.20) | collective-permute-done | bytes 262176 | tf_op jit(solution)/shard_map/ppermute | solution.py:156
  122.5 8.0 %convolution_convert_fusion.query.key.value = bf16[768,1536]{1,0:T(8,128)(2,1)S(1)} fusion(bf16[768,2048]{1,0:T(8,128)(2,1)S(1)} %pad_maximum_fusion, bf16[2048,1536]{1,0:T(8,128)(2,1)} %constant_dynamic-update-slice_fusion.28), kind=kOutput, calls=%fused_computation.19 | convolution fusion | flops 4833017856 | bytes 11796480 | tf_op jit(solution)/shard_map/dot_general | solution.py:20
  132.7 4.4 shard_map.195
  138.9 5.6 collective-permute-done.26
  171.9 8.4 %collective-permute-done.32 = bf16[512,1024]{1,0:T(8,128)(2,1)} collective-permute-done((bf16[512,1024]{1,0:T(8,128)(2,1)}, bf16[512,1024]{1,0:T(8,128)(2,1)}, u32[]{:S(2)}, u32[]{:S(2)}) %collective-permute-start.32) | collective-permute-done | bytes 1048608 | tf_op jit(solution)/shard_map/ppermute | solution.py:163
  188.2 3.1 collective-permute-done.33
  195.7 13.2 %collective-permute-done.36 = bf16[1024,512]{1,0:T(8,128)(2,1)S(1)} collective-permute-done((bf16[1024,512]{1,0:T(8,128)(2,1)}, bf16[1024,512]{1,0:T(8,128)(2,1)S(1)}, u32[]{:S(2)}, u32[]{:S(2)}) %collective-permute-start.36) | collective-permute-done | bytes 1048608 | tf_op jit(solution)/shard_map/ppermute | solution.py:163
  213.6 20.7 %collective-permute-done.42 = bf16[1024,512]{1,0:T(8,128)(2,1)S(1)} collective-permute-done((bf16[1024,512]{1,0:T(8,128)(2,1)S(1)}, bf16[1024,512]{1,0:T(8,128)(2,1)S(1)}, u32[]{:S(2)}, u32[]{:S(2)}) %collective-permute-start.42) | collective-permute-done | bytes 1048608 | tf_op jit(solution)/shard_map/ppermute | solution.py:163
  240.0 12.0 %fusion.4 = (bf16[1536,1024]{1,0:T(8,128)(2,1)}, bf16[1536,1024]{1,0:T(8,128)(2,1)S(1)}) fusion(bf16[1536,2048]{1,0:T(8,128)(2,1)S(1)} %maximum_dynamic-update-slice_fusion, bf16[2048,1024]{1,0:T(8,128)(2,1)} %constant_dynamic-update-slice_fusion.16), kind=kOutput, calls=%fused_computation.5 | convolution fusion | flops 6459752448 | bytes 16777216 | tf_op jit(solution)/shard_map/dot_general | solution.py:20
  253.7 3.0 fusion.39
  256.7 6.5 %collective-permute-done.47 = bf16[1024,512]{1,0:T(8,128)(2,1)S(1)} collective-permute-done((bf16[1024,512]{1,0:T(8,128)(2,1)S(1)}, bf16[1024,512]{1,0:T(8,128)(2,1)S(1)}, u32[]{:S(2)}, u32[]{:S(2)}) %collective-permute-start.47) | collective-permute-done | bytes 1048608 | tf_op jit(solution)/shard_map/ppermute | solution.py:163
  263.4 10.3 %multiply_convert_fusion = bf16[1536,1024]{1,0:T(8,128)(2,1)} fusion(bf16[1536,1024]{1,0:T(8,128)(2,1)} %get-tuple-element.1150, bf16[1536,2048]{1,0:T(8,128)(2,1)S(1)} %maximum_dynamic-update-slice_fusion.1, bf16[1024,2048]{1,0:T(8,128)(2,1)S(1)} %constant_dynamic-update-slice_fusion.2), kind=kOutput, calls=%fused_computation.6 | convolution fusion | flops 6447169536 | bytes 16777216 | tf_op jit(solution)/shard_map/dot_general | solution.py:28
  273.8 4.3 convolution_convert_fusion.4
  279.9 4.0 fusion.83
  292.9 2.9 add_convert_fusion.3
  295.8 4.0 convolution_convert_fusion.3
  300.0 4.0 fusion.80
  309.1 2.9 collective-permute-done.58
  314.7 13.4 %collective-permute-done.62 = bf16[192,2048]{1,0:T(8,128)(2,1)} collective-permute-done((bf16[192,2048]{1,0:T(8,128)(2,1)}, bf16[192,2048]{1,0:T(8,128)(2,1)}, u32[]{:S(2)}, u32[]{:S(2)}) %collective-permute-start.62) | collective-permute-done | bytes 786464 | tf_op jit(solution)/shard_map/ppermute | solution.py:156
  333.2 3.5 fusion.109
  336.7 5.7 collective-permute-done.54
  342.4 3.2 add_convert_fusion.2
  367.2 4.3 add_convert_fusion.1
  384.0 6.1 %collective-permute-done.83 = bf16[512,1024]{1,0:T(8,128)(2,1)S(1)} collective-permute-done((bf16[512,1024]{1,0:T(8,128)(2,1)S(1)}, bf16[512,1024]{1,0:T(8,128)(2,1)S(1)}, u32[]{:S(2)}, u32[]{:S(2)}) %collective-permute-start.83) | collective-permute-done | bytes 1048608 | tf_op jit(solution)/shard_map/ppermute | solution.py:163
  390.1 4.2 add_convert_fusion
  398.6 7.0 %shard_map.196 = (bf16[768,512]{1,0:T(8,128)(2,1)S(1)}, bf16[768,512]{1,0:T(8,128)(2,1)S(1)}, bf16[768,512]{1,0:T(8,128)(2,1)S(1)}) custom-call(bf16[768,1536]{1,0:T(8,128)(2,1)S(1)} %convolution_convert_fusion.query.key.value, bf16[768,1536]{1,0:T(8,128)(2,1)S(1)} %convolution_convert_fusion.query.key.value, ...), custom_call_target="tpu_custom_call" | custom-call | tf_op jit(solution)/shard_map/pallas_call | solution.py:103
  405.8 6.1 %collective-permute-done.84 = bf16[1024,512]{1,0:T(8,128)(2,1)} collective-permute-done((bf16[1024,512]{1,0:T(8,128)(2,1)}, bf16[1024,512]{1,0:T(8,128)(2,1)}, u32[]{:S(2)}, u32[]{:S(2)}) %collective-permute-start.84) | collective-permute-done | bytes 1048608 | tf_op jit(solution)/shard_map/ppermute | solution.py:163
  423.5 5.4 convolution_convert_fusion.5
  429.0 5.0 fusion.55
  441.7 5.5 collective-permute-done.78
  447.3 5.6 collective-permute-done.79
  454.4 4.1 collective-permute-done.80
  463.3 3.7 convert_add_fusion.2
  473.5 3.2 convert_add_fusion.1
  484.0 25.0 %collective-permute-done.94 = bf16[512,256]{1,0:T(8,128)(2,1)} collective-permute-done((bf16[512,256]{1,0:T(8,128)(2,1)S(1)}, bf16[512,256]{1,0:T(8,128)(2,1)}, u32[]{:S(2)}, u32[]{:S(2)}) %collective-permute-start.94) | collective-permute-done | bytes 262176 | tf_op jit(solution)/shard_map/ppermute | solution.py:163
  509.0 8.8 %collective-permute-done.96 = bf16[1024,128]{1,0:T(8,128)(2,1)} collective-permute-done((bf16[1024,128]{1,0:T(8,128)(2,1)}, bf16[1024,128]{1,0:T(8,128)(2,1)}, u32[]{:S(2)}, u32[]{:S(2)}) %collective-permute-start.96) | collective-permute-done | bytes 262176 | tf_op jit(solution)/shard_map/ppermute | solution.py:156
  523.1 4.4 maximum_add_fusion
  528.6 9.6 %collective-permute-done.104 = bf16[192,2048]{1,0:T(8,128)(2,1)S(1)} collective-permute-done((bf16[192,2048]{1,0:T(8,128)(2,1)S(1)}, bf16[192,2048]{1,0:T(8,128)(2,1)S(1)}, u32[]{:S(2)}, u32[]{:S(2)}) %collective-permute-start.104) | collective-permute-done | bytes 786464 | tf_op jit(solution)/shard_map/ppermute | solution.py:166
  538.2 16.0 %collective-permute-done.105 = bf16[192,2048]{1,0:T(8,128)(2,1)S(1)} collective-permute-done((bf16[192,2048]{1,0:T(8,128)(2,1)S(1)}, bf16[192,2048]{1,0:T(8,128)(2,1)S(1)}, u32[]{:S(2)}, u32[]{:S(2)}) %collective-permute-start.105) | collective-permute-done | bytes 786464 | tf_op jit(solution)/shard_map/ppermute | solution.py:166
  555.4 6.3 %collective-permute-done.103 = bf16[128,1024]{1,0:T(8,128)(2,1)S(1)} collective-permute-done((bf16[128,1024]{1,0:T(8,128)(2,1)S(1)}, bf16[128,1024]{1,0:T(8,128)(2,1)S(1)}, u32[]{:S(2)}, u32[]{:S(2)}) %collective-permute-start.103) | collective-permute-done | bytes 262176 | tf_op jit(solution)/shard_map/ppermute | solution.py:156
  565.2 4.8 fusion.14
  570.0 19.4 %collective-permute-done.107 = bf16[512,256]{1,0:T(8,128)(2,1)S(1)} collective-permute-done((bf16[512,256]{1,0:T(8,128)(2,1)S(1)}, bf16[512,256]{1,0:T(8,128)(2,1)S(1)}, u32[]{:S(2)}, u32[]{:S(2)}) %collective-permute-start.107) | collective-permute-done | bytes 262176 | tf_op jit(solution)/shard_map/ppermute | solution.py:163
  593.2 3.3 collective-permute-done.113
  (611 shorter events, 229.5 us)
Async XLA Ops:
  8.0 28.6 %collective-permute-start.5 = (bf16[256,1536]{1,0:T(8,128)(2,1)S(1)}, bf16[256,1536]{1,0:T(8,128)(2,1)}, u32[]{:S(2)}, u32[]{:S(2)}) collective-permute-start(bf16[256,1536]{1,0:T(8,128)(2,1)S(1)} %maximum_select_fusion), channel_id=1, source_target_pairs={{0,8},{2,10},{4,12},{6,14},{8,16},{10,18},{12,20},{14,22},{16,24},... | collective-permute-start | bytes 2359304 | tf_op jit(solution)/shard_map/ppermute | solution.py:163
  11.1 25.5 %collective-permute-start.7 = (bf16[256,1536]{1,0:T(8,128)(2,1)S(1)}, bf16[256,1536]{1,0:T(8,128)(2,1)S(1)}, u32[]{:S(2)}, u32[]{:S(2)}) collective-permute-start(bf16[256,1536]{1,0:T(8,128)(2,1)S(1)} %maximum_select_fusion), channel_id=1, source_target_pairs={{0,4},{2,6},{4,0},{6,2},{8,12},{10,14},{12,8},{14,10},{16,20},{18,... | collective-permute-start | bytes 2359304 | tf_op jit(solution)/shard_map/ppermute | solution.py:156
  37.5 26.7 %collective-permute-start.10 = (bf16[256,1536]{1,0:T(8,128)(2,1)}, bf16[256,1536]{1,0:T(8,128)(2,1)}, u32[]{:S(2)}, u32[]{:S(2)}) collective-permute-start(bf16[256,1536]{1,0:T(8,128)(2,1)} %collective-permute-done.5), channel_id=1, source_target_pairs={{0,8},{2,10},{4,12},{6,14},{8,16},{10,18},{12,20},{14,22},{16,24},... | collective-permute-start | bytes 2359304 | tf_op jit(solution)/shard_map/ppermute | solution.py:163
  38.4 25.8 %collective-permute-start.12 = (bf16[256,1536]{1,0:T(8,128)(2,1)}, bf16[256,1536]{1,0:T(8,128)(2,1)}, u32[]{:S(2)}, u32[]{:S(2)}) collective-permute-start(bf16[256,1536]{1,0:T(8,128)(2,1)} %collective-permute-done.5), channel_id=1, source_target_pairs={{0,4},{2,6},{4,0},{6,2},{8,12},{10,14},{12,8},{14,10},{16,20},{18,... | collective-permute-start | bytes 2359304 | tf_op jit(solution)/shard_map/ppermute | solution.py:156
  41.2 53.6 %collective-permute-start.2 = (bf16[384,2048]{1,0:T(8,128)(2,1)}, bf16[384,2048]{1,0:T(8,128)(2,1)S(1)}, u32[]{:S(2)}, u32[]{:S(2)}) collective-permute-start(bf16[384,2048]{1,0:T(8,128)(2,1)} %fusion.17), channel_id=1, source_target_pairs={{0,2},{2,0},{4,6},{6,4},{8,10},{10,8},{12,14},{14,12},{16,18},{18,... | collective-permute-start | bytes 4718600 | tf_op jit(solution)/shard_map/ppermute | solution.py:156
  41.2 23.0 %collective-permute-start.11 = (bf16[512,256]{1,0:T(8,128)(2,1)}, bf16[512,256]{1,0:T(8,128)(2,1)}, u32[]{:S(2)}, u32[]{:S(2)}) collective-permute-start(bf16[512,256]{1,0:T(8,128)(2,1)} %collective-permute-done.6), channel_id=1, source_target_pairs={{0,8},{2,10},{4,12},{6,14},{8,16},{10,18},{12,20},{14,22},{16,24},... | collective-permute-start | bytes 786440 | tf_op jit(solution)/shard_map/ppermute | solution.py:163
  64.2 26.3 %collective-permute-start.14 = (bf16[256,1536]{1,0:T(8,128)(2,1)}, bf16[256,1536]{1,0:T(8,128)(2,1)S(1)}, u32[]{:S(2)}, u32[]{:S(2)}) collective-permute-start(bf16[256,1536]{1,0:T(8,128)(2,1)} %collective-permute-done.10), channel_id=1, source_target_pairs={{0,8},{2,10},{4,12},{6,14},{8,16},{10,18},{12,20},{14,22},{16,24},... | collective-permute-start | bytes 2359304 | tf_op jit(solution)/shard_map/ppermute | solution.py:163
  64.3 26.2 %collective-permute-start.16 = (bf16[256,1536]{1,0:T(8,128)(2,1)}, bf16[256,1536]{1,0:T(8,128)(2,1)S(1)}, u32[]{:S(2)}, u32[]{:S(2)}) collective-permute-start(bf16[256,1536]{1,0:T(8,128)(2,1)} %collective-permute-done.10), channel_id=1, source_target_pairs={{0,4},{2,6},{4,0},{6,2},{8,12},{10,14},{12,8},{14,10},{16,20},{18,... | collective-permute-start | bytes 2359304 | tf_op jit(solution)/shard_map/ppermute | solution.py:156
  90.5 27.1 %collective-permute-start.18 = (bf16[512,1024]{1,0:T(8,128)(2,1)S(1)}, bf16[512,1024]{1,0:T(8,128)(2,1)}, u32[]{:S(2)}, u32[]{:S(2)}) collective-permute-start(bf16[512,1024]{1,0:T(8,128)(2,1)S(1)} %constant_dynamic-update-slice_fusion.34), channel_id=1, source_target_pairs={{0,8},{2,10},{4,12},{6,14},{8,16},{10,18},{12,20},{14,22},{16,24},... | collective-permute-start | bytes 3145736 | tf_op jit(solution)/shard_map/ppermute | solution.py:163
  90.5 25.2 %collective-permute-start.19 = (bf16[256,1536]{1,0:T(8,128)(2,1)S(1)}, bf16[256,1536]{1,0:T(8,128)(2,1)S(1)}, u32[]{:S(2)}, u32[]{:S(2)}) collective-permute-start(bf16[256,1536]{1,0:T(8,128)(2,1)S(1)} %collective-permute-done.14), channel_id=1, source_target_pairs={{0,4},{2,6},{4,0},{6,2},{8,12},{10,14},{12,8},{14,10},{16,20},{18,... | collective-permute-start | bytes 2359304 | tf_op jit(solution)/shard_map/ppermute | solution.py:156
  118.5 26.9 %collective-permute-start.22 = (bf16[512,1024]{1,0:T(8,128)(2,1)}, bf16[512,1024]{1,0:T(8,128)(2,1)}, u32[]{:S(2)}, u32[]{:S(2)}) collective-permute-start(bf16[512,1024]{1,0:T(8,128)(2,1)} %collective-permute-done.18), channel_id=1, source_target_pairs={{0,8},{2,10},{4,12},{6,14},{8,16},{10,18},{12,20},{14,22},{16,24},... | collective-permute-start | bytes 3145736 | tf_op jit(solution)/shard_map/ppermute | solution.py:163
  121.2 23.3 %collective-permute-start.26 = (bf16[512,256]{1,0:T(8,128)(2,1)}, bf16[512,256]{1,0:T(8,128)(2,1)}, u32[]{:S(2)}, u32[]{:S(2)}) collective-permute-start(bf16[512,256]{1,0:T(8,128)(2,1)} %collective-permute-done.15), channel_id=1, source_target_pairs={{0,4},{2,6},{4,0},{6,2},{8,12},{10,14},{12,8},{14,10},{16,20},{18,... | collective-permute-start | bytes 786440 | tf_op jit(solution)/shard_map/ppermute | solution.py:156
  137.1 57.6 %collective-permute-start.37 = (bf16[384,2048]{1,0:T(8,128)(2,1)S(1)}, bf16[384,2048]{1,0:T(8,128)(2,1)}, u32[]{:S(2)}, u32[]{:S(2)}) collective-permute-start(bf16[384,2048]{1,0:T(8,128)(2,1)S(1)} %copy-done.21), channel_id=1, source_target_pairs={{0,2},{2,0},{4,6},{6,4},{8,10},{10,8},{12,14},{14,12},{16,18},{18,... | collective-permute-start | bytes 4718600 | tf_op jit(solution)/shard_map/ppermute | solution.py:156
  152.9 27.3 %collective-permute-start.32 = (bf16[512,1024]{1,0:T(8,128)(2,1)}, bf16[512,1024]{1,0:T(8,128)(2,1)}, u32[]{:S(2)}, u32[]{:S(2)}) collective-permute-start(bf16[512,1024]{1,0:T(8,128)(2,1)} %collective-permute-done.22), channel_id=1, source_target_pairs={{0,8},{2,10},{4,12},{6,14},{8,16},{10,18},{12,20},{14,22},{16,24},... | collective-permute-start | bytes 3145736 | tf_op jit(solution)/shard_map/ppermute | solution.py:163
  153.5 42.0 %collective-permute-start.38 = (bf16[192,2048]{1,0:T(8,128)(2,1)}, bf16[192,2048]{1,0:T(8,128)(2,1)}, u32[]{:S(2)}, u32[]{:S(2)}) collective-permute-start(bf16[192,2048]{1,0:T(8,128)(2,1)} %get-tuple-element.1241), channel_id=1, source_target_pairs={{0,4},{2,6},{4,0},{6,2},{8,12},{10,14},{12,8},{14,10},{16,20},{18,... | collective-permute-start | bytes 2359304 | tf_op jit(solution)/shard_map/ppermute | solution.py:156
  155.0 27.5 %collective-permute-start.29 = (bf16[192,2048]{1,0:T(8,128)(2,1)S(1)}, bf16[192,2048]{1,0:T(8,128)(2,1)S(1)}, u32[]{:S(2)}, u32[]{:S(2)}) collective-permute-start(bf16[192,2048]{1,0:T(8,128)(2,1)S(1)} %add_convert_fusion.18), channel_id=1, source_target_pairs={{0,1},{1,0},{2,3},{3,2},{4,5},{5,4},{6,7},{7,6},{8,9},{9,8},{10,11... | collective-permute-start | bytes 2359304 | tf_op jit(solution)/shard_map/ppermute | solution.py:166
  182.5 26.4 %collective-permute-start.36 = (bf16[1024,512]{1,0:T(8,128)(2,1)}, bf16[1024,512]{1,0:T(8,128)(2,1)S(1)}, u32[]{:S(2)}, u32[]{:S(2)}) collective-permute-start(bf16[1024,512]{1,0:T(8,128)(2,1)} %constant_dynamic-update-slice_fusion.21), channel_id=1, source_target_pairs={{0,8},{2,10},{4,12},{6,14},{8,16},{10,18},{12,20},{14,22},{16,24},... | collective-permute-start | bytes 3145736 | tf_op jit(solution)/shard_map/ppermute | solution.py:163
  186.8 25.2 %collective-permute-start.34 = (bf16[192,2048]{1,0:T(8,128)(2,1)S(1)}, bf16[192,2048]{1,0:T(8,128)(2,1)S(1)}, u32[]{:S(2)}, u32[]{:S(2)}) collective-permute-start(bf16[192,2048]{1,0:T(8,128)(2,1)S(1)} %get-tuple-element.1060), channel_id=1, source_target_pairs={{0,4},{2,6},{4,0},{6,2},{8,12},{10,14},{12,8},{14,10},{16,20},{18,... | collective-permute-start | bytes 2359304 | tf_op jit(solution)/shard_map/ppermute | solution.py:156
  194.7 39.8 %collective-permute-start.39 = (bf16[192,2048]{1,0:T(8,128)(2,1)S(1)}, bf16[192,2048]{1,0:T(8,128)(2,1)S(1)}, u32[]{:S(2)}, u32[]{:S(2)}) collective-permute-start(bf16[192,2048]{1,0:T(8,128)(2,1)S(1)} %get-tuple-element.1085), channel_id=1, source_target_pairs={{0,4},{2,6},{4,0},{6,2},{8,12},{10,14},{12,8},{14,10},{16,20},{18,... | collective-permute-start | bytes 2359304 | tf_op jit(solution)/shard_map/ppermute | solution.py:156
  195.5 39.0 %collective-permute-start.40 = (bf16[192,2048]{1,0:T(8,128)(2,1)S(1)}, bf16[192,2048]{1,0:T(8,128)(2,1)S(1)}, u32[]{:S(2)}, u32[]{:S(2)}) collective-permute-start(bf16[192,2048]{1,0:T(8,128)(2,1)S(1)} %get-tuple-element.1085), channel_id=1, source_target_pairs={{0,2},{2,0},{4,6},{6,4},{8,10},{10,8},{12,14},{14,12},{16,18},{18,... | collective-permute-start | bytes 2359304 | tf_op jit(solution)/shard_map/ppermute | solution.py:156
  208.9 25.4 %collective-permute-start.42 = (bf16[1024,512]{1,0:T(8,128)(2,1)S(1)}, bf16[1024,512]{1,0:T(8,128)(2,1)S(1)}, u32[]{:S(2)}, u32[]{:S(2)}) collective-permute-start(bf16[1024,512]{1,0:T(8,128)(2,1)S(1)} %collective-permute-done.36), channel_id=1, source_target_pairs={{0,8},{2,10},{4,12},{6,14},{8,16},{10,18},{12,20},{14,22},{16,24},... | collective-permute-start | bytes 3145736 | tf_op jit(solution)/shard_map/ppermute | solution.py:163
  212.1 22.5 %collective-permute-start.41 = (bf16[192,2048]{1,0:T(8,128)(2,1)S(1)}, bf16[192,2048]{1,0:T(8,128)(2,1)S(1)}, u32[]{:S(2)}, u32[]{:S(2)}) collective-permute-start(bf16[192,2048]{1,0:T(8,128)(2,1)S(1)} %collective-permute-done.34), channel_id=1, source_target_pairs={{0,2},{2,0},{4,6},{6,4},{8,10},{10,8},{12,14},{14,12},{16,18},{18,... | collective-permute-start | bytes 2359304 | tf_op jit(solution)/shard_map/ppermute | solution.py:156
  212.3 27.1 %collective-permute-start.45 = (bf16[192,2048]{1,0:T(8,128)(2,1)S(1)}, bf16[192,2048]{1,0:T(8,128)(2,1)S(1)}, u32[]{:S(2)}, u32[]{:S(2)}) collective-permute-start(bf16[192,2048]{1,0:T(8,128)(2,1)S(1)} %copy-done.32), channel_id=1, source_target_pairs={{0,4},{2,6},{4,0},{6,2},{8,12},{10,14},{12,8},{14,10},{16,20},{18,... | collective-permute-start | bytes 2359304 | tf_op jit(solution)/shard_map/ppermute | solution.py:156
  235.5 27.8 %collective-permute-start.47 = (bf16[1024,512]{1,0:T(8,128)(2,1)S(1)}, bf16[1024,512]{1,0:T(8,128)(2,1)S(1)}, u32[]{:S(2)}, u32[]{:S(2)}) collective-permute-start(bf16[1024,512]{1,0:T(8,128)(2,1)S(1)} %collective-permute-done.42), channel_id=1, source_target_pairs={{0,8},{2,10},{4,12},{6,14},{8,16},{10,18},{12,20},{14,22},{16,24},... | collective-permute-start | bytes 3145736 | tf_op jit(solution)/shard_map/ppermute | solution.py:163
  256.7 36.2 %collective-permute-start.55 = (bf16[1024,512]{1,0:T(8,128)(2,1)}, bf16[1024,512]{1,0:T(8,128)(2,1)S(1)}, u32[]{:S(2)}, u32[]{:S(2)}) collective-permute-start(bf16[1024,512]{1,0:T(8,128)(2,1)} %fusion.39), channel_id=1, source_target_pairs={{0,8},{2,10},{4,12},{6,14},{8,16},{10,18},{12,20},{14,22},{16,24},... | collective-permute-start | bytes 3145736 | tf_op jit(solution)/shard_map/ppermute | solution.py:163
  314.3 28.1 %collective-permute-start.54 = (bf16[512,1024]{1,0:T(8,128)(2,1)}, bf16[512,1024]{1,0:T(8,128)(2,1)S(1)}, u32[]{:S(2)}, u32[]{:S(2)}) collective-permute-start(bf16[512,1024]{1,0:T(8,128)(2,1)} %fusion.42), channel_id=1, source_target_pairs={{0,8},{2,10},{4,12},{6,14},{8,16},{10,18},{12,20},{14,22},{16,24},... | collective-permute-start | bytes 3145736 | tf_op jit(solution)/shard_map/ppermute | solution.py:163
  314.3 52.4 %collective-permute-start.76 = (bf16[1024,512]{1,0:T(8,128)(2,1)}, bf16[1024,512]{1,0:T(8,128)(2,1)S(1)}, u32[]{:S(2)}, u32[]{:S(2)}) collective-permute-start(bf16[1024,512]{1,0:T(8,128)(2,1)} %add_convert_fusion.3), channel_id=1, source_target_pairs={{0,8},{2,10},{4,12},{6,14},{8,16},{10,18},{12,20},{14,22},{16,24},... | collective-permute-start | bytes 3145736 | tf_op jit(solution)/shard_map/ppermute | solution.py:163
  330.0 33.7 %collective-permute-start.69 = (bf16[192,2048]{1,0:T(8,128)(2,1)S(1)}, bf16[192,2048]{1,0:T(8,128)(2,1)S(1)}, u32[]{:S(2)}, u32[]{:S(2)}) collective-permute-start(bf16[192,2048]{1,0:T(8,128)(2,1)S(1)} %add_convert_fusion.13), channel_id=1, source_target_pairs={{0,1},{1,0},{2,3},{3,2},{4,5},{5,4},{6,7},{7,6},{8,9},{9,8},{10,11... | collective-permute-start | bytes 2359304 | tf_op jit(solution)/shard_map/ppermute | solution.py:166
  362.2 28.0 %collective-permute-start.83 = (bf16[512,1024]{1,0:T(8,128)(2,1)S(1)}, bf16[512,1024]{1,0:T(8,128)(2,1)S(1)}, u32[]{:S(2)}, u32[]{:S(2)}) collective-permute-start(bf16[512,1024]{1,0:T(8,128)(2,1)S(1)} %add_convert_fusion.2), channel_id=1, source_target_pairs={{0,8},{2,10},{4,12},{6,14},{8,16},{10,18},{12,20},{14,22},{16,24},... | collective-permute-start | bytes 3145736 | tf_op jit(solution)/shard_map/ppermute | solution.py:163
  371.4 87.1 %collective-permute-start.81 = (bf16[192,2048]{1,0:T(8,128)(2,1)}, bf16[192,2048]{1,0:T(8,128)(2,1)}, u32[]{:S(2)}, u32[]{:S(2)}) collective-permute-start(bf16[192,2048]{1,0:T(8,128)(2,1)} %add_convert_fusion.12), channel_id=1, source_target_pairs={{0,4},{2,6},{4,0},{6,2},{8,12},{10,14},{12,8},{14,10},{16,20},{18,... | collective-permute-start | bytes 2359304 | tf_op jit(solution)/shard_map/ppermute | solution.py:156
  373.0 85.6 %collective-permute-start.82 = (bf16[192,2048]{1,0:T(8,128)(2,1)}, bf16[192,2048]{1,0:T(8,128)(2,1)}, u32[]{:S(2)}, u32[]{:S(2)}) collective-permute-start(bf16[192,2048]{1,0:T(8,128)(2,1)} %add_convert_fusion.11), channel_id=1, source_target_pairs={{0,4},{2,6},{4,0},{6,2},{8,12},{10,14},{12,8},{14,10},{16,20},{18,... | collective-permute-start | bytes 2359304 | tf_op jit(solution)/shard_map/ppermute | solution.py:156
  373.5 38.4 %collective-permute-start.84 = (bf16[1024,512]{1,0:T(8,128)(2,1)}, bf16[1024,512]{1,0:T(8,128)(2,1)}, u32[]{:S(2)}, u32[]{:S(2)}) collective-permute-start(bf16[1024,512]{1,0:T(8,128)(2,1)} %add_convert_fusion.1), channel_id=1, source_target_pairs={{0,8},{2,10},{4,12},{6,14},{8,16},{10,18},{12,20},{14,22},{16,24},... | collective-permute-start | bytes 3145736 | tf_op jit(solution)/shard_map/ppermute | solution.py:163
  378.1 61.9 %collective-permute-start.77 = (bf16[512,256]{1,0:T(8,128)(2,1)}, bf16[512,256]{1,0:T(8,128)(2,1)}, u32[]{:S(2)}, u32[]{:S(2)}) collective-permute-start(bf16[512,256]{1,0:T(8,128)(2,1)} %dynamic-slice_convert_fusion.14), channel_id=1, source_target_pairs={{0,4},{2,6},{4,0},{6,2},{8,12},{10,14},{12,8},{14,10},{16,20},{18,... | collective-permute-start | bytes 786440 | tf_op jit(solution)/shard_map/ppermute | solution.py:156
  447.3 25.4 %collective-permute-start.92 = (bf16[512,1024]{1,0:T(8,128)(2,1)S(1)}, bf16[512,1024]{1,0:T(8,128)(2,1)S(1)}, u32[]{:S(2)}, u32[]{:S(2)}) collective-permute-start(bf16[512,1024]{1,0:T(8,128)(2,1)S(1)} %copy-done.84), channel_id=1, source_target_pairs={{0,8},{2,10},{4,12},{6,14},{8,16},{10,18},{12,20},{14,22},{16,24},... | collective-permute-start | bytes 3145736 | tf_op jit(solution)/shard_map/ppermute | solution.py:163
  452.9 27.3 %collective-permute-start.89 = (bf16[256,1536]{1,0:T(8,128)(2,1)S(1)}, bf16[256,1536]{1,0:T(8,128)(2,1)S(1)}, u32[]{:S(2)}, u32[]{:S(2)}) collective-permute-start(bf16[256,1536]{1,0:T(8,128)(2,1)S(1)} %dynamic-slice_convert_fusion.3), channel_id=1, source_target_pairs={{0,4},{2,6},{4,0},{6,2},{8,12},{10,14},{12,8},{14,10},{16,20},{18,... | collective-permute-start | bytes 2359304 | tf_op jit(solution)/shard_map/ppermute | solution.py:156
  470.3 48.2 %collective-permute-start.97 = (bf16[192,2048]{1,0:T(8,128)(2,1)}, bf16[192,2048]{1,0:T(8,128)(2,1)}, u32[]{:S(2)}, u32[]{:S(2)}) collective-permute-start(bf16[192,2048]{1,0:T(8,128)(2,1)} %add_convert_fusion.8), channel_id=1, source_target_pairs={{0,1},{1,0},{2,3},{3,2},{4,5},{5,4},{6,7},{7,6},{8,9},{9,8},{10,11... | collective-permute-start | bytes 2359304 | tf_op jit(solution)/shard_map/ppermute | solution.py:166
  472.7 47.2 %collective-permute-start.98 = (bf16[192,2048]{1,0:T(8,128)(2,1)}, bf16[192,2048]{1,0:T(8,128)(2,1)}, u32[]{:S(2)}, u32[]{:S(2)}) collective-permute-start(bf16[192,2048]{1,0:T(8,128)(2,1)} %add_convert_fusion.7), channel_id=1, source_target_pairs={{0,1},{1,0},{2,3},{3,2},{4,5},{5,4},{6,7},{7,6},{8,9},{9,8},{10,11... | collective-permute-start | bytes 2359304 | tf_op jit(solution)/shard_map/ppermute | solution.py:166
  482.3 37.5 %collective-permute-start.93 = (bf16[256,1536]{1,0:T(8,128)(2,1)}, bf16[256,1536]{1,0:T(8,128)(2,1)}, u32[]{:S(2)}, u32[]{:S(2)}) collective-permute-start(bf16[256,1536]{1,0:T(8,128)(2,1)} %add_convert_fusion.6), channel_id=1, source_target_pairs={{0,8},{2,10},{4,12},{6,14},{8,16},{10,18},{12,20},{14,22},{16,24},... | collective-permute-start | bytes 2359304 | tf_op jit(solution)/shard_map/ppermute | solution.py:163
  482.4 37.5 %collective-permute-start.95 = (bf16[256,1536]{1,0:T(8,128)(2,1)}, bf16[256,1536]{1,0:T(8,128)(2,1)}, u32[]{:S(2)}, u32[]{:S(2)}) collective-permute-start(bf16[256,1536]{1,0:T(8,128)(2,1)} %dynamic-slice_convert_fusion.2), channel_id=1, source_target_pairs={{0,4},{2,6},{4,0},{6,2},{8,12},{10,14},{12,8},{14,10},{16,20},{18,... | collective-permute-start | bytes 2359304 | tf_op jit(solution)/shard_map/ppermute | solution.py:156
  484.0 25.0 %collective-permute-start.94 = (bf16[512,256]{1,0:T(8,128)(2,1)S(1)}, bf16[512,256]{1,0:T(8,128)(2,1)}, u32[]{:S(2)}, u32[]{:S(2)}) collective-permute-start(bf16[512,256]{1,0:T(8,128)(2,1)S(1)} %add_convert_fusion.21), channel_id=1, source_target_pairs={{0,8},{2,10},{4,12},{6,14},{8,16},{10,18},{12,20},{14,22},{16,24},... | collective-permute-start | bytes 786440 | tf_op jit(solution)/shard_map/ppermute | solution.py:163
  518.5 35.7 %collective-permute-start.105 = (bf16[192,2048]{1,0:T(8,128)(2,1)S(1)}, bf16[192,2048]{1,0:T(8,128)(2,1)S(1)}, u32[]{:S(2)}, u32[]{:S(2)}) collective-permute-start(bf16[192,2048]{1,0:T(8,128)(2,1)S(1)} %add_convert_fusion.9), channel_id=1, source_target_pairs={{0,1},{1,0},{2,3},{3,2},{4,5},{5,4},{6,7},{7,6},{8,9},{9,8},{10,11... | collective-permute-start | bytes 2359304 | tf_op jit(solution)/shard_map/ppermute | solution.py:166
  527.5 34.2 %collective-permute-start.99 = (bf16[256,1536]{1,0:T(8,128)(2,1)S(1)}, bf16[256,1536]{1,0:T(8,128)(2,1)S(1)}, u32[]{:S(2)}, u32[]{:S(2)}) collective-permute-start(bf16[256,1536]{1,0:T(8,128)(2,1)S(1)} %add_convert_fusion.5), channel_id=1, source_target_pairs={{0,8},{2,10},{4,12},{6,14},{8,16},{10,18},{12,20},{14,22},{16,24},... | collective-permute-start | bytes 2359304 | tf_op jit(solution)/shard_map/ppermute | solution.py:163
  527.6 27.8 %collective-permute-start.100 = (bf16[512,256]{1,0:T(8,128)(2,1)S(1)}, bf16[512,256]{1,0:T(8,128)(2,1)S(1)}, u32[]{:S(2)}, u32[]{:S(2)}) collective-permute-start(bf16[512,256]{1,0:T(8,128)(2,1)S(1)} %add_convert_fusion.20), channel_id=1, source_target_pairs={{0,8},{2,10},{4,12},{6,14},{8,16},{10,18},{12,20},{14,22},{16,24},... | collective-permute-start | bytes 786440 | tf_op jit(solution)/shard_map/ppermute | solution.py:163
  527.6 34.0 %collective-permute-start.101 = (bf16[256,1536]{1,0:T(8,128)(2,1)S(1)}, bf16[256,1536]{1,0:T(8,128)(2,1)S(1)}, u32[]{:S(2)}, u32[]{:S(2)}) collective-permute-start(bf16[256,1536]{1,0:T(8,128)(2,1)S(1)} %copy-done.53), channel_id=1, source_target_pairs={{0,4},{2,6},{4,0},{6,2},{8,12},{10,14},{12,8},{14,10},{16,20},{18,... | collective-permute-start | bytes 2359304 | tf_op jit(solution)/shard_map/ppermute | solution.py:156
  564.1 25.3 %collective-permute-start.106 = (bf16[256,1536]{1,0:T(8,128)(2,1)S(1)}, bf16[256,1536]{1,0:T(8,128)(2,1)S(1)}, u32[]{:S(2)}, u32[]{:S(2)}) collective-permute-start(bf16[256,1536]{1,0:T(8,128)(2,1)S(1)} %add_convert_fusion.4), channel_id=1, source_target_pairs={{0,8},{2,10},{4,12},{6,14},{8,16},{10,18},{12,20},{14,22},{16,24},... | collective-permute-start | bytes 2359304 | tf_op jit(solution)/shard_map/ppermute | solution.py:163
  564.2 25.2 %collective-permute-start.107 = (bf16[512,256]{1,0:T(8,128)(2,1)S(1)}, bf16[512,256]{1,0:T(8,128)(2,1)S(1)}, u32[]{:S(2)}, u32[]{:S(2)}) collective-permute-start(bf16[512,256]{1,0:T(8,128)(2,1)S(1)} %add_convert_fusion.19), channel_id=1, source_target_pairs={{0,8},{2,10},{4,12},{6,14},{8,16},{10,18},{12,20},{14,22},{16,24},... | collective-permute-start | bytes 786440 | tf_op jit(solution)/shard_map/ppermute | solution.py:163
  564.2 25.1 %collective-permute-start.108 = (bf16[256,1536]{1,0:T(8,128)(2,1)S(1)}, bf16[256,1536]{1,0:T(8,128)(2,1)S(1)}, u32[]{:S(2)}, u32[]{:S(2)}) collective-permute-start(bf16[256,1536]{1,0:T(8,128)(2,1)S(1)} %copy-done.52), channel_id=1, source_target_pairs={{0,4},{2,6},{4,0},{6,2},{8,12},{10,14},{12,8},{14,10},{16,20},{18,... | collective-permute-start | bytes 2359304 | tf_op jit(solution)/shard_map/ppermute | solution.py:156
  564.6 24.8 %collective-permute-start.109 = (bf16[128,1024]{1,0:T(8,128)(2,1)S(1)}, bf16[128,1024]{1,0:T(8,128)(2,1)S(1)}, u32[]{:S(2)}, u32[]{:S(2)}) collective-permute-start(bf16[128,1024]{1,0:T(8,128)(2,1)S(1)} %copy-done.57), channel_id=1, source_target_pairs={{0,6},{2,4},{4,2},{6,0},{8,14},{10,12},{12,10},{14,8},{16,22},{18,... | collective-permute-start | bytes 786440 | tf_op jit(solution)/shard_map/ppermute | solution.py:156
  (158 other events, 1417.8 us)
